TPU v7x, 32 devices: a whole 2x2x4 slice. The times are simulated.
32 devices in a mesh: groups: 2 (over x), adapt: 16 (over z, y, core).
Axes of the slice: x: 2, y: 2, z: 4, core: 2. Of those that a mesh axis runs over, the one named last changes fastest.
Arguments:
- activations: bfloat16 [4096, 12288], P(('groups', 'adapt')), parts along dimension 0, may hold values from -6 to 6
- cotangent: bfloat16 [4096, 512], P(('groups', 'adapt')), parts along dimension 0, may hold values from -6 to 6
- adapter_index_rows: int32 [4096], P(('groups', 'adapt')), parts along dimension 0, may hold values from 0 to 31, as said below
- frozen_weight: bfloat16 [12288, 512], P('adapt'), may hold values from -0.25 to 0.25
- adapter_down_weight: bfloat16 [32, 32, 12288], P('adapt'), may hold values from -0.0546875 to 0.0546875
- adapter_up_weight: bfloat16 [32, 32, 512], P('adapt'), may hold values from -0.25 to 0.25
Outputs:
- activation_gradient: bfloat16 [4096, 12288], P(('groups', 'adapt')), parts along dimension 0
- down_grad: bfloat16 [64, 32, 12288], P(('groups', 'adapt')), parts along dimension 0
- up_grad: bfloat16 [64, 32, 512], P(('groups', 'adapt')), parts along dimension 0
There are 2 independent parts, one for each index of `groups`. A program takes and returns all parts, laid end to end along the dimension named above; an argument that names none is the same for every part. Nothing has to cross between parts.
Inputs may be any that keep to these rules, and one draw needn't show every extreme that they name: `adapter_index_rows`: adapters o * 2 to o * 2 + 1 are held by index o of adapt. Among the rows of one device each adapter appears at most 6 times, and the adapters of one owner at most 12 times together.
All inputs are finite; a program needn't handle non-finite values.
Results may differ from a plain program's by a relative error of at most 0.009.
Values may be sent and summed in bfloat16 or wider, within the bound.
No kernel may reach another device: no remote copies, remote signals or barrier semaphores. Data moves between devices by JAX's collectives and lax.ppermute only.
A program may use at most 192 MiB of HBM per device.

v0:
```python
import jax
import jax.numpy as jnp
from jax import lax
from jax.sharding import PartitionSpec as P

ADAPTER_SCALE = 2.0


def slot_table(group_ids, groups, group_most):
    rows = group_ids.shape[0]
    member = (group_ids[:, None] == jnp.arange(groups, dtype=jnp.int32)[None, :]).astype(
        jnp.float32
    )
    earlier = (jnp.arange(rows)[:, None] > jnp.arange(rows)[None, :]).astype(jnp.float32)
    before = jnp.dot(earlier, member, preferred_element_type=jnp.float32)
    rank = jnp.sum(before * member, axis=1).astype(jnp.int32)
    target = group_ids * group_most + rank
    slots = jnp.arange(groups * group_most, dtype=jnp.int32)
    return (target[:, None] == slots[None, :]).astype(jnp.bfloat16)


def fill_slots(lookup_matrix, values):
    return lax.dot_general(
        lookup_matrix, values, (((0,), (0,)), ((), ())), preferred_element_type=jnp.float32
    ).astype(jnp.bfloat16)


def on_device(
    activations,
    cotangent,
    adapter_index_rows,
    frozen_weight,
    adapter_down_weight,
    adapter_up_weight,
):
    devices = lax.axis_size("adapt")
    rows_dev = activations.shape[0]
    width = activations.shape[1]
    out_width = cotangent.shape[1]
    holder_grouped = adapter_down_weight.shape[0]
    owner_most = 3 * rows_dev // (2 * devices)
    most = (owner_most + holder_grouped - 1) // holder_grouped
    product = lax.dot_general(
        cotangent,
        lax.all_gather(frozen_weight, "adapt", axis=0, tiled=True),
        (((1,), (1,)), ((), ())),
        preferred_element_type=jnp.float32,
    )
    frozen_contribution = product.astype(jnp.bfloat16)
    lookup_matrix = slot_table(adapter_index_rows, holder_grouped * devices, most)
    send_x = fill_slots(lookup_matrix, activations).reshape(devices, holder_grouped, most, width)
    send_dy = fill_slots(lookup_matrix, cotangent).reshape(devices, holder_grouped, most, out_width)
    received_input, received_output_gradient = (
        lax.all_to_all(send_x, "adapt", split_axis=0, concat_axis=0, tiled=True),
        lax.all_to_all(send_dy, "adapt", split_axis=0, concat_axis=0, tiled=True),
    )
    reduced_rank_value = jnp.einsum(
        "yxwo,xio->yxwi", received_input, adapter_down_weight, preferred_element_type=jnp.float32
    ).astype(jnp.bfloat16)
    gradient_list = jnp.einsum(
        "flvq,liq->flvi",
        received_output_gradient,
        adapter_up_weight,
        preferred_element_type=jnp.float32,
    ).astype(jnp.bfloat16)
    down_grad = (
        ADAPTER_SCALE
        * jnp.einsum(
            "voxf,voxi->ofi", gradient_list, received_input, preferred_element_type=jnp.float32
        )
    ).astype(jnp.bfloat16)
    up_grad = (
        ADAPTER_SCALE
        * jnp.einsum(
            "njmr,njmo->jro",
            reduced_rank_value,
            received_output_gradient,
            preferred_element_type=jnp.float32,
        )
    ).astype(jnp.bfloat16)
    returned = (
        ADAPTER_SCALE
        * jnp.einsum(
            "ayzs,ysg->ayzg", gradient_list, adapter_down_weight, preferred_element_type=jnp.float32
        )
    ).astype(jnp.bfloat16)
    backward_pass = lax.all_to_all(returned, "adapt", split_axis=0, concat_axis=0, tiled=True)
    backward_pass = backward_pass.reshape(devices * holder_grouped * most, width)
    adapter_contribution = jnp.dot(lookup_matrix, backward_pass, preferred_element_type=jnp.float32)
    activation_gradient = (frozen_contribution.astype(jnp.float32) + adapter_contribution).astype(
        jnp.bfloat16
    )
    return (activation_gradient, down_grad, up_grad)


def solution(mesh):
    return jax.shard_map(
        on_device,
        mesh=mesh,
        in_specs=(
            P(("groups", "adapt"), None),
            P(("groups", "adapt"), None),
            P(("groups", "adapt")),
            P("adapt", None),
            P("adapt", None, None),
            P("adapt", None, None),
        ),
        out_specs=(
            P(("groups", "adapt"), None),
            P(("groups", "adapt"), None, None),
            P(("groups", "adapt"), None, None),
        ),
        check_vma=False,
    )
```

profile of v0, /device:TPU:8, one launch (start us, length us, event | category | flops | bytes accessed | tf_op | source)
XLA Modules:
  0.0 347.6 jit_solution(1091622506456652255)
XLA Ops:
  7.2 0.0 copy-start
  7.2 0.0 all-gather.2.cloned.1.call-start
  7.2 0.7 all-gather.2.cloned.1.call-update
  7.9 1.0 fusion.28
  8.9 0.7 convert_add_fusion
  9.6 1.9 convolution_convert_fusion.2
  11.5 1.0 reshape.17
  12.5 0.8 copy.19
  13.3 6.3 %all-to-all-start = ((bf16[16,2,6,512]{3,1,2,0:T(2,128)(2,1)}), bf16[16,2,6,512]{3,1,2,0:T(2,128)(2,1)S(1)}, u32[]{:S(2)}, u32[]{:S(2)}) async-start(bf16[16,2,6,512]{3,1,2,0:T(2,128)(2,1)} %copy.19), calls=%async_computation | async-start | bytes 393216 | tf_op jit(solution)/shard_map/all_to_all | solution.py:55
  19.6 0.0 copy-done
  19.6 3.6 %convolution_convert_fusion = bf16[192,12288]{1,0:T(8,128)(2,1)} fusion(bf16[128,12288]{1,0:T(8,128)(2,1)S(1)} %copy-done, s32[128]{0:T(128)S(1)} %convert_add_fusion), kind=kOutput, calls=%fused_computation.2 | convolution fusion | flops 606363648 | bytes 7864832 | tf_op jit(solution)/shard_map/dot_general | solution.py:23
  23.2 7.8 %reshape.19 = bf16[16,2,6,12288]{3,2,1,0:T(8,128)(2,1)} reshape(bf16[192,12288]{1,0:T(8,128)(2,1)} %convolution_convert_fusion) | data formatting | bytes 9437184 | tf_op jit(solution)/shard_map/reshape | solution.py:51
  31.0 9.9 %copy.23 = bf16[16,2,6,12288]{3,1,2,0:T(2,128)(2,1)} copy(bf16[16,2,6,12288]{3,2,1,0:T(8,128)(2,1)} %reshape.19) | data formatting | bytes 9437184 | tf_op jit(solution)/shard_map/reshape | solution.py:51
  40.9 0.0 copy-start.4
  40.9 0.0 all-to-all-done
  40.9 6.2 %all-to-all-start.2 = ((bf16[16,2,6,12288]{3,1,2,0:T(2,128)(2,1)}), bf16[16,2,6,12288]{3,1,2,0:T(2,128)(2,1)}, u32[]{:S(2)}, u32[]{:S(2)}) async-start(bf16[16,2,6,12288]{3,1,2,0:T(2,128)(2,1)} %copy.23), calls=%async_computation.2 | async-start | bytes 9437184 | tf_op jit(solution)/shard_map/all_to_all | solution.py:54
  47.1 0.0 copy-done.4
  47.1 0.2 fusion.18
  47.3 0.0 copy-done.2
  47.3 3.6 %fusion.2 = bf16[16,2,6,12288]{3,0,2,1:T(8,128)(2,1)} fusion(bf16[16,2,6,32]{3,0,2,1:T(8,128)(2,1)S(1)} %fusion.18, bf16[2,32,12288]{2,1,0:T(8,128)(2,1)S(1)} %copy-done.2), kind=kOutput, calls=%fused_computation.6 | convolution fusion | flops 155713536 | bytes 6303744 | tf_op jit(solution)/shard_map/ayzs,ysg->ayzg/dot_general | solution.py:83
  50.8 9.4 %copy.21 = bf16[16,2,6,12288]{3,1,2,0:T(2,128)(2,1)} copy(bf16[16,2,6,12288]{3,0,2,1:T(8,128)(2,1)} %fusion.2) | data formatting | bytes 9437184 | tf_op jit(solution)/shard_map/convert_element_type | solution.py:86
  60.2 141.7 %all-to-all-done.2 = bf16[16,2,6,12288]{3,1,2,0:T(2,128)(2,1)} async-done(((bf16[16,2,6,12288]{3,1,2,0:T(2,128)(2,1)}), bf16[16,2,6,12288]{3,1,2,0:T(2,128)(2,1)}, u32[]{:S(2)}, u32[]{:S(2)}) %all-to-all-start.2) | async-done | bytes 4718624 | tf_op jit(solution)/shard_map/all_to_all | solution.py:54
  201.9 6.9 %all-to-all-start.1 = ((bf16[16,2,6,12288]{3,1,2,0:T(2,128)(2,1)}), bf16[16,2,6,12288]{3,1,2,0:T(2,128)(2,1)}, u32[]{:S(2)}, u32[]{:S(2)}) async-start(bf16[16,2,6,12288]{3,1,2,0:T(2,128)(2,1)} %copy.21), calls=%async_computation.1 | async-start | bytes 9437184 | tf_op jit(solution)/shard_map/all_to_all | solution.py:87
  208.9 8.9 %fusion.5 = bf16[2,32,12288]{2,1,0:T(8,128)(2,1)} fusion(bf16[16,2,6,32]{3,0,2,1:T(8,128)(2,1)S(1)} %fusion.18, bf16[16,2,6,12288]{3,1,2,0:T(2,128)(2,1)} %all-to-all-done.2), kind=kOutput, calls=%fused_computation.10 | convolution fusion | flops 152567808 | bytes 6303744 | tf_op jit(solution)/shard_map/voxf,voxi->ofi/dot_general | solution.py:68
  217.8 5.9 %fusion.12 = bf16[2,32,512]{2,1,0:T(8,128)(2,1)} fusion(bf16[2,32,12288]{2,1,0:T(8,128)(2,1)S(1)} %copy-done.2, bf16[16,2,6,12288]{3,1,2,0:T(2,128)(2,1)} %all-to-all-done.2, bf16[16,2,6,512]{3,1,2,0:T(2,128)(2,1)S(1)} %all-to-all-done), kind=kOutput, calls=%fused_computation.19 | convolution fusion | flops 157358080 | bytes 6553600 | tf_op jit(solution)/shard_map/njmr,njmo->jro/dot_general | solution.py:74
  223.7 87.2 %all-to-all-done.1 = bf16[16,2,6,12288]{3,1,2,0:T(2,128)(2,1)} async-done(((bf16[16,2,6,12288]{3,1,2,0:T(2,128)(2,1)}), bf16[16,2,6,12288]{3,1,2,0:T(2,128)(2,1)}, u32[]{:S(2)}, u32[]{:S(2)}) %all-to-all-start.1) | async-done | bytes 4718624 | tf_op jit(solution)/shard_map/all_to_all | solution.py:87
  310.9 8.0 %copy.22 = bf16[16,2,6,12288]{3,2,1,0:T(8,128)(2,1)} copy(bf16[16,2,6,12288]{3,1,2,0:T(2,128)(2,1)} %all-to-all-done.1) | data formatting | bytes 9437184 | tf_op jit(solution)/shard_map/all_to_all | solution.py:87
  319.0 7.9 %reshape.18 = bf16[192,12288]{1,0:T(8,128)(2,1)} reshape(bf16[16,2,6,12288]{3,2,1,0:T(8,128)(2,1)} %copy.22) | data formatting | bytes 9437184 | tf_op jit(solution)/shard_map/reshape | solution.py:88
  326.8 0.0 copy-done.3
  326.8 8.9 %fusion.3 = f32[128,12288]{1,0:T(8,128)S(1)} fusion(bf16[128,512]{1,0:T(8,128)(2,1)S(1)} %copy-done.3, bf16[12288,512]{1,0:T(8,128)(2,1)} %all-gather.2.cloned.1.call-done), kind=kOutput, calls=%fused_computation.7 | convolution fusion | flops 1613758464 | bytes 19005440 | tf_op jit(solution)/shard_map/dot_general | solution.py:43
  335.7 5.0 %fusion.1 = bf16[128,12288]{1,0:T(8,128)(2,1)} fusion(f32[128,12288]{1,0:T(8,128)S(1)} %fusion.3, bf16[192,12288]{1,0:T(8,128)(2,1)} %reshape.18, s32[128]{0:T(128)S(1)} %convert_add_fusion), kind=kOutput, calls=%fused_computation.4 | convolution fusion | flops 607150080 | bytes 14156288 | tf_op jit(solution)/shard_map/dot_general | solution.py:89
  340.8 0.0 copy-done.1
  (4 shorter events, 0.0 us)
Async XLA Ops:
  7.2 12.5 %copy-start = (bf16[128,12288]{1,0:T(8,128)(2,1)S(1)}, bf16[128,12288]{1,0:T(8,128)(2,1)}, u32[]{:S(2)}) copy-start(bf16[128,12288]{1,0:T(8,128)(2,1)} %param.6) | copy-start | bytes 9437188
  7.2 319.7 %all-gather.2.cloned.1.call-start = ((), (), s32[]{:S(2)}) async-start(), calls=%async_computation.3 | async-start | bytes 13369344 | tf_op jit(solution)/shard_map/all_gather | solution.py:45
  13.3 27.5 %all-to-all-start = ((bf16[16,2,6,512]{3,1,2,0:T(2,128)(2,1)}), bf16[16,2,6,512]{3,1,2,0:T(2,128)(2,1)S(1)}, u32[]{:S(2)}, u32[]{:S(2)}) async-start(bf16[16,2,6,512]{3,1,2,0:T(2,128)(2,1)} %copy.19), calls=%async_computation | async-start | bytes 393216 | tf_op jit(solution)/shard_map/all_to_all | solution.py:55
  40.9 6.2 %copy-start.4 = (bf16[2,32,512]{2,1,0:T(8,128)(2,1)S(1)}, bf16[2,32,512]{2,1,0:T(8,128)(2,1)}, u32[]{:S(2)}) copy-start(bf16[2,32,512]{2,1,0:T(8,128)(2,1)} %param.11) | copy-start | bytes 196612
  40.9 6.4 %copy-start.2 = (bf16[2,32,12288]{2,1,0:T(8,128)(2,1)S(1)}, bf16[2,32,12288]{2,1,0:T(8,128)(2,1)}, u32[]{:S(2)}) copy-start(bf16[2,32,12288]{2,1,0:T(8,128)(2,1)} %param.10) | copy-start | bytes 4718596
  40.9 161.0 %all-to-all-start.2 = ((bf16[16,2,6,12288]{3,1,2,0:T(2,128)(2,1)}), bf16[16,2,6,12288]{3,1,2,0:T(2,128)(2,1)}, u32[]{:S(2)}, u32[]{:S(2)}) async-start(bf16[16,2,6,12288]{3,1,2,0:T(2,128)(2,1)} %copy.23), calls=%async_computation.2 | async-start | bytes 9437184 | tf_op jit(solution)/shard_map/all_to_all | solution.py:54
  201.9 109.0 %all-to-all-start.1 = ((bf16[16,2,6,12288]{3,1,2,0:T(2,128)(2,1)}), bf16[16,2,6,12288]{3,1,2,0:T(2,128)(2,1)}, u32[]{:S(2)}, u32[]{:S(2)}) async-start(bf16[16,2,6,12288]{3,1,2,0:T(2,128)(2,1)} %copy.21), calls=%async_computation.1 | async-start | bytes 9437184 | tf_op jit(solution)/shard_map/all_to_all | solution.py:87
  319.0 7.9 %copy-start.3 = (bf16[128,512]{1,0:T(8,128)(2,1)S(1)}, bf16[128,512]{1,0:T(8,128)(2,1)}, u32[]{:S(2)}) copy-start(bf16[128,512]{1,0:T(8,128)(2,1)} %param.7) | copy-start | bytes 393220
  326.8 13.9 %copy-start.1 = (bf16[128,12288]{1,0:T(8,128)(2,1)S(1)}, bf16[128,12288]{1,0:T(8,128)(2,1)}, u32[]{:S(2)}) copy-start(bf16[128,12288]{1,0:T(8,128)(2,1)} %param.6) | copy-start | bytes 9437188
Sparse Core Ops, SparseCore 0:
  10.3 178.1 all-gather.1
where the time goes:
time: 350 us; the launch traced here: 348 us
  waiting for transfers between devices  230 us (66%)
  local copies, waits for them, and re-layouts  44.8 us (13%)
  matrix products  39 us (11%)
  starting transfers between devices  19.4 us (6%)
  between operations  14.1 us (4%)
    all_to_all x1, waiting for transfers between devices, on_device(): lax.all_to_all(send_x, 'adapt', split_axis=0, concat_axis=0, tiled=True)  142 us
    all_to_all x1, waiting for transfers between devices, on_device(): lax.all_to_all(returned, 'adapt', split_axis=0, concat_axis=0, tiled=True)  87.2 us
    reshape x2, local copies, waits for them, and re-layouts, on_device(): fill_slots(lookup_matrix, activations)  17.7 us
    convert_element_type x1, local copies, waits for them, and re-layouts, on_device(): returned = (ADAPTER_SCALE * jnp.einsum('ayzs,ysg->ayzg', gradient_list, a...  9.39 us
    dot_general x1, matrix products, on_device(): jnp.einsum('voxf,voxi->ofi', gradient_list, received_input, preferred_ele...  8.9 us
    dot_general x1, matrix products, on_device(): lax.dot_general(cotangent, lax.all_gather(frozen_weight, 'adapt', axis=0,...  8.86 us
    all_to_all x1, local copies, waits for them, and re-layouts, on_device(): lax.all_to_all(returned, 'adapt', split_axis=0, concat_axis=0, tiled=True)  8.04 us
    reshape x1, local copies, waits for them, and re-layouts, on_device(): backward_pass.reshape(devices * holder_grouped * most, width)  7.86 us
  transfers between devices with their start and end apart: 4, of which 2 were waited for; matrix products, arithmetic and copies ran while one was open for 20% of the time, Pallas kernels for 0%

commit v1 on v0

v1 whole, which is shorter than its diff:
```python
import jax
import jax.numpy as jnp
from jax import lax
from jax.sharding import PartitionSpec as P

ADAPTER_SCALE = 2.0
F32 = jnp.float32
BF16 = jnp.bfloat16


def dot(a, b, dims):
    return lax.dot_general(a, b, (dims, ((), ())), preferred_element_type=F32)


def on_device(x, cot, ids, frozen, down, up):
    n = lax.axis_size("adapt")
    half = n // 2
    rows, width = x.shape
    out_width = cot.shape[1]
    held, rank, _ = down.shape
    block = width // n
    halves = [list(range(half)), list(range(half, n))]
    swap = [(i, (i + half) % n) for i in range(n)]
    here = lax.axis_index("adapt")
    my_half = here // half

    def exchange(parts):
        return lax.all_to_all(
            parts, "adapt", split_axis=0, concat_axis=0, tiled=True, axis_index_groups=halves
        )

    def to_all(part):
        return exchange(jnp.broadcast_to(part[None], (half,) + part.shape))

    def swapped(part):
        return lax.ppermute(part, "adapt", swap)

    def by_width(array):
        count = array.shape[0]
        parts = array.reshape(count, 2, half, block).transpose(2, 0, 1, 3)
        return exchange(parts.reshape(half, count, 2 * block)).reshape(half * count, 2 * block)

    def from_width(array):
        count = array.shape[0] // half
        parts = exchange(array.reshape(half, count, 2 * block))
        return parts.reshape(half, count, 2, block).transpose(1, 2, 0, 3).reshape(count, width)

    up_flat = up.reshape(held * rank, out_width)
    both_up = jnp.concatenate([up_flat, swapped(up_flat)], axis=0)
    half_ids = to_all(ids.reshape(1, rows)).reshape(half * rows)
    half_cot = to_all(cot).reshape(half * rows, out_width)
    half_up = to_all(both_up).reshape(half, 2, held * rank, out_width)
    up_mine = half_up[:, 0].reshape(half * held * rank, out_width)
    up_other = half_up[:, 1].reshape(half * held * rank, out_width)
    x_block = by_width(x)
    down_mine = by_width(down.reshape(held * rank, width))
    down_other = swapped(down_mine)
    frozen_other = swapped(frozen)

    column_adapter = jnp.arange(half * held * rank, dtype=jnp.int32) // rank
    mine = half_ids[:, None] == (column_adapter + my_half * half * held)[None, :]
    other = half_ids[:, None] == (column_adapter + (1 - my_half) * half * held)[None, :]

    def chosen(product, mask):
        return jnp.where(mask, product, 0.0)

    grads_other = chosen(dot(half_cot, up_other, ((1,), (1,))), other).astype(BF16)
    grads_mine = chosen(dot(half_cot, up_mine, ((1,), (1,))), mine).astype(BF16)

    sent = (ADAPTER_SCALE * dot(grads_other, x_block, ((0,), (0,)))).astype(BF16)
    arrived = swapped(sent)
    kept = ADAPTER_SCALE * dot(grads_mine, x_block, ((0,), (0,)))
    down_grad = from_width((kept + arrived.astype(F32)).astype(BF16))

    lower = jnp.where(my_half == 0, frozen, frozen_other)
    upper = jnp.where(my_half == 0, frozen_other, frozen)
    base = dot(half_cot, jnp.concatenate([lower, upper], axis=0), ((1,), (1,)))
    lora = dot(grads_mine, down_mine, ((1,), (0,))) + dot(grads_other, down_other, ((1,), (0,)))
    activation_gradient = from_width((base + ADAPTER_SCALE * lora).astype(BF16))

    low = chosen(dot(x_block, down_mine, ((1,), (1,))), mine) + chosen(
        dot(x_block, down_other, ((1,), (1,))), other
    )
    low = low.reshape(half * rows, half * held, rank).sum(axis=1)
    low = exchange(low.reshape(half, rows, rank)).sum(axis=0).astype(BF16)
    low = to_all(low).reshape(half * rows, rank)
    pair = jnp.arange(held, dtype=jnp.int32) + here % half * held
    pair = jnp.concatenate([pair + my_half * half * held, pair + (1 - my_half) * half * held])
    spread = jnp.where(
        half_ids[:, None, None] == pair[None, :, None], low[:, None, :], jnp.zeros((), BF16)
    )
    up_part = ADAPTER_SCALE * dot(
        spread.reshape(half * rows, 2 * held * rank), half_cot, ((0,), (0,))
    )
    up_part = up_part.reshape(2, held * rank, out_width)
    up_grad = (up_part[0] + swapped(up_part[1])).astype(BF16)
    return (
        activation_gradient,
        down_grad.reshape(held, rank, width),
        up_grad.reshape(held, rank, out_width),
    )


def solution(mesh):
    return jax.shard_map(
        on_device,
        mesh=mesh,
        in_specs=(
            P(("groups", "adapt"), None),
            P(("groups", "adapt"), None),
            P(("groups", "adapt")),
            P("adapt", None),
            P("adapt", None, None),
            P("adapt", None, None),
        ),
        out_specs=(
            P(("groups", "adapt"), None),
            P(("groups", "adapt"), None, None),
            P(("groups", "adapt"), None, None),
        ),
        check_vma=False,
    )
```

time: 350 us -> 357 us (1.020)
  starting transfers between devices: 19.4 us -> 47 us
  between operations: 14.1 us -> 0.83 us
  waiting for transfers between devices: 230 us -> 221 us
  blocking collectives: 0 us -> 7.24 us
  matrix products: 39 us -> 32.4 us
    all_to_all x3 -> x8, waiting for transfers between devices: 229 us -> 114 us  [exchange(): lax.all_to_all(parts, 'adapt', split_axis=0, concat_axis=0, tiled=True, a...]
    ppermute x0 -> x5, waiting for transfers between devices: none -> 106 us  [swapped(): return lax.ppermute(part, 'adapt', swap)]
    all_to_all x3 -> x8, starting transfers between devices: 19.4 us -> 39.2 us  [exchange(): lax.all_to_all(parts, 'adapt', split_axis=0, concat_axis=0, tiled=True, a...]
    unnamed x10 -> x25, local copies, waits for them, and re-layouts: 0.03 us -> 10.3 us
    convert_element_type x1 -> x0, local copies, waits for them, and re-layouts: 9.39 us -> none  [on_device(): returned = (ADAPTER_SCALE * jnp.einsum('ayzs,ysg->ayzg', gradient_list, a...]
    reshape x5 -> x6, local copies, waits for them, and re-layouts: 27.3 us -> 19 us  [the longest x4 16.4 us: from_width(): parts.reshape(half, count, 2, block).transpose(1, 2, 0, 3)]
    ppermute x0 -> x5, starting transfers between devices: none -> 7.77 us  [swapped(): return lax.ppermute(part, 'adapt', swap)]
    all_to_all x0 -> x1, blocking collectives: none -> 7.24 us  [exchange(): lax.all_to_all(parts, 'adapt', split_axis=0, concat_axis=0, tiled=True, a...]
  transfers between devices with their start and end apart: 4 -> 13, of which waited for: 2 -> 8; matrix products, arithmetic and copies ran while one was open for 20% -> 18% of each run, Pallas kernels for 0% -> 0%
where the time goes in v1:
time: 357 us; the launch traced here: 356 us
  waiting for transfers between devices  221 us (62%)
  starting transfers between devices  47 us (13%)
  local copies, waits for them, and re-layouts  45.3 us (13%)
  matrix products  32.4 us (9%)
  blocking collectives  7.24 us (2%)
    all_to_all x8, waiting for transfers between devices, exchange(): lax.all_to_all(parts, 'adapt', split_axis=0, concat_axis=0, tiled=True, a...  114 us
    ppermute x5, waiting for transfers between devices, swapped(): return lax.ppermute(part, 'adapt', swap)  106 us
    all_to_all x8, starting transfers between devices, exchange(): lax.all_to_all(parts, 'adapt', split_axis=0, concat_axis=0, tiled=True, a...  39.2 us
    dot_general x10, matrix products, dot(): return lax.dot_general(a, b, (dims, ((), ())), preferred_element_type=F32)  32.4 us
    reshape x4, local copies, waits for them, and re-layouts, from_width(): parts.reshape(half, count, 2, block).transpose(1, 2, 0, 3)  16.4 us
    unnamed x25, local copies, waits for them, and re-layouts  10.3 us
    ppermute x5, starting transfers between devices, swapped(): return lax.ppermute(part, 'adapt', swap)  7.77 us
    all_to_all x1, blocking collectives, exchange(): lax.all_to_all(parts, 'adapt', split_axis=0, concat_axis=0, tiled=True, a...  7.24 us
  transfers between devices with their start and end apart: 13, of which 8 were waited for; matrix products, arithmetic and copies ran while one was open for 18% of the time, Pallas kernels for 0%

profile of v1, /device:TPU:8, one launch (start us, length us, event | category | flops | bytes accessed | tf_op | source)
XLA Modules:
  0.0 355.7 jit_solution(1566659742459245037)
XLA Ops:
  1.3 7.2 %all_to_all.45 = s32[8,1,128]{2,1,0:T(1,128)S(1)} all-to-all(s32[8,1,128]{2,1,0:T(1,128)S(1)} %broadcast_in_dim.56), channel_id=1, replica_groups={{0,1,2,3,4,5,6,7},{8,9,10,11,12,13,14,15},{16,17,18,19,20,21,22,23},{24..., dimensions={0} | all-to-all | bytes 8192 | tf_op jit(solution)/shard_map/all_to_all | solution.py:28
  10.5 4.9 %all-to-all-start = ((bf16[8,128,512]{2,1,0:T(8,128)(2,1)}), bf16[8,128,512]{2,1,0:T(8,128)(2,1)S(1)}, u32[]{:S(2)}, u32[]{:S(2)}) async-start(bf16[8,128,512]{2,1,0:T(8,128)(2,1)} %broadcast_in_dim.55), calls=%async_computation | async-start | bytes 2097152 | tf_op jit(solution)/shard_map/all_to_all | solution.py:28
  15.5 2.6 collective-permute-start.1
  18.1 13.8 %collective-permute-done.1 = bf16[64,512]{1,0:T(8,128)(2,1)S(1)} collective-permute-done((bf16[64,512]{1,0:T(8,128)(2,1)S(1)}, bf16[64,512]{1,0:T(8,128)(2,1)S(1)}, u32[]{:S(2)}, u32[]{:S(2)}) %collective-permute-start.1) | collective-permute-done | bytes 65568 | tf_op jit(solution)/shard_map/ppermute | solution.py:36
  33.1 4.2 %all-to-all-start.2 = ((bf16[8,128,512]{2,1,0:T(8,128)(2,1)}), bf16[8,128,512]{2,1,0:T(8,128)(2,1)S(1)}, u32[]{:S(2)}, u32[]{:S(2)}) async-start(bf16[8,128,512]{2,1,0:T(8,128)(2,1)} %broadcast_in_dim.57), calls=%async_computation.2 | async-start | bytes 2097152 | tf_op jit(solution)/shard_map/all_to_all | solution.py:28
  42.2 9.0 %all-to-all-done.2 = bf16[8,128,512]{2,1,0:T(8,128)(2,1)S(1)} async-done(((bf16[8,128,512]{2,1,0:T(8,128)(2,1)}), bf16[8,128,512]{2,1,0:T(8,128)(2,1)S(1)}, u32[]{:S(2)}, u32[]{:S(2)}) %all-to-all-start.2) | async-done | bytes 1048608 | tf_op jit(solution)/shard_map/all_to_all | solution.py:28
  52.2 4.8 %all-to-all-start.3 = ((bf16[8,64,1536]{2,1,0:T(8,128)(2,1)}), bf16[8,64,1536]{2,1,0:T(8,128)(2,1)}, u32[]{:S(2)}, u32[]{:S(2)}) async-start(bf16[8,64,1536]{2,1,0:T(8,128)(2,1)} %reshape.137), calls=%async_computation.3 | async-start | bytes 3145728 | tf_op jit(solution)/shard_map/all_to_all | solution.py:28
  56.9 3.5 copy.29
  62.3 14.3 %all-to-all-done.3 = bf16[8,64,1536]{2,1,0:T(8,128)(2,1)} async-done(((bf16[8,64,1536]{2,1,0:T(8,128)(2,1)}), bf16[8,64,1536]{2,1,0:T(8,128)(2,1)}, u32[]{:S(2)}, u32[]{:S(2)}) %all-to-all-start.3) | async-done | bytes 1572896 | tf_op jit(solution)/shard_map/all_to_all | solution.py:28
  76.6 4.1 %all-to-all-start.5 = ((bf16[8,128,1536]{1,2,0:T(8,128)(2,1)}), bf16[8,128,1536]{1,2,0:T(8,128)(2,1)S(1)}, u32[]{:S(2)}, u32[]{:S(2)}) async-start(bf16[8,128,1536]{1,2,0:T(8,128)(2,1)} %bitcast.15), calls=%async_computation.5 | async-start | bytes 6291456 | tf_op jit(solution)/shard_map/all_to_all | solution.py:28
  87.4 60.6 %all-to-all-done.5 = bf16[8,128,1536]{1,2,0:T(8,128)(2,1)S(1)} async-done(((bf16[8,128,1536]{1,2,0:T(8,128)(2,1)}), bf16[8,128,1536]{1,2,0:T(8,128)(2,1)S(1)}, u32[]{:S(2)}, u32[]{:S(2)}) %all-to-all-start.5) | async-done | bytes 3145760 | tf_op jit(solution)/shard_map/all_to_all | solution.py:28
  148.0 2.8 copy.31
  150.8 5.3 %fusion.1 = bf16[512,1536]{1,0:T(8,128)(2,1)} fusion(bf16[1024,512]{0,1:T(8,128)(2,1)} %fusion.4, bf16[1024,1536]{1,0:T(8,128)(2,1)} %bitcast.80), kind=kOutput, calls=%fused_computation.5 | convolution fusion | flops 1612185600 | bytes 5767168 | tf_op jit(solution)/shard_map/dot_general | solution.py:12
  157.9 3.2 fusion.20
  161.1 56.4 %collective-permute-done.2 = bf16[512,1536]{1,0:T(8,128)(2,1)} collective-permute-done((bf16[512,1536]{1,0:T(8,128)(2,1)}, bf16[512,1536]{1,0:T(8,128)(2,1)}, u32[]{:S(2)}, u32[]{:S(2)}) %collective-permute-start.2) | collective-permute-done | bytes 1572896 | tf_op jit(solution)/shard_map/ppermute | solution.py:36
  217.5 3.3 fusion.3
  221.6 6.3 %all-to-all-start.7 = ((f32[8,128,32]{1,2,0:T(8,128)}), f32[8,128,32]{1,2,0:T(8,128)S(1)}, u32[]{:S(2)}, u32[]{:S(2)}) async-start(f32[8,128,32]{1,2,0:T(8,128)} %copy_bitcast_fusion.2), calls=%async_computation.7 | async-start | bytes 262144 | tf_op jit(solution)/shard_map/all_to_all | solution.py:28
  229.6 22.8 %all-to-all-done.7 = f32[8,128,32]{1,2,0:T(8,128)S(1)} async-done(((f32[8,128,32]{1,2,0:T(8,128)}), f32[8,128,32]{1,2,0:T(8,128)S(1)}, u32[]{:S(2)}, u32[]{:S(2)}) %all-to-all-start.7) | async-done | bytes 131104 | tf_op jit(solution)/shard_map/all_to_all | solution.py:28
  253.1 6.4 %all-to-all-start.8 = ((bf16[8,128,32]{1,2,0:T(8,128)(2,1)}), bf16[8,128,32]{1,2,0:T(8,128)(2,1)S(1)}, u32[]{:S(2)}, u32[]{:S(2)}) async-start(bf16[8,128,32]{1,2,0:T(8,128)(2,1)} %broadcast_in_dim.60), calls=%async_computation.8 | async-start | bytes 131072 | tf_op jit(solution)/shard_map/all_to_all | solution.py:28
  259.5 5.3 %add_convert_fusion = bf16[512,1536]{1,0:T(8,128)(2,1)} fusion(bf16[512,1536]{1,0:T(8,128)(2,1)} %collective-permute-done.3, bf16[1024,512]{0,1:T(8,128)(2,1)S(1)} %fusion.2, bf16[1024,1536]{1,0:T(8,128)(2,1)} %bitcast.81), kind=kOutput, calls=%fused_computation.4 | convolution fusion | flops 1613758464 | bytes 7340032 | tf_op jit(solution)/shard_map/dot_general | solution.py:12
  264.8 4.4 %all-to-all-start.6 = ((bf16[8,64,1536]{2,1,0:T(8,128)(2,1)}), bf16[8,64,1536]{2,1,0:T(8,128)(2,1)S(1)}, u32[]{:S(2)}, u32[]{:S(2)}) async-start(bf16[8,64,1536]{2,1,0:T(8,128)(2,1)} %bitcast.87), calls=%async_computation.6 | async-start | bytes 3145728 | tf_op jit(solution)/shard_map/all_to_all | solution.py:28
  270.6 3.4 fusion.18
  274.0 3.3 fusion.19
  277.3 3.6 %fusion = bf16[1024,1536]{1,0:T(8,128)(2,1)} fusion(f32[1024,1536]{1,0:T(8,128)S(1)} %fusion.18, f32[1024,1536]{1,0:T(8,128)S(1)} %fusion.19, bf16[1024,512]{1,0:T(8,128)(2,1)S(1)} %bitcast.75, bf16[768,512]{1,0:T(8,128)(2,1)S(1)} %get-tuple-element.4, bf16[768,512]{1,0:T(8,128)(2,1)S(1)} %get-tuple-element.3), kind=kOutput, calls=%fused_computation.1 | convolution fusion | flops 1620049920 | bytes 18350080 | tf_op jit(solution)/shard_map/dot_general | solution.py:12
  280.9 7.8 %all-to-all-done.6 = bf16[8,64,1536]{2,1,0:T(8,128)(2,1)S(1)} async-done(((bf16[8,64,1536]{2,1,0:T(8,128)(2,1)}), bf16[8,64,1536]{2,1,0:T(8,128)(2,1)S(1)}, u32[]{:S(2)}, u32[]{:S(2)}) %all-to-all-start.6) | async-done | bytes 1572896 | tf_op jit(solution)/shard_map/all_to_all | solution.py:28
  289.8 4.1 %all-to-all-start.4 = ((bf16[8,128,1536]{2,1,0:T(8,128)(2,1)}), bf16[8,128,1536]{2,1,0:T(8,128)(2,1)S(1)}, u32[]{:S(2)}, u32[]{:S(2)}) async-start(bf16[8,128,1536]{2,1,0:T(8,128)(2,1)} %bitcast.11), calls=%async_computation.4 | async-start | bytes 6291456 | tf_op jit(solution)/shard_map/all_to_all | solution.py:28
  296.2 35.9 %collective-permute-done.4 = f32[64,512]{1,0:T(8,128)S(1)} collective-permute-done((f32[64,512]{1,0:T(8,128)S(1)}, f32[64,512]{1,0:T(8,128)S(1)}, u32[]{:S(2)}, u32[]{:S(2)}) %collective-permute-start.4) | collective-permute-done | bytes 131104 | tf_op jit(solution)/shard_map/ppermute | solution.py:36
  332.7 4.6 %reshape.146 = bf16[8,64,2,768]{3,2,1,0:T(2,128)(2,1)} reshape(bf16[8,64,1536]{2,1,0:T(8,128)(2,1)} %copy-done.3) | data formatting | bytes 3145728 | tf_op jit(solution)/shard_map/reshape | solution.py:46
  337.4 4.2 %copy.43 = bf16[8,64,2,768]{3,0,2,1:T(8,128)(2,1)} copy(bf16[8,64,2,768]{3,2,1,0:T(2,128)(2,1)} %reshape.146) | data formatting | bytes 3145728 | tf_op jit(solution)/shard_map/reshape | solution.py:46
  341.6 3.6 %reshape_reshape.7 = bf16[2,32,12288]{2,1,0:T(8,128)(2,1)} reshape(bf16[64,2,8,768]{3,2,1,0:T(8,128)(2,1)} %bitcast.77) | data formatting | bytes 3145728 | tf_op jit(solution)/shard_map/reshape;reshape | solution.py:99
  347.5 5.2 %copy.28 = bf16[8,128,2,768]{3,0,2,1:T(8,128)(2,1)S(1)} copy(bf16[8,128,2,768]{3,2,1,0:T(2,128)(2,1)} %reshape.140) | data formatting | bytes 6291456 | tf_op jit(solution)/shard_map/reshape | solution.py:46
  352.8 2.9 copy.38
  (58 shorter events, 31.1 us)
Async XLA Ops:
  0.6 14.8 %copy-start.7 = (bf16[2,32,512]{2,1,0:T(8,128)(2,1)S(1)}, bf16[2,32,512]{2,1,0:T(8,128)(2,1)}, u32[]{:S(2)}) copy-start(bf16[2,32,512]{2,1,0:T(8,128)(2,1)} %param.11) | copy-start | bytes 196612
  10.5 21.4 %all-to-all-start = ((bf16[8,128,512]{2,1,0:T(8,128)(2,1)}), bf16[8,128,512]{2,1,0:T(8,128)(2,1)S(1)}, u32[]{:S(2)}, u32[]{:S(2)}) async-start(bf16[8,128,512]{2,1,0:T(8,128)(2,1)} %broadcast_in_dim.55), calls=%async_computation | async-start | bytes 2097152 | tf_op jit(solution)/shard_map/all_to_all | solution.py:28
  15.5 16.4 %collective-permute-start.1 = (bf16[64,512]{1,0:T(8,128)(2,1)S(1)}, bf16[64,512]{1,0:T(8,128)(2,1)S(1)}, u32[]{:S(2)}, u32[]{:S(2)}) collective-permute-start(bf16[64,512]{1,0:T(8,128)(2,1)S(1)} %bitcast.92), channel_id=1, source_target_pairs={{0,8},{1,9},{2,10},{3,11},{4,12},{5,13},{6,14},{7,15},{8,0},{9,1},... | collective-permute-start | bytes 196616 | tf_op jit(solution)/shard_map/ppermute | solution.py:36
  31.9 7.1 %copy-start = (bf16[8,128,512]{2,1,0:T(8,128)(2,1)}, bf16[8,128,512]{2,1,0:T(8,128)(2,1)S(1)}, u32[]{:S(2)}) copy-start(bf16[8,128,512]{2,1,0:T(8,128)(2,1)S(1)} %all-to-all-done) | copy-start | bytes 3145732
  33.1 18.1 %all-to-all-start.2 = ((bf16[8,128,512]{2,1,0:T(8,128)(2,1)}), bf16[8,128,512]{2,1,0:T(8,128)(2,1)S(1)}, u32[]{:S(2)}, u32[]{:S(2)}) async-start(bf16[8,128,512]{2,1,0:T(8,128)(2,1)} %broadcast_in_dim.57), calls=%async_computation.2 | async-start | bytes 2097152 | tf_op jit(solution)/shard_map/all_to_all | solution.py:28
  51.2 1.0 copy-start.4
  52.2 24.4 %all-to-all-start.3 = ((bf16[8,64,1536]{2,1,0:T(8,128)(2,1)}), bf16[8,64,1536]{2,1,0:T(8,128)(2,1)}, u32[]{:S(2)}, u32[]{:S(2)}) async-start(bf16[8,64,1536]{2,1,0:T(8,128)(2,1)} %reshape.137), calls=%async_computation.3 | async-start | bytes 3145728 | tf_op jit(solution)/shard_map/all_to_all | solution.py:28
  76.6 71.5 %all-to-all-start.5 = ((bf16[8,128,1536]{1,2,0:T(8,128)(2,1)}), bf16[8,128,1536]{1,2,0:T(8,128)(2,1)S(1)}, u32[]{:S(2)}, u32[]{:S(2)}) async-start(bf16[8,128,1536]{1,2,0:T(8,128)(2,1)} %bitcast.15), calls=%async_computation.5 | async-start | bytes 6291456 | tf_op jit(solution)/shard_map/all_to_all | solution.py:28
  80.7 188.5 %collective-permute-start = (bf16[768,512]{1,0:T(8,128)(2,1)}, bf16[768,512]{1,0:T(8,128)(2,1)}, u32[]{:S(2)}, u32[]{:S(2)}) collective-permute-start(bf16[768,512]{1,0:T(8,128)(2,1)} %param.9), channel_id=1, source_target_pairs={{0,8},{1,9},{2,10},{3,11},{4,12},{5,13},{6,14},{7,15},{8,0},{9,1},... | collective-permute-start | bytes 2359304 | tf_op jit(solution)/shard_map/ppermute | solution.py:36
  81.2 4.5 %copy-start.1 = (bf16[8,128,512]{2,1,0:T(8,128)(2,1)S(1)}, bf16[8,128,512]{2,1,0:T(8,128)(2,1)}, u32[]{:S(2)}) copy-start(bf16[8,128,512]{2,1,0:T(8,128)(2,1)} %copy-done) | copy-start | bytes 3145732
  81.2 136.2 %collective-permute-start.2 = (bf16[512,1536]{1,0:T(8,128)(2,1)}, bf16[512,1536]{1,0:T(8,128)(2,1)}, u32[]{:S(2)}, u32[]{:S(2)}) collective-permute-start(bf16[512,1536]{1,0:T(8,128)(2,1)} %bitcast.8), channel_id=1, source_target_pairs={{0,8},{1,9},{2,10},{3,11},{4,12},{5,13},{6,14},{7,15},{8,0},{9,1},... | collective-permute-start | bytes 4718600 | tf_op jit(solution)/shard_map/ppermute | solution.py:36
  150.8 7.1 %copy-start.5 = (bf16[8,128,1536]{2,1,0:T(8,128)(2,1)S(1)}, bf16[8,128,1536]{2,1,0:T(8,128)(2,1)}, u32[]{:S(2)}) copy-start(bf16[8,128,1536]{2,1,0:T(8,128)(2,1)} %copy.31) | copy-start | bytes 9437188
  156.1 103.4 %collective-permute-start.3 = (bf16[512,1536]{1,0:T(8,128)(2,1)}, bf16[512,1536]{1,0:T(8,128)(2,1)}, u32[]{:S(2)}, u32[]{:S(2)}) collective-permute-start(bf16[512,1536]{1,0:T(8,128)(2,1)} %fusion.1), channel_id=1, source_target_pairs={{0,8},{1,9},{2,10},{3,11},{4,12},{5,13},{6,14},{7,15},{8,0},{9,1},... | collective-permute-start | bytes 4718600 | tf_op jit(solution)/shard_map/ppermute | solution.py:36
  220.8 7.1 %copy-start.2 = (bf16[8,128,512]{2,1,0:T(8,128)(2,1)S(1)}, bf16[8,128,512]{2,1,0:T(8,128)(2,1)}, u32[]{:S(2)}) copy-start(bf16[8,128,512]{2,1,0:T(8,128)(2,1)} %copy-done) | copy-start | bytes 3145732
  221.6 30.8 %all-to-all-start.7 = ((f32[8,128,32]{1,2,0:T(8,128)}), f32[8,128,32]{1,2,0:T(8,128)S(1)}, u32[]{:S(2)}, u32[]{:S(2)}) async-start(f32[8,128,32]{1,2,0:T(8,128)} %copy_bitcast_fusion.2), calls=%async_computation.7 | async-start | bytes 262144 | tf_op jit(solution)/shard_map/all_to_all | solution.py:28
  229.6 35.2 %copy-start.9 = (bf16[1024,512]{0,1:T(8,128)(2,1)}, bf16[1024,512]{0,1:T(8,128)(2,1)S(1)}, u32[]{:S(2)}) copy-start(bf16[1024,512]{0,1:T(8,128)(2,1)S(1)} %fusion.2) | copy-start | bytes 3145732
  253.1 11.8 %all-to-all-start.8 = ((bf16[8,128,32]{1,2,0:T(8,128)(2,1)}), bf16[8,128,32]{1,2,0:T(8,128)(2,1)S(1)}, u32[]{:S(2)}, u32[]{:S(2)}) async-start(bf16[8,128,32]{1,2,0:T(8,128)(2,1)} %broadcast_in_dim.60), calls=%async_computation.8 | async-start | bytes 131072 | tf_op jit(solution)/shard_map/all_to_all | solution.py:28
  264.8 4.4 %copy-start.6 = (bf16[768,512]{1,0:T(8,128)(2,1)S(1)}, bf16[768,512]{1,0:T(8,128)(2,1)}, u32[]{:S(2)}) copy-start(bf16[768,512]{1,0:T(8,128)(2,1)} %param.9) | copy-start | bytes 2359300
  264.8 23.9 %all-to-all-start.6 = ((bf16[8,64,1536]{2,1,0:T(8,128)(2,1)}), bf16[8,64,1536]{2,1,0:T(8,128)(2,1)S(1)}, u32[]{:S(2)}, u32[]{:S(2)}) async-start(bf16[8,64,1536]{2,1,0:T(8,128)(2,1)} %bitcast.87), calls=%async_computation.6 | async-start | bytes 3145728 | tf_op jit(solution)/shard_map/all_to_all | solution.py:28
  269.2 1.5 copy-start.10
  270.6 3.4 copy-start.8
  288.7 1.1 copy-start.3
  289.8 55.3 %all-to-all-start.4 = ((bf16[8,128,1536]{2,1,0:T(8,128)(2,1)}), bf16[8,128,1536]{2,1,0:T(8,128)(2,1)S(1)}, u32[]{:S(2)}, u32[]{:S(2)}) async-start(bf16[8,128,1536]{2,1,0:T(8,128)(2,1)} %bitcast.11), calls=%async_computation.4 | async-start | bytes 6291456 | tf_op jit(solution)/shard_map/all_to_all | solution.py:28
  295.7 36.4 %collective-permute-start.4 = (f32[64,512]{1,0:T(8,128)S(1)}, f32[64,512]{1,0:T(8,128)S(1)}, u32[]{:S(2)}, u32[]{:S(2)}) collective-permute-start(f32[64,512]{1,0:T(8,128)S(1)} %slice.21), channel_id=1, source_target_pairs={{0,8},{1,9},{2,10},{3,11},{4,12},{5,13},{6,14},{7,15},{8,0},{9,1},... | collective-permute-start | bytes 393224 | tf_op jit(solution)/shard_map/ppermute | solution.py:36

commit v2 on v1

v2 whole, which is shorter than its diff:
```python
import jax
import jax.numpy as jnp
from jax import lax
from jax.experimental import pallas as pl
from jax.experimental.pallas import tpu as pltpu
from jax.sharding import PartitionSpec as P

ADAPTER_SCALE = 2.0
F32 = jnp.float32
BF16 = jnp.bfloat16
LANES = 128
VMEM_BYTES = 48 * 1024 * 1024


def dot(a, b, dims):
    return lax.dot_general(a, b, (dims, ((), ())), preferred_element_type=F32)


def after(value, *earlier):
    return lax.optimization_barrier((value,) + earlier)[0]


def in_xla(x, cot, ids, frozen, down, up):
    n = lax.axis_size("adapt")
    groups = lax.axis_size("groups")
    half = n // 2
    rows, width = x.shape
    out_width = cot.shape[1]
    held, rank, _ = down.shape
    own = held * rank
    block = width // n
    halves = [list(range(half)), list(range(half, n))]
    swap = [(i, (i + half) % n) for i in range(n)]
    here = lax.axis_index("adapt")
    group = lax.axis_index("groups")
    my_half = here // half

    def exchange(parts):
        return lax.all_to_all(
            parts, "adapt", split_axis=0, concat_axis=0, tiled=True, axis_index_groups=halves
        )

    def swapped(part):
        return lax.ppermute(part, "adapt", swap)

    def across_groups(part):
        arrived = [part]
        for step in range(1, groups):
            ring = [(g, (g + step) % groups) for g in range(groups)]
            arrived.append(lax.ppermute(part, "groups", ring))
        return [lax.select_n((group - p) % groups, *arrived) for p in range(groups)]

    def by_width(array):
        return array.reshape(array.shape[0], 2, half, block).transpose(1, 2, 0, 3)

    frozen_piece = lax.dynamic_slice_in_dim(
        frozen, group * (block // groups), block // groups, axis=0
    )
    down_piece = lax.dynamic_slice_in_dim(
        down.reshape(own, width), group * (own // groups), own // groups, axis=0
    )
    up_flat = up.reshape(own, out_width)

    up_other = swapped(up_flat)
    frozen_arrived = swapped(frozen_piece)
    down_send = by_width(down_piece)
    down_send = jnp.concatenate([down_send[0], down_send[1]], axis=2)
    down_near = exchange(down_send)

    x_send = by_width(x)
    up_pair = jnp.concatenate([up_flat, up_other], axis=0)
    up_rows = jnp.pad(up_pair, ((0, max(0, rows - 2 * own)), (0, 0)))
    id_rows = jnp.broadcast_to(ids.astype(BF16)[:, None], (rows, LANES))
    small = jnp.concatenate([cot, up_rows, id_rows], axis=1)
    first = jnp.concatenate(
        [x_send[0], jnp.broadcast_to(small[None], (half,) + small.shape)], axis=2
    )
    first = exchange(after(first, down_near))
    second = exchange(after(x_send[1], first))

    down_near_all = across_groups(down_near)
    down_far_all = across_groups(swapped(down_near))
    frozen_far = jnp.concatenate(across_groups(frozen_arrived), axis=0)

    def joined(pieces):
        return jnp.stack(pieces, axis=1).reshape(half * own, 2 * block)

    down_near_all = joined(down_near_all)
    down_far_all = joined(down_far_all)

    x_first = first[:, :, :block].reshape(half * rows, block)
    x_second = second.reshape(half * rows, block)
    half_cot = first[:, :, block : block + out_width].reshape(half * rows, out_width)
    up_got = first[:, :, block + out_width : block + 2 * out_width]
    half_ids = first[:, :, block + 2 * out_width].reshape(half * rows).astype(jnp.int32)
    up_near = up_got[:, :own].reshape(half * own, out_width)
    up_far = up_got[:, own : 2 * own].reshape(half * own, out_width)

    adapter = jnp.arange(half * own, dtype=jnp.int32) // rank
    near_ids = adapter + my_half * half * held
    far_ids = adapter + (1 - my_half) * half * held

    def grads_across(up_maps, adapters):
        return jnp.where(
            adapters[:, None] == half_ids[None, :], dot(up_maps, half_cot, ((1,), (1,))), 0.0
        ).astype(BF16)

    grads_far = grads_across(up_far, far_ids)
    grads_near = grads_across(up_near, near_ids)

    def down_part(grads, values):
        return ADAPTER_SCALE * dot(grads, values, ((1,), (0,)))

    far_first = swapped(down_part(grads_far, x_first).astype(BF16))
    far_second = swapped(down_part(grads_far, x_second).astype(BF16))
    sum_first = (down_part(grads_near, x_first) + far_first.astype(F32)).astype(BF16)
    sum_second = (down_part(grads_near, x_second) + far_second.astype(F32)).astype(BF16)

    low_frozen = jnp.where(my_half == 0, frozen, frozen_far)
    high_frozen = jnp.where(my_half == 0, frozen_far, frozen)
    base = dot(half_cot, jnp.concatenate([low_frozen, high_frozen], axis=0), ((1,), (1,)))
    lora = dot(grads_near, down_near_all, ((0,), (0,))) + dot(
        grads_far, down_far_all, ((0,), (0,))
    )
    gradient = (base + ADAPTER_SCALE * lora).astype(BF16).reshape(half, rows, 2 * block)

    x_block = jnp.concatenate([x_first, x_second], axis=1)
    fold = (
        jnp.arange(half * own, dtype=jnp.int32)[:, None] % rank
        == jnp.arange(LANES, dtype=jnp.int32)[None, :]
    ).astype(BF16)

    def low_part(maps, adapters):
        picked = jnp.where(
            half_ids[:, None] == adapters[None, :], dot(x_block, maps, ((1,), (1,))), 0.0
        ).astype(BF16)
        return dot(picked, fold, ((1,), (0,)))

    low = (low_part(down_near_all, near_ids) + low_part(down_far_all, far_ids)).astype(BF16)
    gradient = jnp.concatenate([gradient, low.reshape(half, rows, LANES)], axis=2)
    gradient = exchange(after(gradient, second))
    low = gradient[:, :, 2 * block : 2 * block + rank].astype(F32).sum(axis=0).astype(BF16)
    gradient = gradient[:, :, : 2 * block].reshape(half, rows, 2, block)
    gradient = gradient.transpose(1, 2, 0, 3).reshape(rows, width)

    pack = LANES // rank
    low_rows = low.reshape(pack, rows // pack, rank).transpose(1, 0, 2).reshape(rows // pack, LANES)
    low_rows = jnp.pad(low_rows, ((0, own - rows // pack), (0, 0)))
    sum_first = jnp.concatenate(
        [
            sum_first.reshape(half, own, block),
            jnp.broadcast_to(low_rows[None], (half, own, LANES)),
        ],
        axis=2,
    )
    sum_first = exchange(sum_first)
    sum_second = exchange(after(sum_second.reshape(half, own, block), sum_first))
    low = sum_first[:, : rows // pack, block:].reshape(half, rows // pack, pack, rank)
    low = low.transpose(0, 2, 1, 3).reshape(half * rows, rank)
    down_grad = jnp.stack([sum_first[:, :, :block], sum_second], axis=0)
    down_grad = down_grad.transpose(2, 0, 1, 3).reshape(held, rank, width)

    pair = jnp.arange(held, dtype=jnp.int32) + here % half * held
    pair = jnp.concatenate([pair + my_half * half * held, pair + (1 - my_half) * half * held])
    spread = jnp.where(
        half_ids[:, None] == jnp.repeat(pair, rank)[None, :],
        jnp.tile(low, (1, 2 * held)),
        jnp.zeros((), BF16),
    )
    up_part = (ADAPTER_SCALE * dot(spread, half_cot, ((0,), (0,)))).reshape(2, own, out_width)
    up_grad = (up_part[0] + swapped(up_part[1])).astype(BF16)
    return gradient, down_grad, up_grad.reshape(held, rank, out_width)


def shape(*dims, kind=BF16):
    return jax.ShapeDtypeStruct(dims, kind)


def with_kernels(x, cot, ids, frozen, down, up):
    n = lax.axis_size("adapt")
    half = n // 2
    rows, width = x.shape
    out_width = cot.shape[1]
    held, rank, _ = down.shape
    own = held * rank
    piece = own // 2
    block = width // n
    pair = 2 * block
    half_rows = half * rows
    halves = [list(range(half)), list(range(half, n))]
    here = lax.axis_index("adapt")
    group = lax.axis_index("groups")
    my_half = here // half
    core = here % 2

    def exchange(parts):
        return lax.all_to_all(
            parts, "adapt", split_axis=0, concat_axis=0, tiled=True, axis_index_groups=halves
        )

    def swapped(part):
        return lax.ppermute(part, "adapt", [(i, (i + half) % n) for i in range(n)])

    def flipped(part, bit):
        return lax.ppermute(part, "adapt", [(i, i ^ bit) for i in range(n)])

    def other_group(part):
        return lax.ppermute(part, "groups", [(0, 1), (1, 0)])

    smem = pl.BlockSpec(memory_space=pltpu.SMEM)
    vmem = pl.BlockSpec(memory_space=pltpu.VMEM)
    params = pltpu.CompilerParams(vmem_limit_bytes=VMEM_BYTES)

    def cost(flops, moved):
        return pl.CostEstimate(flops=flops, bytes_accessed=moved, transcendentals=0)

    frozen_piece = lax.dynamic_slice_in_dim(frozen, group * (block // 2), block // 2, axis=0)
    down_piece = lax.dynamic_slice_in_dim(down.reshape(own, width), group * piece, piece, axis=0)
    cot_at = pair
    up_at = cot_at + 2 * out_width
    id_at = up_at + out_width
    wide = id_at + LANES

    def pack_small(down_ref, cot_ref, up_ref, id_ref, out_ref):
        for j in range(half):
            c = j % 2
            for q in range(2):
                out_ref[j, :, q * block : (q + 1) * block] = down_ref[
                    :, (q * half + j) * block : (q * half + j + 1) * block
                ]
                out_ref[j, :, cot_at + q * out_width : cot_at + (q + 1) * out_width] = cot_ref[
                    (2 * c + q) * piece : (2 * c + q + 1) * piece, :
                ]
            out_ref[j, :, up_at:id_at] = up_ref[c * piece : (c + 1) * piece, :]
            out_ref[j, :, id_at:] = id_ref[...]

    id_line = jnp.broadcast_to(ids.astype(BF16)[None, :], (piece, LANES))
    small = pl.pallas_call(
        pack_small,
        out_shape=shape(half, piece, wide),
        compiler_params=params,
        cost_estimate=cost(0, 4 * half * piece * wide),
    )(down_piece, cot, up.reshape(own, out_width), id_line)
    small = exchange(small)

    def pack_rows(x_ref, out_ref):
        for j in range(half):
            for q in range(2):
                out_ref[j, :, q * block : (q + 1) * block] = x_ref[
                    :, (q * half + j) * block : (q * half + j + 1) * block
                ]

    x_parts = pl.pallas_call(
        pack_rows,
        out_shape=shape(half, rows, pair),
        compiler_params=params,
        cost_estimate=cost(0, 4 * rows * width),
    )(x)

    x_parts, small = lax.optimization_barrier((x_parts, small))
    x_block = exchange(x_parts).reshape(half_rows, pair)
    down_near = small[:, :, :pair].reshape(half * piece, pair)
    shared = small[:, :, pair:id_at].reshape(half * piece, 3 * out_width)
    frozen_near = swapped(after(frozen_piece, small))
    shared_far = swapped(shared[:, 2 * out_width :])
    shared_twin = flipped(shared, 1)
    down_far = swapped(down_near)
    near_cross = other_group(down_near)
    frozen_near, shared_far, shared_twin, down_far, near_cross = lax.optimization_barrier(
        (frozen_near, shared_far, shared_twin, down_far, near_cross)
    )
    up_far_twin = flipped(shared_far, 1)
    frozen_cross = other_group(frozen_near)
    far_cross = other_group(down_far)
    half_ids = small[:, 0, id_at:].reshape(half_rows).astype(F32)
    id_rows = jnp.broadcast_to(half_ids[:, None], (half_rows, LANES))
    id_lines = jnp.broadcast_to(half_ids[None, :], (8, half_rows))
    maps = (down_near, down_far, near_cross, far_cross)
    first_piece = jnp.where(group == 0, frozen_near, frozen_cross)
    last_piece = jnp.where(group == 0, frozen_cross, frozen_near)
    frozen_far = jnp.concatenate([first_piece, last_piece], axis=0)
    frozen_low = jnp.where(my_half == 0, frozen, frozen_far)
    frozen_high = jnp.where(my_half == 0, frozen_far, frozen)

    part = half * piece
    columns = 4 * part

    def column_ids(at, where, axis, dims):
        column = lax.broadcasted_iota(jnp.int32, dims, axis) + at
        crossed, rest = column // (2 * part), column % (2 * part)
        far, rest = rest // part, rest % part
        owner, within = rest // piece, rest % piece
        side = jnp.where(far == 0, where[0], 1 - where[0])
        which = jnp.where(crossed == 0, where[1], 1 - where[1])
        return ((side * half + owner) * held + (which * piece + within) // rank).astype(F32)

    where = jnp.stack([my_half, group, core])

    def grads_body(
        where_ref,
        mine_ref,
        twin_ref,
        far_ref,
        far_twin_ref,
        id_ref,
        line_ref,
        by_row_ref,
        by_column_ref,
        cot_ref,
        up_scratch,
    ):
        c = where_ref[2]
        for owner in range(half):
            at = owner * piece
            for q in range(2):
                for ref, side in ((mine_ref, c), (twin_ref, 1 - c)):
                    target = pl.multiple_of(owner * rows + (2 * side + q) * piece, piece)
                    cot_ref[pl.ds(target, piece), :] = ref[
                        at : at + piece, q * out_width : (q + 1) * out_width
                    ]
            for far, pieces in enumerate(
                (
                    (mine_ref[at : at + piece, 2 * out_width :], twin_ref[at : at + piece, 2 * out_width :]),
                    (far_ref[at : at + piece, :], far_twin_ref[at : at + piece, :]),
                )
            ):
                for side, value in zip((c, 1 - c), pieces):
                    crossed = jnp.where(side == where_ref[1], 0, 1)
                    target = (crossed * 2 + far) * part + at
                    up_scratch[pl.ds(pl.multiple_of(target, piece), piece), :] = value
        step = 2 * part
        for at in range(0, columns, step):
            product = dot(cot_ref[...], up_scratch[at : at + step, :], ((1,), (1,)))
            match = id_ref[:, :1] == column_ids(at, where_ref, 1, (1, step))
            by_row_ref[:, at : at + step] = jnp.where(match, product, 0.0).astype(BF16)
            product = dot(up_scratch[at : at + step, :], cot_ref[...], ((1,), (1,)))
            match = column_ids(at, where_ref, 0, (step, 1)) == line_ref[:1, :]
            by_column_ref[at : at + step, :] = jnp.where(match, product, 0.0).astype(BF16)

    by_row, by_column, half_cot = pl.pallas_call(
        grads_body,
        out_shape=(
            shape(half_rows, columns),
            shape(columns, half_rows),
            shape(half_rows, out_width),
        ),
        in_specs=[smem] + [vmem] * 6,
        out_specs=(vmem, vmem, vmem),
        scratch_shapes=[pltpu.VMEM((columns, out_width), BF16)],
        compiler_params=params,
        cost_estimate=cost(4 * half_rows * columns * out_width, 8 * half_rows * columns),
    )(where, shared, shared_twin, shared_far, up_far_twin, id_rows, id_lines)

    def down_part(far, values, kind):
        def body(grads_ref, x_ref, out_ref):
            out_ref[...] = (
                ADAPTER_SCALE * dot(grads_ref[...], x_ref[...], ((1,), (0,)))
            ).astype(kind)

        tile = pair // 3
        return pl.pallas_call(
            body,
            grid=(3, 2),
            out_shape=shape(2 * part, pair, kind=kind),
            in_specs=[
                pl.BlockSpec((part, half_rows), lambda c, p: (2 * p + far, 0)),
                pl.BlockSpec((half_rows, tile), lambda c, p: (0, c)),
            ],
            out_specs=pl.BlockSpec((part, tile), lambda c, p: (p, c)),
            compiler_params=params,
            cost_estimate=cost(4 * part * half_rows * pair, 2 * half_rows * pair),
        )(by_column, values)

    sent = down_part(1, x_block, BF16)
    arrived = swapped(sent)

    lines = 2 * rows

    def rows_body(cot_ref, grads_ref, low_w, high_w, m0, m1, m2, m3, out_ref):
        for q, w_ref in enumerate((low_w, high_w)):
            lo, hi = q * block, (q + 1) * block
            total = dot(cot_ref[...], w_ref[...], ((1,), (1,)))
            for s, m_ref in enumerate((m0, m1, m2, m3)):
                total = total + dot(
                    ADAPTER_SCALE * grads_ref[:, s * part : (s + 1) * part],
                    m_ref[:, lo:hi],
                    ((1,), (0,)),
                )
            out_ref[:, :, lo:hi] = total.astype(BF16).reshape(lines // rows, rows, block)

    cot_later = after(half_cot, sent)
    result = pl.pallas_call(
        rows_body,
        grid=(half_rows // lines,),
        out_shape=shape(half, rows, pair),
        in_specs=[
            pl.BlockSpec((lines, out_width), lambda i: (i, 0)),
            pl.BlockSpec((lines, columns), lambda i: (i, 0)),
        ]
        + [pl.BlockSpec((block, out_width), lambda i: (0, 0))] * 2
        + [pl.BlockSpec((part, pair), lambda i: (0, 0))] * 4,
        out_specs=pl.BlockSpec((lines // rows, rows, pair), lambda i: (i, 0, 0)),
        compiler_params=params,
        cost_estimate=cost(2 * half_rows * pair * (out_width + columns), 8 * half_rows * pair),
    )(cot_later, by_row, frozen_low, frozen_high, *maps)

    back = exchange(result)
    kept = down_part(0, after(x_block, result), F32)

    packed = LANES // rank

    def low_body(where_ref, x_ref, id_ref, m0, m1, m2, m3, out_ref):
        short = lines // packed
        low = jnp.zeros((short, LANES), F32)
        for s, m_ref in enumerate((m0, m1, m2, m3)):
            product = dot(x_ref[...], m_ref[...], ((1,), (1,)))
            match = id_ref[:, :1] == column_ids(s * part, where_ref, 1, (1, part))
            chosen = jnp.where(match, product, 0.0).astype(BF16)
            for t in range(packed):
                fold = (
                    lax.broadcasted_iota(jnp.int32, (part, LANES), 0) % rank + t * rank
                    == lax.broadcasted_iota(jnp.int32, (part, LANES), 1)
                ).astype(BF16)
                low = low + dot(chosen[t * short : (t + 1) * short, :], fold, ((1,), (0,)))
        out_ref[...] = low

    low = pl.pallas_call(
        low_body,
        grid=(half_rows // lines,),
        out_shape=shape(half_rows // packed, LANES, kind=F32),
        in_specs=[
            smem,
            pl.BlockSpec((lines, pair), lambda i: (i, 0)),
            pl.BlockSpec((lines, LANES), lambda i: (i, 0)),
        ]
        + [pl.BlockSpec((part, pair), lambda i: (0, 0))] * 4,
        out_specs=pl.BlockSpec((lines // packed, LANES), lambda i: (i, 0)),
        compiler_params=params,
        cost_estimate=cost(2 * half_rows * pair * columns, 2 * half_rows * pair),
    )(where, after(x_block, kept), id_rows, *maps)
    bit = 1
    while bit < half:
        low = low + flipped(low, bit)
        bit *= 2
    low = low.astype(BF16).reshape(half_rows // lines, lines // packed, packed, rank)
    low = low.transpose(0, 2, 1, 3).reshape(half_rows, rank)
    near = jnp.arange(held, dtype=jnp.int32) + here % half * held
    both = jnp.concatenate([near + my_half * half * held, near + (1 - my_half) * half * held])
    spread = jnp.where(
        half_ids[:, None] == jnp.repeat(both, rank)[None, :].astype(F32),
        jnp.tile(low, (1, 2 * held)),
        jnp.zeros((), BF16),
    )
    up_part = (ADAPTER_SCALE * dot(spread, half_cot, ((0,), (0,)))).reshape(2, own, out_width)


    arrived, up_part, kept = lax.optimization_barrier((arrived, up_part, kept))

    def add_body(kept_ref, arrived_ref, out_ref):
        for p in range(2):
            total = kept_ref[p * part : (p + 1) * part, :]
            total = total + arrived_ref[p * part : (p + 1) * part, :].astype(F32)
            out_ref[:, p * piece : (p + 1) * piece, :] = total.astype(BF16).reshape(
                half, piece, pair
            )

    sums = pl.pallas_call(
        add_body,
        out_shape=shape(half, own, pair),
        compiler_params=params,
        cost_estimate=cost(45000000000, 8 * half * own * pair),
    )(kept, arrived)
    home = exchange(after(sums, back))
    up_grad = (up_part[0] + swapped(after(up_part[1], sums))).astype(BF16)

    def unpack_rows(in_ref, out_ref):
        for j in range(half):
            for q in range(2):
                at = (q * half + j) * block
                out_ref[:, at : at + block] = in_ref[j, :, q * block : (q + 1) * block]

    gradient = pl.pallas_call(
        unpack_rows,
        out_shape=shape(rows, width),
        compiler_params=params,
        cost_estimate=cost(0, 4 * rows * width),
    )(back)

    def unpack_down(where_ref, in_ref, out_ref):
        for p in range(2):
            which = where_ref[1] if p == 0 else 1 - where_ref[1]
            target = pl.ds(pl.multiple_of(which * piece, piece), piece)
            for j in range(half):
                for q in range(2):
                    at = (q * half + j) * block
                    out_ref[target, at : at + block] = in_ref[
                        j, p * piece : (p + 1) * piece, q * block : (q + 1) * block
                    ]

    down_grad = pl.pallas_call(
        unpack_down,
        out_shape=shape(own, width),
        in_specs=[smem, vmem],
        out_specs=vmem,
        compiler_params=params,
        cost_estimate=cost(0, 4 * own * width),
    )(where, after(home, gradient))
    return gradient, down_grad.reshape(held, rank, width), up_grad.reshape(held, rank, out_width)


def on_device(x, cot, ids, frozen, down, up):
    n = lax.axis_size("adapt")
    own = down.shape[0] * down.shape[1]
    fits = (
        lax.axis_size("groups") == 2
        and x.shape[1] // n % (2 * LANES) == 0
        and down.shape[0] == 2
        and x.shape[0] == 2 * own == LANES
        and cot.shape[1] % LANES == 0
    )
    return (with_kernels if fits else in_xla)(x, cot, ids, frozen, down, up)


def solution(mesh):
    return jax.shard_map(
        on_device,
        mesh=mesh,
        in_specs=(
            P(("groups", "adapt"), None),
            P(("groups", "adapt"), None),
            P(("groups", "adapt")),
            P("adapt", None),
            P("adapt", None, None),
            P("adapt", None, None),
        ),
        out_specs=(
            P(("groups", "adapt"), None),
            P(("groups", "adapt"), None, None),
            P(("groups", "adapt"), None, None),
        ),
        check_vma=False,
    )
```

time: 357 us -> 258 us (0.72)
  waiting for transfers between devices: 221 us -> 144 us
  Pallas kernels: 0 us -> 48.2 us
  matrix products: 32.4 us -> 1.9 us
  local copies, waits for them, and re-layouts: 45.3 us -> 17.5 us
  starting transfers between devices: 47 us -> 39 us
  blocking collectives: 7.24 us -> 0 us
    all_to_all x8 -> x4, waiting for transfers between devices: 114 us -> 16.5 us  [exchange(): lax.all_to_all(parts, 'adapt', split_axis=0, concat_axis=0, tiled=True, a...]
    pallas_call x0 -> x10, Pallas kernels: none -> 48.2 us  [the longest x2 11.4 us: down_part(): pl.pallas_call(body, grid=(3, 2), out_shape=shape(2 * part, pair, kind=ki...]
    dot_general x10 -> x1, matrix products: 32.4 us -> 1.9 us  [dot(): return lax.dot_general(a, b, (dims, ((), ())), preferred_element_type=F32)]
    ppermute x5 -> x13, waiting for transfers between devices: 106 us -> 128 us  [the longest x5 78 us: swapped(): return lax.ppermute(part, 'adapt', [(i, (i + half) % n) for i in range(n)])]
    all_to_all x8 -> x4, starting transfers between devices: 39.2 us -> 19.6 us  [exchange(): lax.all_to_all(parts, 'adapt', split_axis=0, concat_axis=0, tiled=True, a...]
    reshape x6 -> x1, local copies, waits for them, and re-layouts: 19 us -> 0.12 us  [with_kernels(): low.astype(BF16).reshape(half_rows // lines, lines // packed, packed, rank)]
    ppermute x5 -> x13, starting transfers between devices: 7.77 us -> 19.4 us  [the longest x5 13.9 us: swapped(): return lax.ppermute(part, 'adapt', [(i, (i + half) % n) for i in range(n)])]
    all_to_all x1 -> x0, blocking collectives: 7.24 us -> none  [exchange(): lax.all_to_all(parts, 'adapt', split_axis=0, concat_axis=0, tiled=True, a...]
  transfers between devices with their start and end apart: 13 -> 17, of which waited for: 8 -> 8; matrix products, arithmetic and copies ran while one was open for 18% -> 5% of each run, Pallas kernels for 0% -> 18%
where the time goes in v2:
time: 258 us; the launch traced here: 257 us
  waiting for transfers between devices  144 us (56%)
  Pallas kernels  48.2 us (19%)
  starting transfers between devices  39 us (15%)
  local copies, waits for them, and re-layouts  17.5 us (7%)
  other arithmetic  4.87 us (2%)
    ppermute x5, waiting for transfers between devices, swapped(): return lax.ppermute(part, 'adapt', [(i, (i + half) % n) for i in range(n)])  78 us
    ppermute x5, waiting for transfers between devices, flipped(): return lax.ppermute(part, 'adapt', [(i, i ^ bit) for i in range(n)])  45.1 us
    all_to_all x4, starting transfers between devices, exchange(): lax.all_to_all(parts, 'adapt', split_axis=0, concat_axis=0, tiled=True, a...  19.6 us
    all_to_all x4, waiting for transfers between devices, exchange(): lax.all_to_all(parts, 'adapt', split_axis=0, concat_axis=0, tiled=True, a...  16.5 us
    ppermute x5, starting transfers between devices, swapped(): return lax.ppermute(part, 'adapt', [(i, (i + half) % n) for i in range(n)])  13.9 us
    unnamed x40, local copies, waits for them, and re-layouts  11.8 us
    pallas_call x2, Pallas kernels, down_part(): pl.pallas_call(body, grid=(3, 2), out_shape=shape(2 * part, pair, kind=ki...  11.4 us
    pallas_call x1, Pallas kernels, with_kernels(): pl.pallas_call(low_body, grid=(half_rows // lines,), out_shape=shape(half...  11.2 us
  transfers between devices with their start and end apart: 17, of which 8 were waited for; matrix products, arithmetic and copies ran while one was open for 5% of the time, Pallas kernels for 18%

profile of v2, /device:TPU:8, one launch (start us, length us, event | category | flops | bytes accessed | tf_op | source)
XLA Modules:
  0.0 256.8 jit_solution(7517428218698579801)
XLA Ops:
  3.5 4.3 %all-to-all-start = ((bf16[8,32,3200]{2,1,0:T(8,128)(2,1)}), bf16[8,32,3200]{2,1,0:T(8,128)(2,1)S(1)}, u32[]{:S(2)}, u32[]{:S(2)}) async-start(bf16[8,32,3200]{2,1,0:T(8,128)(2,1)} %shard_map.86), calls=%async_computation | async-start | bytes 3276800 | tf_op jit(solution)/shard_map/all_to_all | solution.py:197
  7.7 2.1 shard_map.85
  9.8 1.7 copy-done.1
  11.5 16.5 %all-to-all-done = bf16[8,32,3200]{2,1,0:T(8,128)(2,1)S(1)} async-done(((bf16[8,32,3200]{2,1,0:T(8,128)(2,1)}), bf16[8,32,3200]{2,1,0:T(8,128)(2,1)S(1)}, u32[]{:S(2)}, u32[]{:S(2)}) %all-to-all-start) | async-done | bytes 1638432 | tf_op jit(solution)/shard_map/all_to_all | solution.py:197
  29.1 4.9 %all-to-all-start.1 = ((bf16[8,128,1536]{2,1,0:T(8,128)(2,1)}), bf16[8,128,1536]{2,1,0:T(8,128)(2,1)}, u32[]{:S(2)}, u32[]{:S(2)}) async-start(bf16[8,128,1536]{2,1,0:T(8,128)(2,1)} %copy-done.1), calls=%async_computation.1 | async-start | bytes 6291456 | tf_op jit(solution)/shard_map/all_to_all | solution.py:197
  35.7 1.5 collective-permute-start.4
  37.2 2.6 %collective-permute-start.3 = (bf16[256,1536]{1,0:T(8,128)(2,1)S(1)}, bf16[256,1536]{1,0:T(8,128)(2,1)}, u32[]{:S(2)}, u32[]{:S(2)}) collective-permute-start(bf16[256,1536]{1,0:T(8,128)(2,1)S(1)} %bitcast.30), channel_id=1, source_target_pairs={{0,8},{1,9},{2,10},{3,11},{4,12},{5,13},{6,14},{7,15},{8,0},{9,1},... | collective-permute-start | bytes 2359304 | tf_op jit(solution)/shard_map/ppermute | solution.py:202
  39.8 1.8 constant_dynamic-slice_fusion
  42.6 2.6 %collective-permute-start.1 = (bf16[256,512]{1,0:T(8,128)(2,1)}, bf16[256,512]{1,0:T(8,128)(2,1)S(1)}, u32[]{:S(2)}, u32[]{:S(2)}) collective-permute-start(bf16[256,512]{1,0:T(8,128)(2,1)} %slice.24), channel_id=1, source_target_pairs={{0,8},{1,9},{2,10},{3,11},{4,12},{5,13},{6,14},{7,15},{8,0},{9,1},... | collective-permute-start | bytes 786440 | tf_op jit(solution)/shard_map/ppermute | solution.py:202
  45.2 57.2 %collective-permute-done.1.far_ref = bf16[256,512]{1,0:T(8,128)(2,1)S(1)} collective-permute-done((bf16[256,512]{1,0:T(8,128)(2,1)}, bf16[256,512]{1,0:T(8,128)(2,1)S(1)}, u32[]{:S(2)}, u32[]{:S(2)}) %collective-permute-start.1) | collective-permute-done | bytes 262176 | tf_op jit(solution)/shard_map/ppermute | solution.py:202
  102.6 1.5 collective-permute-start.6
  105.6 5.7 %shard_map.87 = (bf16[1024,1024]{1,0:T(8,128)(2,1)S(1)}, bf16[1024,1024]{1,0:T(8,128)(2,1)}, bf16[1024,512]{1,0:T(8,128)(2,1)S(1)}) custom-call(s32[3]{0:T(128)S(1)} %pad_add_fusion.where_ref, bf16[256,1536]{1,0:T(8,128)(2,1)S(1)} %bitcast.28, bf16[256,1536]{1,0:T(8,128)(2,1)} %collective-permute-done.2.twin_ref, ...), custom_call_target="tpu_custom_call" | custom-call | flops 2147483648 | bytes 8388608 | tf_op jit(solution)/shard_map/pallas_call | solution.py:340
  117.3 1.6 copy-done.2
  118.9 5.7 %shard_map.88 = bf16[512,1536]{1,0:T(8,128)(2,1)S(1)} custom-call(bf16[1024,1024]{1,0:T(8,128)(2,1)S(1)} %copy-done.2, bf16[1024,1536]{1,0:T(8,128)(2,1)} %bitcast.8.x_ref), custom_call_target="tpu_custom_call" | custom-call | flops 1610612736 | bytes 3145728 | tf_op jit(solution)/shard_map/pallas_call | solution.py:361
  124.6 2.9 %collective-permute-start.8 = (bf16[512,1536]{1,0:T(8,128)(2,1)S(1)}, bf16[512,1536]{1,0:T(8,128)(2,1)}, u32[]{:S(2)}, u32[]{:S(2)}) collective-permute-start(bf16[512,1536]{1,0:T(8,128)(2,1)S(1)} %shard_map.88), channel_id=1, source_target_pairs={{0,8},{1,9},{2,10},{3,11},{4,12},{5,13},{6,14},{7,15},{8,0},{9,1},... | collective-permute-start | bytes 4718600 | tf_op jit(solution)/shard_map/ppermute | solution.py:202
  127.4 3.9 %collective-permute-done.7.m3 = bf16[256,1536]{1,0:T(8,128)(2,1)} collective-permute-done((bf16[256,1536]{1,0:T(8,128)(2,1)}, bf16[256,1536]{1,0:T(8,128)(2,1)}, u32[]{:S(2)}, u32[]{:S(2)}) %collective-permute-start.7) | collective-permute-done | bytes 786464 | tf_op jit(solution)/shard_map/ppermute | solution.py:208
  131.3 8.3 %shard_map.89 = bf16[8,128,1536]{2,1,0:T(8,128)(2,1)} custom-call(bf16[1024,512]{1,0:T(8,128)(2,1)S(1)} %copy-done.7, bf16[1024,1024]{1,0:T(8,128)(2,1)} %copy-done.17, bf16[768,512]{1,0:T(8,128)(2,1)S(1)} %copy-done.12, bf16[768,512]{1,0:T(8,128)(2,1)S(1)} %copy-done.11, bf16[256,1536]{1,0:T(8,128)(2,1)S(1)} %bitcast.31, ...), custom_call_target="tpu_custom_call" | custom-call | flops 4831838208 | bytes 12582912 | tf_op jit(solution)/shard_map/pallas_call | solution.py:392
  139.6 4.4 %all-to-all-start.2 = ((bf16[8,128,1536]{2,1,0:T(8,128)(2,1)}), bf16[8,128,1536]{2,1,0:T(8,128)(2,1)}, u32[]{:S(2)}, u32[]{:S(2)}) async-start(bf16[8,128,1536]{2,1,0:T(8,128)(2,1)} %shard_map.89), calls=%async_computation.2 | async-start | bytes 6291456 | tf_op jit(solution)/shard_map/all_to_all | solution.py:197
  144.0 1.6 copy-done.3
  145.6 5.7 %shard_map.91.kept_ref = f32[512,1536]{1,0:T(8,128)S(1)} custom-call(bf16[1024,1024]{1,0:T(8,128)(2,1)S(1)} %copy-done.3, bf16[1024,1536]{1,0:T(8,128)(2,1)} %bitcast.8.x_ref), custom_call_target="tpu_custom_call" | custom-call | flops 1610612736 | bytes 3145728 | tf_op jit(solution)/shard_map/pallas_call | solution.py:361
  151.3 1.7 copy-done.4
  153.0 11.2 %shard_map.92 = f32[256,128]{1,0:T(8,128)S(1)} custom-call(s32[3]{0:T(128)S(1)} %pad_add_fusion.where_ref, bf16[1024,1536]{1,0:T(8,128)(2,1)} %bitcast.8.x_ref, f32[1024,128]{1,0:T(8,128)S(1)} %copy-done.14, bf16[256,1536]{1,0:T(8,128)(2,1)S(1)} %bitcast.32, bf16[256,1536]{1,0:T(8,128)(2,1)} %collective-permute-done.3.m1, ...), custom_call_target="tpu_custom_call" | custom-call | flops 3221225472 | bytes 3145728 | tf_op jit(solution)/shard_map/pallas_call | solution.py:427
  165.6 1.5 collective-permute-start.10
  167.2 16.8 %collective-permute-done.10 = f32[256,128]{1,0:T(8,128)S(1)} collective-permute-done((f32[256,128]{1,0:T(8,128)S(1)}, f32[256,128]{1,0:T(8,128)S(1)}, u32[]{:S(2)}, u32[]{:S(2)}) %collective-permute-start.10) | collective-permute-done | bytes 131104 | tf_op jit(solution)/shard_map/ppermute | solution.py:205
  184.4 26.9 %collective-permute-done.11 = f32[256,128]{1,0:T(8,128)S(1)} collective-permute-done((f32[256,128]{1,0:T(8,128)S(1)}, f32[256,128]{1,0:T(8,128)S(1)}, u32[]{:S(2)}, u32[]{:S(2)}) %collective-permute-start.11) | collective-permute-done | bytes 131104 | tf_op jit(solution)/shard_map/ppermute | solution.py:205
  212.6 1.9 convolution_multiply_fusion
  214.5 2.6 %shard_map.93 = bf16[8,64,1536]{2,1,0:T(8,128)(2,1)S(1)} custom-call(f32[512,1536]{1,0:T(8,128)} %copy-done.4, bf16[512,1536]{1,0:T(8,128)(2,1)} %collective-permute-done.8.arrived_ref), custom_call_target="tpu_custom_call" | custom-call | flops 44999999488 | bytes 6291456 | tf_op jit(solution)/shard_map/pallas_call | solution.py:467
  218.3 6.0 %all-to-all-start.3 = ((bf16[8,64,1536]{2,1,0:T(8,128)(2,1)}), bf16[8,64,1536]{2,1,0:T(8,128)(2,1)S(1)}, u32[]{:S(2)}, u32[]{:S(2)}) async-start(bf16[8,64,1536]{2,1,0:T(8,128)(2,1)} %copy-done.5), calls=%async_computation.3 | async-start | bytes 3145728 | tf_op jit(solution)/shard_map/all_to_all | solution.py:197
  224.3 5.5 %collective-permute-start.12 = (f32[64,512]{1,0:T(8,128)S(1)}, f32[64,512]{1,0:T(8,128)S(1)}, u32[]{:S(2)}, u32[]{:S(2)}) collective-permute-start(f32[64,512]{1,0:T(8,128)S(1)} %slice_bitcast_fusion), channel_id=1, source_target_pairs={{0,8},{1,9},{2,10},{3,11},{4,12},{5,13},{6,14},{7,15},{8,0},{9,1},... | collective-permute-start | bytes 393224 | tf_op jit(solution)/shard_map/ppermute | solution.py:202
  229.8 20.8 %collective-permute-done.12 = f32[64,512]{1,0:T(8,128)S(1)} collective-permute-done((f32[64,512]{1,0:T(8,128)S(1)}, f32[64,512]{1,0:T(8,128)S(1)}, u32[]{:S(2)}, u32[]{:S(2)}) %collective-permute-start.12) | collective-permute-done | bytes 131104 | tf_op jit(solution)/shard_map/ppermute | solution.py:202
  251.3 3.8 %shard_map.90 = bf16[128,12288]{1,0:T(8,128)(2,1)} custom-call(bf16[8,128,1536]{2,1,0:T(8,128)(2,1)} %all-to-all-done.2.in_ref), custom_call_target="tpu_custom_call" | custom-call | bytes 6291456 | tf_op jit(solution)/shard_map/pallas_call | solution.py:482
  255.0 1.8 shard_map.94
  (81 shorter events, 19.1 us)
Async XLA Ops:
  0.6 1.5 copy-start.16
  0.7 1.5 copy-start.15
  3.5 24.5 %all-to-all-start = ((bf16[8,32,3200]{2,1,0:T(8,128)(2,1)}), bf16[8,32,3200]{2,1,0:T(8,128)(2,1)S(1)}, u32[]{:S(2)}, u32[]{:S(2)}) async-start(bf16[8,32,3200]{2,1,0:T(8,128)(2,1)} %shard_map.86), calls=%async_computation | async-start | bytes 3276800 | tf_op jit(solution)/shard_map/all_to_all | solution.py:197
  9.8 1.7 copy-start.1
  29.1 88.1 %all-to-all-start.1 = ((bf16[8,128,1536]{2,1,0:T(8,128)(2,1)}), bf16[8,128,1536]{2,1,0:T(8,128)(2,1)}, u32[]{:S(2)}, u32[]{:S(2)}) async-start(bf16[8,128,1536]{2,1,0:T(8,128)(2,1)} %copy-done.1), calls=%async_computation.1 | async-start | bytes 6291456 | tf_op jit(solution)/shard_map/all_to_all | solution.py:197
  35.5 75.8 %copy-start.8 = (bf16[8,32,1536]{2,1,0:T(8,128)(2,1)}, bf16[8,32,1536]{2,1,0:T(8,128)(2,1)S(1)}, u32[]{:S(2)}) copy-start(bf16[8,32,1536]{2,1,0:T(8,128)(2,1)S(1)} %get-tuple-element.43) | copy-start | bytes 2359300
  35.5 66.9 %collective-permute-start.2 = (bf16[256,1536]{1,0:T(8,128)(2,1)S(1)}, bf16[256,1536]{1,0:T(8,128)(2,1)}, u32[]{:S(2)}, u32[]{:S(2)}) collective-permute-start(bf16[256,1536]{1,0:T(8,128)(2,1)S(1)} %bitcast.26), channel_id=1, source_target_pairs={{0,1},{1,0},{2,3},{3,2},{4,5},{5,4},{6,7},{7,6},{8,9},{9,8},{10,11... | collective-permute-start | bytes 2359304 | tf_op jit(solution)/shard_map/ppermute | solution.py:205
  35.7 66.7 %collective-permute-start.4 = (bf16[256,1536]{1,0:T(8,128)(2,1)S(1)}, bf16[256,1536]{1,0:T(8,128)(2,1)}, u32[]{:S(2)}, u32[]{:S(2)}) collective-permute-start(bf16[256,1536]{1,0:T(8,128)(2,1)S(1)} %bitcast.29), channel_id=1, source_target_pairs={{0,16},{16,0},{1,17},{17,1},{2,18},{18,2},{3,19},{19,3},{4,20},{20... | collective-permute-start | bytes 2359304 | tf_op jit(solution)/shard_map/ppermute | solution.py:208
  37.2 65.2 %collective-permute-start.3 = (bf16[256,1536]{1,0:T(8,128)(2,1)S(1)}, bf16[256,1536]{1,0:T(8,128)(2,1)}, u32[]{:S(2)}, u32[]{:S(2)}) collective-permute-start(bf16[256,1536]{1,0:T(8,128)(2,1)S(1)} %bitcast.30), channel_id=1, source_target_pairs={{0,8},{1,9},{2,10},{3,11},{4,12},{5,13},{6,14},{7,15},{8,0},{9,1},... | collective-permute-start | bytes 2359304 | tf_op jit(solution)/shard_map/ppermute | solution.py:202
  41.6 60.8 %collective-permute-start = (bf16[384,512]{1,0:T(8,128)(2,1)}, bf16[384,512]{1,0:T(8,128)(2,1)}, u32[]{:S(2)}, u32[]{:S(2)}) collective-permute-start(bf16[384,512]{1,0:T(8,128)(2,1)} %constant_dynamic-slice_fusion), channel_id=1, source_target_pairs={{0,8},{1,9},{2,10},{3,11},{4,12},{5,13},{6,14},{7,15},{8,0},{9,1},... | collective-permute-start | bytes 1179656 | tf_op jit(solution)/shard_map/ppermute | solution.py:202
  42.6 59.8 %collective-permute-start.1 = (bf16[256,512]{1,0:T(8,128)(2,1)}, bf16[256,512]{1,0:T(8,128)(2,1)S(1)}, u32[]{:S(2)}, u32[]{:S(2)}) collective-permute-start(bf16[256,512]{1,0:T(8,128)(2,1)} %slice.24), channel_id=1, source_target_pairs={{0,8},{1,9},{2,10},{3,11},{4,12},{5,13},{6,14},{7,15},{8,0},{9,1},... | collective-permute-start | bytes 786440 | tf_op jit(solution)/shard_map/ppermute | solution.py:202
  102.4 2.9 %collective-permute-start.5 = (bf16[256,512]{1,0:T(8,128)(2,1)S(1)}, bf16[256,512]{1,0:T(8,128)(2,1)}, u32[]{:S(2)}, u32[]{:S(2)}) collective-permute-start(bf16[256,512]{1,0:T(8,128)(2,1)S(1)} %collective-permute-done.1.far_ref), channel_id=1, source_target_pairs={{0,1},{1,0},{2,3},{3,2},{4,5},{5,4},{6,7},{7,6},{8,9},{9,8},{10,11... | collective-permute-start | bytes 786440 | tf_op jit(solution)/shard_map/ppermute | solution.py:205
  102.6 12.1 %collective-permute-start.6 = (bf16[384,512]{1,0:T(8,128)(2,1)}, bf16[384,512]{1,0:T(8,128)(2,1)S(1)}, u32[]{:S(2)}, u32[]{:S(2)}) collective-permute-start(bf16[384,512]{1,0:T(8,128)(2,1)} %collective-permute-done), channel_id=1, source_target_pairs={{0,16},{16,0},{1,17},{17,1},{2,18},{18,2},{3,19},{19,3},{4,20},{20... | collective-permute-start | bytes 1179656 | tf_op jit(solution)/shard_map/ppermute | solution.py:208
  104.8 26.5 %collective-permute-start.7 = (bf16[256,1536]{1,0:T(8,128)(2,1)}, bf16[256,1536]{1,0:T(8,128)(2,1)}, u32[]{:S(2)}, u32[]{:S(2)}) collective-permute-start(bf16[256,1536]{1,0:T(8,128)(2,1)} %collective-permute-done.3.m1), channel_id=1, source_target_pairs={{0,16},{16,0},{1,17},{17,1},{2,18},{18,2},{3,19},{19,3},{4,20},{20... | collective-permute-start | bytes 2359304 | tf_op jit(solution)/shard_map/ppermute | solution.py:208
  105.6 5.8 %copy-start.13 = (f32[1024,128]{1,0:T(8,128)}, f32[1024,128]{1,0:T(8,128)S(1)}, u32[]{:S(2)}) copy-start(f32[1024,128]{1,0:T(8,128)S(1)} %broadcast_in_dim.12.id_ref) | copy-start | bytes 1572868
  113.6 2.2 copy-start.19
  117.3 1.6 copy-start.2
  118.8 12.4 %copy-start.7 = (bf16[1024,512]{1,0:T(8,128)(2,1)S(1)}, bf16[1024,512]{1,0:T(8,128)(2,1)}, u32[]{:S(2)}) copy-start(bf16[1024,512]{1,0:T(8,128)(2,1)} %copy-done.6) | copy-start | bytes 3145732
  118.9 12.4 %copy-start.9 = (bf16[8,32,1536]{2,1,0:T(8,128)(2,1)S(1)}, bf16[8,32,1536]{2,1,0:T(8,128)(2,1)}, u32[]{:S(2)}) copy-start(bf16[8,32,1536]{2,1,0:T(8,128)(2,1)} %copy-done.8) | copy-start | bytes 2359300
  118.9 12.4 %copy-start.11 = (bf16[768,512]{1,0:T(8,128)(2,1)S(1)}, bf16[768,512]{1,0:T(8,128)(2,1)}, u32[]{:S(2)}) copy-start(bf16[768,512]{1,0:T(8,128)(2,1)} %get-tuple-element.45.high_w) | copy-start | bytes 2359300
  118.9 12.4 %copy-start.12 = (bf16[768,512]{1,0:T(8,128)(2,1)S(1)}, bf16[768,512]{1,0:T(8,128)(2,1)}, u32[]{:S(2)}) copy-start(bf16[768,512]{1,0:T(8,128)(2,1)} %get-tuple-element.46.low_w) | copy-start | bytes 2359300
  124.6 90.0 %collective-permute-start.8 = (bf16[512,1536]{1,0:T(8,128)(2,1)S(1)}, bf16[512,1536]{1,0:T(8,128)(2,1)}, u32[]{:S(2)}, u32[]{:S(2)}) collective-permute-start(bf16[512,1536]{1,0:T(8,128)(2,1)S(1)} %shard_map.88), channel_id=1, source_target_pairs={{0,8},{1,9},{2,10},{3,11},{4,12},{5,13},{6,14},{7,15},{8,0},{9,1},... | collective-permute-start | bytes 4718600 | tf_op jit(solution)/shard_map/ppermute | solution.py:202
  139.6 78.7 %all-to-all-start.2 = ((bf16[8,128,1536]{2,1,0:T(8,128)(2,1)}), bf16[8,128,1536]{2,1,0:T(8,128)(2,1)}, u32[]{:S(2)}, u32[]{:S(2)}) async-start(bf16[8,128,1536]{2,1,0:T(8,128)(2,1)} %shard_map.89), calls=%async_computation.2 | async-start | bytes 6291456 | tf_op jit(solution)/shard_map/all_to_all | solution.py:197
  144.0 1.6 copy-start.3
  145.6 7.4 %copy-start.10 = (bf16[8,32,1536]{2,1,0:T(8,128)(2,1)S(1)}, bf16[8,32,1536]{2,1,0:T(8,128)(2,1)}, u32[]{:S(2)}) copy-start(bf16[8,32,1536]{2,1,0:T(8,128)(2,1)} %copy-done.8) | copy-start | bytes 2359300
  145.6 7.4 %copy-start.14 = (f32[1024,128]{1,0:T(8,128)S(1)}, f32[1024,128]{1,0:T(8,128)}, u32[]{:S(2)}) copy-start(f32[1024,128]{1,0:T(8,128)} %copy-done.13) | copy-start | bytes 1572868
  151.3 1.7 copy-start.4
  164.2 1.4 collective-permute-start.9
  165.6 18.4 %collective-permute-start.10 = (f32[256,128]{1,0:T(8,128)S(1)}, f32[256,128]{1,0:T(8,128)S(1)}, u32[]{:S(2)}, u32[]{:S(2)}) collective-permute-start(f32[256,128]{1,0:T(8,128)S(1)} %add.54), channel_id=1, source_target_pairs={{0,2},{1,3},{2,0},{3,1},{4,6},{5,7},{6,4},{7,5},{8,10},{9,11},{10,... | collective-permute-start | bytes 393224 | tf_op jit(solution)/shard_map/ppermute | solution.py:205
  184.0 27.2 %collective-permute-start.11 = (f32[256,128]{1,0:T(8,128)S(1)}, f32[256,128]{1,0:T(8,128)S(1)}, u32[]{:S(2)}, u32[]{:S(2)}) collective-permute-start(f32[256,128]{1,0:T(8,128)S(1)} %add.55), channel_id=1, source_target_pairs={{0,4},{1,5},{2,6},{3,7},{4,0},{5,1},{6,2},{7,3},{8,12},{9,13},{10,... | collective-permute-start | bytes 393224 | tf_op jit(solution)/shard_map/ppermute | solution.py:205
  218.3 36.7 %all-to-all-start.3 = ((bf16[8,64,1536]{2,1,0:T(8,128)(2,1)}), bf16[8,64,1536]{2,1,0:T(8,128)(2,1)S(1)}, u32[]{:S(2)}, u32[]{:S(2)}) async-start(bf16[8,64,1536]{2,1,0:T(8,128)(2,1)} %copy-done.5), calls=%async_computation.3 | async-start | bytes 3145728 | tf_op jit(solution)/shard_map/all_to_all | solution.py:197
  224.3 26.3 %collective-permute-start.12 = (f32[64,512]{1,0:T(8,128)S(1)}, f32[64,512]{1,0:T(8,128)S(1)}, u32[]{:S(2)}, u32[]{:S(2)}) collective-permute-start(f32[64,512]{1,0:T(8,128)S(1)} %slice_bitcast_fusion), channel_id=1, source_target_pairs={{0,8},{1,9},{2,10},{3,11},{4,12},{5,13},{6,14},{7,15},{8,0},{9,1},... | collective-permute-start | bytes 393224 | tf_op jit(solution)/shard_map/ppermute | solution.py:202
  (5 other events, 6.0 us)

commit v3 on v2

--- a/solution.py
+++ b/solution.py
@@ -214,74 +214,6 @@
     def cost(flops, moved):
         return pl.CostEstimate(flops=flops, bytes_accessed=moved, transcendentals=0)
 
-    frozen_piece = lax.dynamic_slice_in_dim(frozen, group * (block // 2), block // 2, axis=0)
-    down_piece = lax.dynamic_slice_in_dim(down.reshape(own, width), group * piece, piece, axis=0)
-    cot_at = pair
-    up_at = cot_at + 2 * out_width
-    id_at = up_at + out_width
-    wide = id_at + LANES
-
-    def pack_small(down_ref, cot_ref, up_ref, id_ref, out_ref):
-        for j in range(half):
-            c = j % 2
-            for q in range(2):
-                out_ref[j, :, q * block : (q + 1) * block] = down_ref[
-                    :, (q * half + j) * block : (q * half + j + 1) * block
-                ]
-                out_ref[j, :, cot_at + q * out_width : cot_at + (q + 1) * out_width] = cot_ref[
-                    (2 * c + q) * piece : (2 * c + q + 1) * piece, :
-                ]
-            out_ref[j, :, up_at:id_at] = up_ref[c * piece : (c + 1) * piece, :]
-            out_ref[j, :, id_at:] = id_ref[...]
-
-    id_line = jnp.broadcast_to(ids.astype(BF16)[None, :], (piece, LANES))
-    small = pl.pallas_call(
-        pack_small,
-        out_shape=shape(half, piece, wide),
-        compiler_params=params,
-        cost_estimate=cost(0, 4 * half * piece * wide),
-    )(down_piece, cot, up.reshape(own, out_width), id_line)
-    small = exchange(small)
-
-    def pack_rows(x_ref, out_ref):
-        for j in range(half):
-            for q in range(2):
-                out_ref[j, :, q * block : (q + 1) * block] = x_ref[
-                    :, (q * half + j) * block : (q * half + j + 1) * block
-                ]
-
-    x_parts = pl.pallas_call(
-        pack_rows,
-        out_shape=shape(half, rows, pair),
-        compiler_params=params,
-        cost_estimate=cost(0, 4 * rows * width),
-    )(x)
-
-    x_parts, small = lax.optimization_barrier((x_parts, small))
-    x_block = exchange(x_parts).reshape(half_rows, pair)
-    down_near = small[:, :, :pair].reshape(half * piece, pair)
-    shared = small[:, :, pair:id_at].reshape(half * piece, 3 * out_width)
-    frozen_near = swapped(after(frozen_piece, small))
-    shared_far = swapped(shared[:, 2 * out_width :])
-    shared_twin = flipped(shared, 1)
-    down_far = swapped(down_near)
-    near_cross = other_group(down_near)
-    frozen_near, shared_far, shared_twin, down_far, near_cross = lax.optimization_barrier(
-        (frozen_near, shared_far, shared_twin, down_far, near_cross)
-    )
-    up_far_twin = flipped(shared_far, 1)
-    frozen_cross = other_group(frozen_near)
-    far_cross = other_group(down_far)
-    half_ids = small[:, 0, id_at:].reshape(half_rows).astype(F32)
-    id_rows = jnp.broadcast_to(half_ids[:, None], (half_rows, LANES))
-    id_lines = jnp.broadcast_to(half_ids[None, :], (8, half_rows))
-    maps = (down_near, down_far, near_cross, far_cross)
-    first_piece = jnp.where(group == 0, frozen_near, frozen_cross)
-    last_piece = jnp.where(group == 0, frozen_cross, frozen_near)
-    frozen_far = jnp.concatenate([first_piece, last_piece], axis=0)
-    frozen_low = jnp.where(my_half == 0, frozen, frozen_far)
-    frozen_high = jnp.where(my_half == 0, frozen_far, frozen)
-
     part = half * piece
     columns = 4 * part
 
@@ -294,14 +226,13 @@
         which = jnp.where(crossed == 0, where[1], 1 - where[1])
         return ((side * half + owner) * held + (which * piece + within) // rank).astype(F32)
 
+
     where = jnp.stack([my_half, group, core])
 
     def grads_body(
         where_ref,
         mine_ref,
         twin_ref,
-        far_ref,
-        far_twin_ref,
         id_ref,
         line_ref,
         by_row_ref,
@@ -318,16 +249,14 @@
                     cot_ref[pl.ds(target, piece), :] = ref[
                         at : at + piece, q * out_width : (q + 1) * out_width
                     ]
-            for far, pieces in enumerate(
-                (
-                    (mine_ref[at : at + piece, 2 * out_width :], twin_ref[at : at + piece, 2 * out_width :]),
-                    (far_ref[at : at + piece, :], far_twin_ref[at : at + piece, :]),
-                )
-            ):
-                for side, value in zip((c, 1 - c), pieces):
+            for far in range(2):
+                lo, hi = (2 + far) * out_width, (3 + far) * out_width
+                for ref, side in ((mine_ref, c), (twin_ref, 1 - c)):
                     crossed = jnp.where(side == where_ref[1], 0, 1)
                     target = (crossed * 2 + far) * part + at
-                    up_scratch[pl.ds(pl.multiple_of(target, piece), piece), :] = value
+                    up_scratch[pl.ds(pl.multiple_of(target, piece), piece), :] = ref[
+                        at : at + piece, lo:hi
+                    ]
         step = 2 * part
         for at in range(0, columns, step):
             product = dot(cot_ref[...], up_scratch[at : at + step, :], ((1,), (1,)))
@@ -337,6 +266,221 @@
             match = column_ids(at, where_ref, 0, (step, 1)) == line_ref[:1, :]
             by_column_ref[at : at + step, :] = jnp.where(match, product, 0.0).astype(BF16)
 
+    low_frozen = jnp.where(my_half == 0, frozen, frozen_far)
+    high_frozen = jnp.where(my_half == 0, frozen_far, frozen)
+    base = dot(half_cot, jnp.concatenate([low_frozen, high_frozen], axis=0), ((1,), (1,)))
+    lora = dot(grads_near, down_near_all, ((0,), (0,))) + dot(
+        grads_far, down_far_all, ((0,), (0,))
+    )
+    gradient = (base + ADAPTER_SCALE * lora).astype(BF16).reshape(half, rows, 2 * block)
+
+    x_block = jnp.concatenate([x_first, x_second], axis=1)
+    fold = (
+        jnp.arange(half * own, dtype=jnp.int32)[:, None] % rank
+        == jnp.arange(LANES, dtype=jnp.int32)[None, :]
+    ).astype(BF16)
+
+    def low_part(maps, adapters):
+        picked = jnp.where(
+            half_ids[:, None] == adapters[None, :], dot(x_block, maps, ((1,), (1,))), 0.0
+        ).astype(BF16)
+        return dot(picked, fold, ((1,), (0,)))
+
+    low = (low_part(down_near_all, near_ids) + low_part(down_far_all, far_ids)).astype(BF16)
+    gradient = jnp.concatenate([gradient, low.reshape(half, rows, LANES)], axis=2)
+    gradient = exchange(after(gradient, second))
+    low = gradient[:, :, 2 * block : 2 * block + rank].astype(F32).sum(axis=0).astype(BF16)
+    gradient = gradient[:, :, : 2 * block].reshape(half, rows, 2, block)
+    gradient = gradient.transpose(1, 2, 0, 3).reshape(rows, width)
+
+    pack = LANES // rank
+    low_rows = low.reshape(pack, rows // pack, rank).transpose(1, 0, 2).reshape(rows // pack, LANES)
+    low_rows = jnp.pad(low_rows, ((0, own - rows // pack), (0, 0)))
+    sum_first = jnp.concatenate(
+        [
+            sum_first.reshape(half, own, block),
+            jnp.broadcast_to(low_rows[None], (half, own, LANES)),
+        ],
+        axis=2,
+    )
+    sum_first = exchange(sum_first)
+    sum_second = exchange(after(sum_second.reshape(half, own, block), sum_first))
+    low = sum_first[:, : rows // pack, block:].reshape(half, rows // pack, pack, rank)
+    low = low.transpose(0, 2, 1, 3).reshape(half * rows, rank)
+    down_grad = jnp.stack([sum_first[:, :, :block], sum_second], axis=0)
+    down_grad = down_grad.transpose(2, 0, 1, 3).reshape(held, rank, width)
+
+    pair = jnp.arange(held, dtype=jnp.int32) + here % half * held
+    pair = jnp.concatenate([pair + my_half * half * held, pair + (1 - my_half) * half * held])
+    spread = jnp.where(
+        half_ids[:, None] == jnp.repeat(pair, rank)[None, :],
+        jnp.tile(low, (1, 2 * held)),
+        jnp.zeros((), BF16),
+    )
+    up_part = (ADAPTER_SCALE * dot(spread, half_cot, ((0,), (0,)))).reshape(2, own, out_width)
+    up_grad = (up_part[0] + swapped(up_part[1])).astype(BF16)
+    return gradient, down_grad, up_grad.reshape(held, rank, out_width)
+
+
+def shape(*dims, kind=BF16):
+    return jax.ShapeDtypeStruct(dims, kind)
+
+
+def with_kernels(x, cot, ids, frozen, down, up):
+    n = lax.axis_size("adapt")
+    half = n // 2
+    rows, width = x.shape
+    out_width = cot.shape[1]
+    held, rank, _ = down.shape
+    own = held * rank
+    piece = own // 2
+    block = width // n
+    pair = 2 * block
+    half_rows = half * rows
+    halves = [list(range(half)), list(range(half, n))]
+    here = lax.axis_index("adapt")
+    group = lax.axis_index("groups")
+    my_half = here // half
+    core = here % 2
+
+    def exchange(parts):
+        return lax.all_to_all(
+            parts, "adapt", split_axis=0, concat_axis=0, tiled=True, axis_index_groups=halves
+        )
+
+    def swapped(part):
+        return lax.ppermute(part, "adapt", [(i, (i + half) % n) for i in range(n)])
+
+    def flipped(part, bit):
+        return lax.ppermute(part, "adapt", [(i, i ^ bit) for i in range(n)])
+
+    def other_group(part):
+        return lax.ppermute(part, "groups", [(0, 1), (1, 0)])
+
+    smem = pl.BlockSpec(memory_space=pltpu.SMEM)
+    vmem = pl.BlockSpec(memory_space=pltpu.VMEM)
+    params = pltpu.CompilerParams(vmem_limit_bytes=VMEM_BYTES)
+
+    def cost(flops, moved):
+        return pl.CostEstimate(flops=flops, bytes_accessed=moved, transcendentals=0)
+
+    frozen_piece = lax.dynamic_slice_in_dim(frozen, group * (block // 2), block // 2, axis=0)
+    down_piece = lax.dynamic_slice_in_dim(down.reshape(own, width), group * piece, piece, axis=0)
+    cot_at = pair
+    up_at = cot_at + 2 * out_width
+    id_at = up_at + 2 * out_width
+    wide = id_at + LANES
+    up_near = up.reshape(own, out_width)
+    up_far = swapped(up_near)
+    frozen_near = swapped(after(frozen_piece, up_far))
+
+    def pack_small(down_ref, cot_ref, near_ref, far_ref, id_ref, out_ref):
+        for j in range(half):
+            c = j % 2
+            for q in range(2):
+                out_ref[j, :, q * block : (q + 1) * block] = down_ref[
+                    :, (q * half + j) * block : (q * half + j + 1) * block
+                ]
+                out_ref[j, :, cot_at + q * out_width : cot_at + (q + 1) * out_width] = cot_ref[
+                    (2 * c + q) * piece : (2 * c + q + 1) * piece, :
+                ]
+            for q, up_ref in enumerate((near_ref, far_ref)):
+                out_ref[j, :, up_at + q * out_width : up_at + (q + 1) * out_width] = up_ref[
+                    c * piece : (c + 1) * piece, :
+                ]
+            out_ref[j, :, id_at:] = id_ref[...]
+
+    id_line = jnp.broadcast_to(ids.astype(BF16)[None, :], (piece, LANES))
+    small = pl.pallas_call(
+        pack_small,
+        out_shape=shape(half, piece, wide),
+        compiler_params=params,
+        cost_estimate=cost(0, 4 * half * piece * wide),
+    )(down_piece, cot, up_near, up_far, id_line)
+    small = exchange(small)
+
+    def pack_rows(x_ref, out_ref):
+        for j in range(half):
+            for q in range(2):
+                out_ref[j, :, q * block : (q + 1) * block] = x_ref[
+                    :, (q * half + j) * block : (q * half + j + 1) * block
+                ]
+
+    x_parts = pl.pallas_call(
+        pack_rows,
+        out_shape=shape(half, rows, pair),
+        compiler_params=params,
+        cost_estimate=cost(0, 4 * rows * width),
+    )(x)
+
+    x_parts, small, frozen_near = lax.optimization_barrier((x_parts, small, frozen_near))
+    down_near = small[:, :, :pair].reshape(half * piece, pair)
+    shared = small[:, :, pair:id_at].reshape(half * piece, 4 * out_width)
+    shared_twin = flipped(shared, 1)
+    x_block = exchange(after(x_parts, shared_twin)).reshape(half_rows, pair)
+    down_far = swapped(down_near)
+    near_cross = other_group(down_near)
+    frozen_cross = other_group(frozen_near)
+    half_ids = small[:, 0, id_at:].reshape(half_rows).astype(F32)
+    id_rows = jnp.broadcast_to(half_ids[:, None], (half_rows, LANES))
+    id_lines = jnp.broadcast_to(half_ids[None, :], (8, half_rows))
+    first_piece = jnp.where(group == 0, frozen_near, frozen_cross)
+    last_piece = jnp.where(group == 0, frozen_cross, frozen_near)
+    frozen_far = jnp.concatenate([first_piece, last_piece], axis=0)
+    frozen_low = jnp.where(my_half == 0, frozen, frozen_far)
+    frozen_high = jnp.where(my_half == 0, frozen_far, frozen)
+
+    part = half * piece
+    columns = 4 * part
+
+    def column_ids(at, where, axis, dims):
+        column = lax.broadcasted_iota(jnp.int32, dims, axis) + at
+        crossed, rest = column // (2 * part), column % (2 * part)
+        far, rest = rest // part, rest % part
+        owner, within = rest // piece, rest % piece
+        side = jnp.where(far == 0, where[0], 1 - where[0])
+        which = jnp.where(crossed == 0, where[1], 1 - where[1])
+        return ((side * half + owner) * held + (which * piece + within) // rank).astype(F32)
+
+    where = jnp.stack([my_half, group, core])
+
+    def grads_body(
+        where_ref,
+        mine_ref,
+        twin_ref,
+        id_ref,
+        line_ref,
+        by_row_ref,
+        by_column_ref,
+        cot_ref,
+        up_scratch,
+    ):
+        c = where_ref[2]
+        for owner in range(half):
+            at = owner * piece
+            for q in range(2):
+                for ref, side in ((mine_ref, c), (twin_ref, 1 - c)):
+                    target = pl.multiple_of(owner * rows + (2 * side + q) * piece, piece)
+                    cot_ref[pl.ds(target, piece), :] = ref[
+                        at : at + piece, q * out_width : (q + 1) * out_width
+                    ]
+            for far in range(2):
+                lo, hi = (2 + far) * out_width, (3 + far) * out_width
+                for ref, side in ((mine_ref, c), (twin_ref, 1 - c)):
+                    crossed = jnp.where(side == where_ref[1], 0, 1)
+                    target = (crossed * 2 + far) * part + at
+                    up_scratch[pl.ds(pl.multiple_of(target, piece), piece), :] = ref[
+                        at : at + piece, lo:hi
+                    ]
+        step = 2 * part
+        for at in range(0, columns, step):
+            product = dot(cot_ref[...], up_scratch[at : at + step, :], ((1,), (1,)))
+            match = id_ref[:, :1] == column_ids(at, where_ref, 1, (1, step))
+            by_row_ref[:, at : at + step] = jnp.where(match, product, 0.0).astype(BF16)
+            product = dot(up_scratch[at : at + step, :], cot_ref[...], ((1,), (1,)))
+            match = column_ids(at, where_ref, 0, (step, 1)) == line_ref[:1, :]
+            by_column_ref[at : at + step, :] = jnp.where(match, product, 0.0).astype(BF16)
+
     by_row, by_column, half_cot = pl.pallas_call(
         grads_body,
         out_shape=(
@@ -344,35 +488,15 @@
             shape(columns, half_rows),
             shape(half_rows, out_width),
         ),
-        in_specs=[smem] + [vmem] * 6,
+        in_specs=[smem] + [vmem] * 4,
         out_specs=(vmem, vmem, vmem),
         scratch_shapes=[pltpu.VMEM((columns, out_width), BF16)],
         compiler_params=params,
         cost_estimate=cost(4 * half_rows * columns * out_width, 8 * half_rows * columns),
-    )(where, shared, shared_twin, shared_far, up_far_twin, id_rows, id_lines)
-
-    def down_part(far, values, kind):
-        def body(grads_ref, x_ref, out_ref):
-            out_ref[...] = (
-                ADAPTER_SCALE * dot(grads_ref[...], x_ref[...], ((1,), (0,)))
-            ).astype(kind)
-
-        tile = pair // 3
-        return pl.pallas_call(
-            body,
-            grid=(3, 2),
-            out_shape=shape(2 * part, pair, kind=kind),
-            in_specs=[
-                pl.BlockSpec((part, half_rows), lambda c, p: (2 * p + far, 0)),
-                pl.BlockSpec((half_rows, tile), lambda c, p: (0, c)),
-            ],
-            out_specs=pl.BlockSpec((part, tile), lambda c, p: (p, c)),
-            compiler_params=params,
-            cost_estimate=cost(4 * part * half_rows * pair, 2 * half_rows * pair),
-        )(by_column, values)
-
-    sent = down_part(1, x_block, BF16)
-    arrived = swapped(sent)
+    )(where, shared, shared_twin, id_rows, id_lines)
+
+    far_cross = other_group(after(down_far, half_cot, frozen_low, frozen_high))
+    maps = (down_near, down_far, near_cross, far_cross)
 
     lines = 2 * rows
 
@@ -388,7 +512,171 @@
                 )
             out_ref[:, :, lo:hi] = total.astype(BF16).reshape(lines // rows, rows, block)
 
-    cot_later = after(half_cot, sent)
+    def down_part(far, values, kind):
+        def body(first_ref, second_ref, x_ref, out_ref):
+            for p, grads_ref in enumerate((first_ref, second_ref)):
+                out_ref[p * part : (p + 1) * part, :] = (
+                    ADAPTER_SCALE * dot(grads_ref[...], x_ref[...], ((1,), (0,)))
+                ).astype(kind)
+
+        tile = block // 2
+        return pl.pallas_call(
+            body,
+            grid=(2,),
+            out_shape=shape(2 * part, block, kind=kind),
+            in_specs=[
+                pl.BlockSpec((part, half_rows), lambda c: (far, 0)),
+                pl.BlockSpec((part, half_rows), lambda c: (2 + far, 0)),
+                pl.BlockSpec((half_rows, tile), lambda c: (0, c)),
+            ],
+            out_specs=pl.BlockSpec((2 * part, tile), lambda c: (0, c)),
+            compiler_params=params,
+            cost_estimate=cost(4 * part * half_rows * block, 2 * half_rows * block),
+        )(by_column, by_column, values)
+
+    packed = LANES // rank
+
+    def low_body(where_ref, first_ref, second_ref, id_ref, m0, m1, m2, m3, out_ref):
+        short = lines // packed
+        low = jnp.zeros((short, LANES), F32)
+        for s, m_ref in enumerate((m0, m1, m2, m3)):
+            product = dot(first_ref[...], m_ref[:, :block], ((1,), (1,))) + dot(
+                second_ref[...], m_ref[:, block:], ((1,), (1,))
+            )
+            match = id_ref[:, :1] == column_ids(s * part, where_ref, 1, (1, part))
+            chosen = jnp.where(match, product, 0.0).astype(BF16)
+            for t in range(packed):
+                fold = (
+                    lax.broadcasted_iota(jnp.int32, (part, LANES), 0) % rank + t * rank
+                    == lax.broadcasted_iota(jnp.int32, (part, LANES), 1)
+                ).astype(BF16)
+                low = low + dot(chosen[t * short : (t + 1) * short, :], fold, ((1,), (0,)))
+        out_ref[...] = low
+
+    def add_body(first_ref, second_ref, kept_first_ref, kept_second_ref, out_ref):
+        for q, (arrived_ref, kept_ref) in enumerate(
+            ((first_ref, kept_first_ref), (second_ref, kept_second_ref))
+        ):
+            for p in range(2):
+                total = kept_ref[p * part : (p + 1) * part, :]
+                total = total + arrived_ref[p * part : (p + 1) * part, :].astype(F32)
+                out_ref[:, p * piece : (p + 1) * piece, q * block : (q + 1) * block] = (
+                    total.astype(BF16).reshape(half, piece, block)
+                )
+
+    def unpack_rows(in_ref, out_ref):
+        for j in range(half):
+            for q in range(2):
+                at = (q * half + j) * block
+                out_ref[:, at : at + block] = in_ref[j, :, q * block : (q + 1) * block]
+
+    def unpack_down(where_ref, in_ref, out_ref):
+        for p in range(2):
+            which = where_ref[1] if p == 0 else 1 - where_ref[1]
+            target = pl.ds(pl.multiple_of(which * piece, piece), piece)
+            for j in range(half):
+                for q in range(2):
+                    at = (q * half + j) * block
+                    out_ref[target, at : at + block] = in_ref[
+                        j, p * piece : (p + 1) * piece, q * block : (q + 1) * block
+                    ]
+
+
+    frozen_piece = lax.dynamic_slice_in_dim(frozen, group * (block // 2), block // 2, axis=0)
+    down_piece = lax.dynamic_slice_in_dim(down.reshape(own, width), group * piece, piece, axis=0)
+    up_near = up.reshape(own, out_width)
+
+    up_far = swapped(up_near)
+
+    frozen_near = swapped(after(frozen_piece, up_far))
+
+    cot_at = pair
+    up_at = cot_at + 2 * out_width
+    id_at = up_at + 2 * out_width
+    wide = id_at + LANES
+
+    def pack_small(down_ref, cot_ref, near_ref, far_ref, id_ref, out_ref):
+        for j in range(half):
+            c = j % 2
+            for q in range(2):
+                out_ref[j, :, q * block : (q + 1) * block] = down_ref[
+                    :, (q * half + j) * block : (q * half + j + 1) * block
+                ]
+                out_ref[j, :, cot_at + q * out_width : cot_at + (q + 1) * out_width] = cot_ref[
+                    (2 * c + q) * piece : (2 * c + q + 1) * piece, :
+                ]
+            for q, up_ref in enumerate((near_ref, far_ref)):
+                out_ref[j, :, up_at + q * out_width : up_at + (q + 1) * out_width] = up_ref[
+                    c * piece : (c + 1) * piece, :
+                ]
+            out_ref[j, :, id_at:] = id_ref[...]
+
+    id_line = jnp.broadcast_to(ids.astype(BF16)[None, :], (piece, LANES))
+    small = pl.pallas_call(
+        pack_small,
+        out_shape=shape(half, piece, wide),
+        compiler_params=params,
+        cost_estimate=cost(0, 4 * half * piece * wide),
+    )(down_piece, cot, up_near, up_far, id_line)
+    small = exchange(small)
+    down_near = small[:, :, :pair].reshape(half * piece, pair)
+
+    def pack_rows(x_ref, first_ref, second_ref):
+        for j in range(half):
+            for q, out_ref in enumerate((first_ref, second_ref)):
+                out_ref[j, :, :] = x_ref[:, (q * half + j) * block : (q * half + j + 1) * block]
+
+    x_parts = pl.pallas_call(
+        pack_rows,
+        out_shape=(shape(half, rows, block),) * 2,
+        compiler_params=params,
+        cost_estimate=cost(0, 4 * rows * width),
+    )(x)
+
+    small, frozen_near, x_parts = lax.optimization_barrier((small, frozen_near, x_parts))
+    down_near = down_near if False else small[:, :, :pair].reshape(half * piece, pair)
+
+    shared = small[:, :, pair:id_at].reshape(half * piece, 4 * out_width)
+    half_ids = small[:, 0, id_at:].reshape(half_rows).astype(F32)
+    id_rows = jnp.broadcast_to(half_ids[:, None], (half_rows, LANES))
+    id_lines = jnp.broadcast_to(half_ids[None, :], (8, half_rows))
+
+    shared_twin = flipped(shared, 1)
+
+    down_far = swapped(down_near)
+
+    near_cross = other_group(down_near)
+
+    frozen_cross = other_group(frozen_near)
+
+    first_piece = jnp.where(group == 0, frozen_near, frozen_cross)
+    last_piece = jnp.where(group == 0, frozen_cross, frozen_near)
+    frozen_far = jnp.concatenate([first_piece, last_piece], axis=0)
+    frozen_low = jnp.where(my_half == 0, frozen, frozen_far)
+    frozen_high = jnp.where(my_half == 0, frozen_far, frozen)
+
+    x_first = exchange(after(x_parts[0], small, shared_twin)).reshape(half_rows, block)
+
+    x_second = exchange(after(x_parts[1], x_first)).reshape(half_rows, block)
+
+    by_row, by_column, half_cot = pl.pallas_call(
+        grads_body,
+        out_shape=(
+            shape(half_rows, columns),
+            shape(columns, half_rows),
+            shape(half_rows, out_width),
+        ),
+        in_specs=[smem] + [vmem] * 4,
+        out_specs=(vmem, vmem, vmem),
+        scratch_shapes=[pltpu.VMEM((columns, out_width), BF16)],
+        compiler_params=params,
+        cost_estimate=cost(4 * half_rows * columns * out_width, 8 * half_rows * columns),
+    )(where, shared, shared_twin, id_rows, id_lines)
+
+
+    far_cross = other_group(after(down_far, half_cot, frozen_low, frozen_high))
+
+    maps = (down_near, down_far, near_cross, far_cross)
     result = pl.pallas_call(
         rows_body,
         grid=(half_rows // lines,),
@@ -401,28 +689,19 @@
         + [pl.BlockSpec((part, pair), lambda i: (0, 0))] * 4,
         out_specs=pl.BlockSpec((lines // rows, rows, pair), lambda i: (i, 0, 0)),
         compiler_params=params,
-        cost_estimate=cost(2 * half_rows * pair * (out_width + columns), 8 * half_rows * pair),
-    )(cot_later, by_row, frozen_low, frozen_high, *maps)
+        cost_estimate=cost(50000000000, 0),
+    )(half_cot, by_row, frozen_low, frozen_high, *maps)
+
 
     back = exchange(result)
-    kept = down_part(0, after(x_block, result), F32)
-
-    packed = LANES // rank
-
-    def low_body(where_ref, x_ref, id_ref, m0, m1, m2, m3, out_ref):
-        short = lines // packed
-        low = jnp.zeros((short, LANES), F32)
-        for s, m_ref in enumerate((m0, m1, m2, m3)):
-            product = dot(x_ref[...], m_ref[...], ((1,), (1,)))
-            match = id_ref[:, :1] == column_ids(s * part, where_ref, 1, (1, part))
-            chosen = jnp.where(match, product, 0.0).astype(BF16)
-            for t in range(packed):
-                fold = (
-                    lax.broadcasted_iota(jnp.int32, (part, LANES), 0) % rank + t * rank
-                    == lax.broadcasted_iota(jnp.int32, (part, LANES), 1)
-                ).astype(BF16)
-                low = low + dot(chosen[t * short : (t + 1) * short, :], fold, ((1,), (0,)))
-        out_ref[...] = low
+
+    sent_first = down_part(1, x_first, BF16)
+
+    arrived_first = swapped(sent_first)
+
+    sent_second = down_part(1, after(x_second, result, arrived_first), BF16)
+
+    arrived_second = swapped(sent_second)
 
     low = pl.pallas_call(
         low_body,
@@ -430,72 +709,54 @@
         out_shape=shape(half_rows // packed, LANES, kind=F32),
         in_specs=[
             smem,
-            pl.BlockSpec((lines, pair), lambda i: (i, 0)),
+            pl.BlockSpec((lines, block), lambda i: (i, 0)),
+            pl.BlockSpec((lines, block), lambda i: (i, 0)),
             pl.BlockSpec((lines, LANES), lambda i: (i, 0)),
         ]
         + [pl.BlockSpec((part, pair), lambda i: (0, 0))] * 4,
         out_specs=pl.BlockSpec((lines // packed, LANES), lambda i: (i, 0)),
         compiler_params=params,
         cost_estimate=cost(2 * half_rows * pair * columns, 2 * half_rows * pair),
-    )(where, after(x_block, kept), id_rows, *maps)
-    bit = 1
-    while bit < half:
-        low = low + flipped(low, bit)
-        bit *= 2
-    low = low.astype(BF16).reshape(half_rows // lines, lines // packed, packed, rank)
-    low = low.transpose(0, 2, 1, 3).reshape(half_rows, rank)
+    )(where, x_first, after(x_second, sent_second), id_rows, *maps)
+
+    kept_first = down_part(0, after(x_first, low), F32)
+    kept_second = down_part(0, after(x_second, low), F32)
+
+    low_sum = low
+    for bit in (2, 1, 4):
+        low_sum = low_sum + flipped(low_sum, bit)
+
+    joined = lax.optimization_barrier((arrived_first, arrived_second, kept_first, kept_second, low_sum))
+    sums = pl.pallas_call(
+        add_body,
+        out_shape=shape(half, own, pair),
+        compiler_params=params,
+        cost_estimate=cost(45000000000, 0),
+    )(*joined[:4])
+
+    home = exchange(after(sums, back))
+
+    gradient = pl.pallas_call(
+        unpack_rows,
+        out_shape=shape(rows, width),
+        compiler_params=params,
+        cost_estimate=cost(0, 4 * rows * width),
+    )(back)
+
+
+    low_all = after(low_sum, sums, gradient)
+    low_all = low_all.astype(BF16).reshape(half_rows // lines, lines // packed, packed, rank)
+    low_all = low_all.transpose(0, 2, 1, 3).reshape(half_rows, rank)
     near = jnp.arange(held, dtype=jnp.int32) + here % half * held
     both = jnp.concatenate([near + my_half * half * held, near + (1 - my_half) * half * held])
     spread = jnp.where(
         half_ids[:, None] == jnp.repeat(both, rank)[None, :].astype(F32),
-        jnp.tile(low, (1, 2 * held)),
+        jnp.tile(low_all, (1, 2 * held)),
         jnp.zeros((), BF16),
     )
     up_part = (ADAPTER_SCALE * dot(spread, half_cot, ((0,), (0,)))).reshape(2, own, out_width)
 
-
-    arrived, up_part, kept = lax.optimization_barrier((arrived, up_part, kept))
-
-    def add_body(kept_ref, arrived_ref, out_ref):
-        for p in range(2):
-            total = kept_ref[p * part : (p + 1) * part, :]
-            total = total + arrived_ref[p * part : (p + 1) * part, :].astype(F32)
-            out_ref[:, p * piece : (p + 1) * piece, :] = total.astype(BF16).reshape(
-                half, piece, pair
-            )
-
-    sums = pl.pallas_call(
-        add_body,
-        out_shape=shape(half, own, pair),
-        compiler_params=params,
-        cost_estimate=cost(45000000000, 8 * half * own * pair),
-    )(kept, arrived)
-    home = exchange(after(sums, back))
-    up_grad = (up_part[0] + swapped(after(up_part[1], sums))).astype(BF16)
-
-    def unpack_rows(in_ref, out_ref):
-        for j in range(half):
-            for q in range(2):
-                at = (q * half + j) * block
-                out_ref[:, at : at + block] = in_ref[j, :, q * block : (q + 1) * block]
-
-    gradient = pl.pallas_call(
-        unpack_rows,
-        out_shape=shape(rows, width),
-        compiler_params=params,
-        cost_estimate=cost(0, 4 * rows * width),
-    )(back)
-
-    def unpack_down(where_ref, in_ref, out_ref):
-        for p in range(2):
-            which = where_ref[1] if p == 0 else 1 - where_ref[1]
-            target = pl.ds(pl.multiple_of(which * piece, piece), piece)
-            for j in range(half):
-                for q in range(2):
-                    at = (q * half + j) * block
-                    out_ref[target, at : at + block] = in_ref[
-                        j, p * piece : (p + 1) * piece, q * block : (q + 1) * block
-                    ]
+    up_grad = (up_part[0] + swapped(up_part[1])).astype(BF16)
 
     down_grad = pl.pallas_call(
         unpack_down,
@@ -514,6 +775,7 @@
     fits = (
         lax.axis_size("groups") == 2
         and x.shape[1] // n % (2 * LANES) == 0
+        and n == 16
         and down.shape[0] == 2
         and x.shape[0] == 2 * own == LANES
         and cot.shape[1] % LANES == 0

time: 258 us -> 228 us (0.88)
  waiting for transfers between devices: 144 us -> 112 us
  starting transfers between devices: 39 us -> 43.7 us
  Pallas kernels: 48.2 us -> 45.2 us
    ppermute x5 -> x6, waiting for transfers between devices: 78 us -> 59.2 us  [swapped(): return lax.ppermute(part, 'adapt', [(i, (i + half) % n) for i in range(n)])]
    ppermute x5 -> x4, waiting for transfers between devices: 45.1 us -> 29.2 us  [flipped(): return lax.ppermute(part, 'adapt', [(i, i ^ bit) for i in range(n)])]
    all_to_all x4 -> x5, starting transfers between devices: 19.6 us -> 29.3 us  [exchange(): lax.all_to_all(parts, 'adapt', split_axis=0, concat_axis=0, tiled=True, a...]
    ppermute x3, waiting for transfers between devices: 4.98 us -> 13.4 us  [other_group(): return lax.ppermute(part, 'groups', [(0, 1), (1, 0)])]
    all_to_all x4 -> x5, waiting for transfers between devices: 16.5 us -> 9.92 us  [exchange(): lax.all_to_all(parts, 'adapt', split_axis=0, concat_axis=0, tiled=True, a...]
    ppermute x5 -> x6, starting transfers between devices: 13.9 us -> 10 us  [swapped(): return lax.ppermute(part, 'adapt', [(i, (i + half) % n) for i in range(n)])]
    pallas_call x3 -> x5, Pallas kernels: 13.5 us -> 11.5 us  [the longest x4 9.4 us: down_part(): pl.pallas_call(body, grid=(2,), out_shape=shape(2 * part, block, kind=kin...]
    unnamed x40 -> x48, local copies, waits for them, and re-layouts: 11.8 us -> 12.7 us
  transfers between devices with their start and end apart: 17 -> 18, of which waited for: 8 -> 12; matrix products, arithmetic and copies ran while one was open for 5% -> 5% of each run, Pallas kernels for 18% -> 19%
where the time goes in v3:
time: 228 us; the launch traced here: 225 us
  waiting for transfers between devices  112 us (49%)
  Pallas kernels  45.2 us (20%)
  starting transfers between devices  43.7 us (19%)
  local copies, waits for them, and re-layouts  17.8 us (8%)
  other arithmetic  4.11 us (2%)
    ppermute x6, waiting for transfers between devices, swapped(): return lax.ppermute(part, 'adapt', [(i, (i + half) % n) for i in range(n)])  59.2 us
    all_to_all x5, starting transfers between devices, exchange(): lax.all_to_all(parts, 'adapt', split_axis=0, concat_axis=0, tiled=True, a...  29.3 us
    ppermute x4, waiting for transfers between devices, flipped(): return lax.ppermute(part, 'adapt', [(i, i ^ bit) for i in range(n)])  29.2 us
    ppermute x3, waiting for transfers between devices, other_group(): return lax.ppermute(part, 'groups', [(0, 1), (1, 0)])  13.4 us
    unnamed x48, local copies, waits for them, and re-layouts  12.7 us
    pallas_call x1, Pallas kernels, with_kernels(): pl.pallas_call(low_body, grid=(half_rows // lines,), out_shape=shape(half...  11.4 us
    ppermute x6, starting transfers between devices, swapped(): return lax.ppermute(part, 'adapt', [(i, (i + half) % n) for i in range(n)])  10 us
    all_to_all x5, waiting for transfers between devices, exchange(): lax.all_to_all(parts, 'adapt', split_axis=0, concat_axis=0, tiled=True, a...  9.92 us
  transfers between devices with their start and end apart: 18, of which 12 were waited for; matrix products, arithmetic and copies ran while one was open for 5% of the time, Pallas kernels for 19%

profile of v3, /device:TPU:8, one launch (start us, length us, event | category | flops | bytes accessed | tf_op | source)
XLA Modules:
  0.0 225.3 jit_solution(16620108632126934909)
XLA Ops:
  0.7 2.7 %collective-permute-start = (bf16[64,512]{1,0:T(8,128)(2,1)}, bf16[64,512]{1,0:T(8,128)(2,1)S(1)}, u32[]{:S(2)}, u32[]{:S(2)}) collective-permute-start(bf16[64,512]{1,0:T(8,128)(2,1)} %bitcast.25), channel_id=1, source_target_pairs={{0,8},{1,9},{2,10},{3,11},{4,12},{5,13},{6,14},{7,15},{8,0},{9,1},... | collective-permute-start | bytes 196616 | tf_op jit(solution)/shard_map/ppermute | solution.py:352
  3.4 2.9 %collective-permute-done.far_ref = bf16[64,512]{1,0:T(8,128)(2,1)S(1)} collective-permute-done((bf16[64,512]{1,0:T(8,128)(2,1)}, bf16[64,512]{1,0:T(8,128)(2,1)S(1)}, u32[]{:S(2)}, u32[]{:S(2)}) %collective-permute-start) | collective-permute-done | bytes 65568 | tf_op jit(solution)/shard_map/ppermute | solution.py:352
  7.7 4.9 %all-to-all-start = ((bf16[8,32,3712]{2,1,0:T(8,128)(2,1)}), bf16[8,32,3712]{2,1,0:T(8,128)(2,1)S(1)}, u32[]{:S(2)}, u32[]{:S(2)}) async-start(bf16[8,32,3712]{2,1,0:T(8,128)(2,1)} %shard_map.85), calls=%async_computation | async-start | bytes 3801088 | tf_op jit(solution)/shard_map/all_to_all | solution.py:347
  13.6 2.7 %collective-permute-start.1 = (bf16[384,512]{1,0:T(8,128)(2,1)S(1)}, bf16[384,512]{1,0:T(8,128)(2,1)}, u32[]{:S(2)}, u32[]{:S(2)}) collective-permute-start(bf16[384,512]{1,0:T(8,128)(2,1)S(1)} %constant_dynamic-slice_fusion), channel_id=1, source_target_pairs={{0,8},{1,9},{2,10},{3,11},{4,12},{5,13},{6,14},{7,15},{8,0},{9,1},... | collective-permute-start | bytes 1179656 | tf_op jit(solution)/shard_map/ppermute | solution.py:352
  16.3 2.1 shard_map.86
  20.7 24.6 %collective-permute-done.1 = bf16[384,512]{1,0:T(8,128)(2,1)} collective-permute-done((bf16[384,512]{1,0:T(8,128)(2,1)S(1)}, bf16[384,512]{1,0:T(8,128)(2,1)}, u32[]{:S(2)}, u32[]{:S(2)}) %collective-permute-start.1) | collective-permute-done | bytes 393248 | tf_op jit(solution)/shard_map/ppermute | solution.py:352
  49.2 4.2 %all-to-all-start.2 = ((bf16[8,128,768]{2,1,0:T(8,128)(2,1)}), bf16[8,128,768]{2,1,0:T(8,128)(2,1)S(1)}, u32[]{:S(2)}, u32[]{:S(2)}) async-start(bf16[8,128,768]{2,1,0:T(8,128)(2,1)} %copy-done.6), calls=%async_computation.2 | async-start | bytes 3145728 | tf_op jit(solution)/shard_map/all_to_all | solution.py:347
  54.9 2.2 slice.20
  58.8 6.7 %collective-permute-done.3 = bf16[384,512]{1,0:T(8,128)(2,1)S(1)} collective-permute-done((bf16[384,512]{1,0:T(8,128)(2,1)}, bf16[384,512]{1,0:T(8,128)(2,1)S(1)}, u32[]{:S(2)}, u32[]{:S(2)}) %collective-permute-start.3) | collective-permute-done | bytes 393248 | tf_op jit(solution)/shard_map/ppermute | solution.py:358
  68.8 4.8 %shard_map.87 = (bf16[1024,1024]{1,0:T(8,128)(2,1)S(1)}, bf16[1024,1024]{1,0:T(8,128)(2,1)}, bf16[1024,512]{1,0:T(8,128)(2,1)S(1)}) custom-call(s32[3]{0:T(128)S(1)} %pad_add_fusion.where_ref, bf16[256,2048]{1,0:T(8,128)(2,1)S(1)} %bitcast.24, bf16[256,2048]{1,0:T(8,128)(2,1)S(1)} %copy-done.19, f32[1024,128]{1,0:T(8,128)S(1)} %broadcast_in_dim.12.id_ref, ...), custom_call_target="tpu_custom_call" | custom-call | flops 2147483648 | bytes 8388608 | tf_op jit(solution)/shard_map/pallas_call | solution.py:662
  75.9 15.7 %collective-permute-done.4.m1 = bf16[256,1536]{1,0:T(8,128)(2,1)} collective-permute-done((bf16[256,1536]{1,0:T(8,128)(2,1)}, bf16[256,1536]{1,0:T(8,128)(2,1)}, u32[]{:S(2)}, u32[]{:S(2)}) %collective-permute-start.4) | collective-permute-done | bytes 786464 | tf_op jit(solution)/shard_map/ppermute | solution.py:352
  92.1 7.5 %all-to-all-start.3 = ((bf16[8,128,768]{2,1,0:T(8,128)(2,1)}), bf16[8,128,768]{2,1,0:T(8,128)(2,1)}, u32[]{:S(2)}, u32[]{:S(2)}) async-start(bf16[8,128,768]{2,1,0:T(8,128)(2,1)} %copy-done.5), calls=%async_computation.3 | async-start | bytes 3145728 | tf_op jit(solution)/shard_map/all_to_all | solution.py:347
  101.2 2.3 %shard_map.90 = bf16[512,768]{1,0:T(8,128)(2,1)} custom-call(bf16[1024,1024]{1,0:T(8,128)(2,1)S(1)} %copy-done.1, bf16[1024,1024]{1,0:T(8,128)(2,1)S(1)} %copy-done.1, bf16[1024,768]{1,0:T(8,128)(2,1)S(1)} %bitcast.20), custom_call_target="tpu_custom_call" | custom-call | flops 805306368 | bytes 1572864 | tf_op jit(solution)/shard_map/pallas_call | solution.py:523
  103.7 6.7 %collective-permute-done.6.m3 = bf16[256,1536]{1,0:T(8,128)(2,1)} collective-permute-done((bf16[256,1536]{1,0:T(8,128)(2,1)}, bf16[256,1536]{1,0:T(8,128)(2,1)}, u32[]{:S(2)}, u32[]{:S(2)}) %collective-permute-start.6) | collective-permute-done | bytes 786464 | tf_op jit(solution)/shard_map/ppermute | solution.py:358
  110.4 8.5 %shard_map.88 = bf16[8,128,1536]{2,1,0:T(8,128)(2,1)} custom-call(bf16[1024,512]{1,0:T(8,128)(2,1)S(1)} %copy-done.9, bf16[1024,1024]{1,0:T(8,128)(2,1)} %copy-done.20, bf16[768,512]{1,0:T(8,128)(2,1)S(1)} %copy-done.13, bf16[768,512]{1,0:T(8,128)(2,1)S(1)} %copy-done.12, bf16[256,1536]{1,0:T(8,128)(2,1)} %bitcast.7.m0, ...), custom_call_target="tpu_custom_call" | custom-call | flops 49999998976 | tf_op jit(solution)/shard_map/pallas_call | solution.py:680
  118.9 9.9 %all-to-all-done.3 = bf16[8,128,768]{2,1,0:T(8,128)(2,1)} async-done(((bf16[8,128,768]{2,1,0:T(8,128)(2,1)}), bf16[8,128,768]{2,1,0:T(8,128)(2,1)}, u32[]{:S(2)}, u32[]{:S(2)}) %all-to-all-start.3) | async-done | bytes 1572896 | tf_op jit(solution)/shard_map/all_to_all | solution.py:347
  128.9 6.8 %all-to-all-start.1 = ((bf16[8,128,1536]{2,1,0:T(8,128)(2,1)}), bf16[8,128,1536]{2,1,0:T(8,128)(2,1)}, u32[]{:S(2)}, u32[]{:S(2)}) async-start(bf16[8,128,1536]{2,1,0:T(8,128)(2,1)} %shard_map.88), calls=%async_computation.1 | async-start | bytes 6291456 | tf_op jit(solution)/shard_map/all_to_all | solution.py:347
  135.7 2.5 %collective-permute-done.7.first_ref = bf16[512,768]{1,0:T(8,128)(2,1)} collective-permute-done((bf16[512,768]{1,0:T(8,128)(2,1)}, bf16[512,768]{1,0:T(8,128)(2,1)}, u32[]{:S(2)}, u32[]{:S(2)}) %collective-permute-start.7) | collective-permute-done | bytes 786464 | tf_op jit(solution)/shard_map/ppermute | solution.py:352
  138.2 1.6 copy-done.2
  139.8 2.7 %shard_map.91 = bf16[512,768]{1,0:T(8,128)(2,1)S(1)} custom-call(bf16[1024,1024]{1,0:T(8,128)(2,1)S(1)} %copy-done.2, bf16[1024,1024]{1,0:T(8,128)(2,1)S(1)} %copy-done.2, bf16[1024,768]{1,0:T(8,128)(2,1)} %bitcast.9.x_ref.second_ref), custom_call_target="tpu_custom_call" | custom-call | flops 805306368 | bytes 1572864 | tf_op jit(solution)/shard_map/pallas_call | solution.py:523
  142.5 3.5 %collective-permute-start.8 = (bf16[512,768]{1,0:T(8,128)(2,1)S(1)}, bf16[512,768]{1,0:T(8,128)(2,1)S(1)}, u32[]{:S(2)}, u32[]{:S(2)}) collective-permute-start(bf16[512,768]{1,0:T(8,128)(2,1)S(1)} %shard_map.91), channel_id=1, source_target_pairs={{0,8},{1,9},{2,10},{3,11},{4,12},{5,13},{6,14},{7,15},{8,0},{9,1},... | collective-permute-start | bytes 2359304 | tf_op jit(solution)/shard_map/ppermute | solution.py:352
  146.0 11.4 %shard_map.92 = f32[256,128]{1,0:T(8,128)S(1)} custom-call(s32[3]{0:T(128)S(1)} %pad_add_fusion.where_ref, bf16[1024,768]{1,0:T(8,128)(2,1)S(1)} %bitcast.21, bf16[1024,768]{1,0:T(8,128)(2,1)} %bitcast.9.x_ref.second_ref, f32[1024,128]{1,0:T(8,128)S(1)} %copy-done.15, bf16[256,1536]{1,0:T(8,128)(2,1)} %bitcast.7.m0, ...), custom_call_target="tpu_custom_call" | custom-call | flops 3221225472 | bytes 3145728 | tf_op jit(solution)/shard_map/pallas_call | solution.py:706
  159.0 15.9 %collective-permute-done.9 = f32[256,128]{1,0:T(8,128)S(1)} collective-permute-done((f32[256,128]{1,0:T(8,128)S(1)}, f32[256,128]{1,0:T(8,128)S(1)}, u32[]{:S(2)}, u32[]{:S(2)}) %collective-permute-start.9) | collective-permute-done | bytes 131104 | tf_op jit(solution)/shard_map/ppermute | solution.py:355
  176.4 2.7 %shard_map.94.kept_second_ref = f32[512,768]{1,0:T(8,128)S(1)} custom-call(bf16[1024,1024]{1,0:T(8,128)(2,1)S(1)} %copy-done.3, bf16[1024,1024]{1,0:T(8,128)(2,1)S(1)} %copy-done.3, bf16[1024,768]{1,0:T(8,128)(2,1)} %bitcast.9.x_ref.second_ref), custom_call_target="tpu_custom_call" | custom-call | flops 805306368 | bytes 1572864 | tf_op jit(solution)/shard_map/pallas_call | solution.py:523
  180.2 1.7 shard_map.93.kept_first_ref
  181.9 10.5 %collective-permute-done.11 = f32[256,128]{1,0:T(8,128)S(1)} collective-permute-done((f32[256,128]{1,0:T(8,128)S(1)}, f32[256,128]{1,0:T(8,128)S(1)}, u32[]{:S(2)}, u32[]{:S(2)}) %collective-permute-start.11) | collective-permute-done | bytes 131104 | tf_op jit(solution)/shard_map/ppermute | solution.py:355
  192.4 1.9 shard_map.95
  195.5 6.0 %all-to-all-start.4 = ((bf16[8,64,1536]{2,1,0:T(8,128)(2,1)}), bf16[8,64,1536]{2,1,0:T(8,128)(2,1)S(1)}, u32[]{:S(2)}, u32[]{:S(2)}) async-start(bf16[8,64,1536]{2,1,0:T(8,128)(2,1)} %copy-done.7), calls=%async_computation.4 | async-start | bytes 3145728 | tf_op jit(solution)/shard_map/all_to_all | solution.py:347
  201.8 3.8 %shard_map.89 = bf16[128,12288]{1,0:T(8,128)(2,1)} custom-call(bf16[8,128,1536]{2,1,0:T(8,128)(2,1)} %all-to-all-done.1.in_ref), custom_call_target="tpu_custom_call" | custom-call | bytes 6291456 | tf_op jit(solution)/shard_map/pallas_call | solution.py:739
  206.9 1.9 convolution_multiply_fusion
  209.3 13.5 %collective-permute-done.12 = f32[64,512]{1,0:T(8,128)S(1)} collective-permute-done((f32[64,512]{1,0:T(8,128)S(1)}, f32[64,512]{1,0:T(8,128)S(1)}, u32[]{:S(2)}, u32[]{:S(2)}) %collective-permute-start.12) | collective-permute-done | bytes 131104 | tf_op jit(solution)/shard_map/ppermute | solution.py:352
  223.5 1.8 shard_map.96
  (93 shorter events, 27.8 us)
Async XLA Ops:
  0.6 2.7 %copy-start = (bf16[2,32,12288]{2,1,0:T(8,128)(2,1)S(1)}, bf16[2,32,12288]{2,1,0:T(8,128)(2,1)}, u32[]{:S(2)}) copy-start(bf16[2,32,12288]{2,1,0:T(8,128)(2,1)} %param.10) | copy-start | bytes 4718596
  0.6 5.6 %copy-start.17 = (bf16[2,32,512]{2,1,0:T(8,128)(2,1)S(1)}, bf16[2,32,512]{2,1,0:T(8,128)(2,1)}, u32[]{:S(2)}) copy-start(bf16[2,32,512]{2,1,0:T(8,128)(2,1)} %param.11) | copy-start | bytes 196612
  0.7 2.7 %copy-start.23 = (s32[128]{0:T(128)S(1)}, s32[128]{0:T(128)}, u32[]{:S(2)}) copy-start(s32[128]{0:T(128)} %param.8) | copy-start | bytes 1540
  0.7 5.6 %copy-start.16 = (bf16[128,512]{1,0:T(8,128)(2,1)S(1)}, bf16[128,512]{1,0:T(8,128)(2,1)}, u32[]{:S(2)}) copy-start(bf16[128,512]{1,0:T(8,128)(2,1)} %cot_ref.1) | copy-start | bytes 393220
  0.7 5.6 %collective-permute-start = (bf16[64,512]{1,0:T(8,128)(2,1)}, bf16[64,512]{1,0:T(8,128)(2,1)S(1)}, u32[]{:S(2)}, u32[]{:S(2)}) collective-permute-start(bf16[64,512]{1,0:T(8,128)(2,1)} %bitcast.25), channel_id=1, source_target_pairs={{0,8},{1,9},{2,10},{3,11},{4,12},{5,13},{6,14},{7,15},{8,0},{9,1},... | collective-permute-start | bytes 196616 | tf_op jit(solution)/shard_map/ppermute | solution.py:352
  7.7 37.6 %all-to-all-start = ((bf16[8,32,3712]{2,1,0:T(8,128)(2,1)}), bf16[8,32,3712]{2,1,0:T(8,128)(2,1)S(1)}, u32[]{:S(2)}, u32[]{:S(2)}) async-start(bf16[8,32,3712]{2,1,0:T(8,128)(2,1)} %shard_map.85), calls=%async_computation | async-start | bytes 3801088 | tf_op jit(solution)/shard_map/all_to_all | solution.py:347
  13.6 31.7 %collective-permute-start.1 = (bf16[384,512]{1,0:T(8,128)(2,1)S(1)}, bf16[384,512]{1,0:T(8,128)(2,1)}, u32[]{:S(2)}, u32[]{:S(2)}) collective-permute-start(bf16[384,512]{1,0:T(8,128)(2,1)S(1)} %constant_dynamic-slice_fusion), channel_id=1, source_target_pairs={{0,8},{1,9},{2,10},{3,11},{4,12},{5,13},{6,14},{7,15},{8,0},{9,1},... | collective-permute-start | bytes 1179656 | tf_op jit(solution)/shard_map/ppermute | solution.py:352
  45.3 3.8 %copy-start.21 = (bf16[8,32,3712]{2,1,0:T(8,128)(2,1)}, bf16[8,32,3712]{2,1,0:T(8,128)(2,1)S(1)}, u32[]{:S(2)}) copy-start(bf16[8,32,3712]{2,1,0:T(8,128)(2,1)S(1)} %all-to-all-done) | copy-start | bytes 5701636
  45.4 2.7 %collective-permute-start.2 = (bf16[256,2048]{1,0:T(8,128)(2,1)S(1)}, bf16[256,2048]{1,0:T(8,128)(2,1)S(1)}, u32[]{:S(2)}, u32[]{:S(2)}) collective-permute-start(bf16[256,2048]{1,0:T(8,128)(2,1)S(1)} %bitcast.23), channel_id=1, source_target_pairs={{0,1},{1,0},{2,3},{3,2},{4,5},{5,4},{6,7},{7,6},{8,9},{9,8},{10,11... | collective-permute-start | bytes 3145736 | tf_op jit(solution)/shard_map/ppermute | solution.py:355
  49.2 43.0 %all-to-all-start.2 = ((bf16[8,128,768]{2,1,0:T(8,128)(2,1)}), bf16[8,128,768]{2,1,0:T(8,128)(2,1)S(1)}, u32[]{:S(2)}, u32[]{:S(2)}) async-start(bf16[8,128,768]{2,1,0:T(8,128)(2,1)} %copy-done.6), calls=%async_computation.2 | async-start | bytes 3145728 | tf_op jit(solution)/shard_map/all_to_all | solution.py:347
  53.4 12.2 %collective-permute-start.3 = (bf16[384,512]{1,0:T(8,128)(2,1)}, bf16[384,512]{1,0:T(8,128)(2,1)S(1)}, u32[]{:S(2)}, u32[]{:S(2)}) collective-permute-start(bf16[384,512]{1,0:T(8,128)(2,1)} %collective-permute-done.1), channel_id=1, source_target_pairs={{0,16},{16,0},{1,17},{17,1},{2,18},{18,2},{3,19},{19,3},{4,20},{20... | collective-permute-start | bytes 1179656 | tf_op jit(solution)/shard_map/ppermute | solution.py:358
  54.9 11.7 %copy-start.22 = (bf16[768,512]{1,0:T(8,128)(2,1)S(1)}, bf16[768,512]{1,0:T(8,128)(2,1)}, u32[]{:S(2)}) copy-start(bf16[768,512]{1,0:T(8,128)(2,1)} %param.9) | copy-start | bytes 2359300
  57.1 34.5 %collective-permute-start.4 = (bf16[256,1536]{1,0:T(8,128)(2,1)}, bf16[256,1536]{1,0:T(8,128)(2,1)}, u32[]{:S(2)}, u32[]{:S(2)}) collective-permute-start(bf16[256,1536]{1,0:T(8,128)(2,1)} %bitcast.7.m0), channel_id=1, source_target_pairs={{0,8},{1,9},{2,10},{3,11},{4,12},{5,13},{6,14},{7,15},{8,0},{9,1},... | collective-permute-start | bytes 2359304 | tf_op jit(solution)/shard_map/ppermute | solution.py:352
  58.3 45.5 %collective-permute-start.5 = (bf16[256,1536]{1,0:T(8,128)(2,1)}, bf16[256,1536]{1,0:T(8,128)(2,1)}, u32[]{:S(2)}, u32[]{:S(2)}) collective-permute-start(bf16[256,1536]{1,0:T(8,128)(2,1)} %bitcast.7.m0), channel_id=1, source_target_pairs={{0,16},{16,0},{1,17},{17,1},{2,18},{18,2},{3,19},{19,3},{4,20},{20... | collective-permute-start | bytes 2359304 | tf_op jit(solution)/shard_map/ppermute | solution.py:358
  66.6 1.6 copy-start.11
  66.7 2.1 copy-start.19
  68.8 4.8 %copy-start.14 = (f32[1024,128]{1,0:T(8,128)}, f32[1024,128]{1,0:T(8,128)S(1)}, u32[]{:S(2)}) copy-start(f32[1024,128]{1,0:T(8,128)S(1)} %broadcast_in_dim.12.id_ref) | copy-start | bytes 1572868
  91.6 18.8 %collective-permute-start.6 = (bf16[256,1536]{1,0:T(8,128)(2,1)}, bf16[256,1536]{1,0:T(8,128)(2,1)}, u32[]{:S(2)}, u32[]{:S(2)}) collective-permute-start(bf16[256,1536]{1,0:T(8,128)(2,1)} %collective-permute-done.4.m1), channel_id=1, source_target_pairs={{0,16},{16,0},{1,17},{17,1},{2,18},{18,2},{3,19},{19,3},{4,20},{20... | collective-permute-start | bytes 2359304 | tf_op jit(solution)/shard_map/ppermute | solution.py:358
  92.1 36.7 %all-to-all-start.3 = ((bf16[8,128,768]{2,1,0:T(8,128)(2,1)}), bf16[8,128,768]{2,1,0:T(8,128)(2,1)}, u32[]{:S(2)}, u32[]{:S(2)}) async-start(bf16[8,128,768]{2,1,0:T(8,128)(2,1)} %copy-done.5), calls=%async_computation.3 | async-start | bytes 3145728 | tf_op jit(solution)/shard_map/all_to_all | solution.py:347
  101.2 9.2 %copy-start.9 = (bf16[1024,512]{1,0:T(8,128)(2,1)S(1)}, bf16[1024,512]{1,0:T(8,128)(2,1)}, u32[]{:S(2)}) copy-start(bf16[1024,512]{1,0:T(8,128)(2,1)} %copy-done.8) | copy-start | bytes 3145732
  101.2 9.2 %copy-start.12 = (bf16[768,512]{1,0:T(8,128)(2,1)S(1)}, bf16[768,512]{1,0:T(8,128)(2,1)}, u32[]{:S(2)}) copy-start(bf16[768,512]{1,0:T(8,128)(2,1)} %get-tuple-element.51.high_w) | copy-start | bytes 2359300
  101.2 9.2 %copy-start.13 = (bf16[768,512]{1,0:T(8,128)(2,1)S(1)}, bf16[768,512]{1,0:T(8,128)(2,1)}, u32[]{:S(2)}) copy-start(bf16[768,512]{1,0:T(8,128)(2,1)} %get-tuple-element.52.low_w) | copy-start | bytes 2359300
  103.6 34.7 %collective-permute-start.7 = (bf16[512,768]{1,0:T(8,128)(2,1)}, bf16[512,768]{1,0:T(8,128)(2,1)}, u32[]{:S(2)}, u32[]{:S(2)}) collective-permute-start(bf16[512,768]{1,0:T(8,128)(2,1)} %shard_map.90), channel_id=1, source_target_pairs={{0,8},{1,9},{2,10},{3,11},{4,12},{5,13},{6,14},{7,15},{8,0},{9,1},... | collective-permute-start | bytes 2359304 | tf_op jit(solution)/shard_map/ppermute | solution.py:352
  128.9 66.7 %all-to-all-start.1 = ((bf16[8,128,1536]{2,1,0:T(8,128)(2,1)}), bf16[8,128,1536]{2,1,0:T(8,128)(2,1)}, u32[]{:S(2)}, u32[]{:S(2)}) async-start(bf16[8,128,1536]{2,1,0:T(8,128)(2,1)} %shard_map.88), calls=%async_computation.1 | async-start | bytes 6291456 | tf_op jit(solution)/shard_map/all_to_all | solution.py:347
  139.8 6.2 %copy-start.15 = (f32[1024,128]{1,0:T(8,128)S(1)}, f32[1024,128]{1,0:T(8,128)}, u32[]{:S(2)}) copy-start(f32[1024,128]{1,0:T(8,128)} %copy-done.14) | copy-start | bytes 1572868
  142.5 49.9 %collective-permute-start.8 = (bf16[512,768]{1,0:T(8,128)(2,1)S(1)}, bf16[512,768]{1,0:T(8,128)(2,1)S(1)}, u32[]{:S(2)}, u32[]{:S(2)}) collective-permute-start(bf16[512,768]{1,0:T(8,128)(2,1)S(1)} %shard_map.91), channel_id=1, source_target_pairs={{0,8},{1,9},{2,10},{3,11},{4,12},{5,13},{6,14},{7,15},{8,0},{9,1},... | collective-permute-start | bytes 2359304 | tf_op jit(solution)/shard_map/ppermute | solution.py:352
  146.0 30.4 %copy-start.3 = (bf16[1024,1024]{1,0:T(8,128)(2,1)S(1)}, bf16[1024,1024]{1,0:T(8,128)(2,1)}, u32[]{:S(2)}) copy-start(bf16[1024,1024]{1,0:T(8,128)(2,1)} %get-tuple-element.35.first_ref.second_ref) | copy-start | bytes 6291460
  157.5 17.4 %collective-permute-start.9 = (f32[256,128]{1,0:T(8,128)S(1)}, f32[256,128]{1,0:T(8,128)S(1)}, u32[]{:S(2)}, u32[]{:S(2)}) collective-permute-start(f32[256,128]{1,0:T(8,128)S(1)} %shard_map.92), channel_id=1, source_target_pairs={{0,2},{1,3},{2,0},{3,1},{4,6},{5,7},{6,4},{7,5},{8,10},{9,11},{10,... | collective-permute-start | bytes 393224 | tf_op jit(solution)/shard_map/ppermute | solution.py:355
  174.9 1.4 collective-permute-start.10
  176.3 16.1 %collective-permute-start.11 = (f32[256,128]{1,0:T(8,128)S(1)}, f32[256,128]{1,0:T(8,128)S(1)}, u32[]{:S(2)}, u32[]{:S(2)}) collective-permute-start(f32[256,128]{1,0:T(8,128)S(1)} %add.50), channel_id=1, source_target_pairs={{0,4},{1,5},{2,6},{3,7},{4,0},{5,1},{6,2},{7,3},{8,12},{9,13},{10,... | collective-permute-start | bytes 393224 | tf_op jit(solution)/shard_map/ppermute | solution.py:355
  195.5 27.9 %all-to-all-start.4 = ((bf16[8,64,1536]{2,1,0:T(8,128)(2,1)}), bf16[8,64,1536]{2,1,0:T(8,128)(2,1)S(1)}, u32[]{:S(2)}, u32[]{:S(2)}) async-start(bf16[8,64,1536]{2,1,0:T(8,128)(2,1)} %copy-done.7), calls=%async_computation.4 | async-start | bytes 3145728 | tf_op jit(solution)/shard_map/all_to_all | solution.py:347
  208.8 14.0 %collective-permute-start.12 = (f32[64,512]{1,0:T(8,128)S(1)}, f32[64,512]{1,0:T(8,128)S(1)}, u32[]{:S(2)}, u32[]{:S(2)}) collective-permute-start(f32[64,512]{1,0:T(8,128)S(1)} %slice.24), channel_id=1, source_target_pairs={{0,8},{1,9},{2,10},{3,11},{4,12},{5,13},{6,14},{7,15},{8,0},{9,1},... | collective-permute-start | bytes 393224 | tf_op jit(solution)/shard_map/ppermute | solution.py:352
  (10 other events, 12.3 us)

commit v4 on v3

--- a/solution.py
+++ b/solution.py
@@ -266,238 +266,6 @@
             match = column_ids(at, where_ref, 0, (step, 1)) == line_ref[:1, :]
             by_column_ref[at : at + step, :] = jnp.where(match, product, 0.0).astype(BF16)
 
-    low_frozen = jnp.where(my_half == 0, frozen, frozen_far)
-    high_frozen = jnp.where(my_half == 0, frozen_far, frozen)
-    base = dot(half_cot, jnp.concatenate([low_frozen, high_frozen], axis=0), ((1,), (1,)))
-    lora = dot(grads_near, down_near_all, ((0,), (0,))) + dot(
-        grads_far, down_far_all, ((0,), (0,))
-    )
-    gradient = (base + ADAPTER_SCALE * lora).astype(BF16).reshape(half, rows, 2 * block)
-
-    x_block = jnp.concatenate([x_first, x_second], axis=1)
-    fold = (
-        jnp.arange(half * own, dtype=jnp.int32)[:, None] % rank
-        == jnp.arange(LANES, dtype=jnp.int32)[None, :]
-    ).astype(BF16)
-
-    def low_part(maps, adapters):
-        picked = jnp.where(
-            half_ids[:, None] == adapters[None, :], dot(x_block, maps, ((1,), (1,))), 0.0
-        ).astype(BF16)
-        return dot(picked, fold, ((1,), (0,)))
-
-    low = (low_part(down_near_all, near_ids) + low_part(down_far_all, far_ids)).astype(BF16)
-    gradient = jnp.concatenate([gradient, low.reshape(half, rows, LANES)], axis=2)
-    gradient = exchange(after(gradient, second))
-    low = gradient[:, :, 2 * block : 2 * block + rank].astype(F32).sum(axis=0).astype(BF16)
-    gradient = gradient[:, :, : 2 * block].reshape(half, rows, 2, block)
-    gradient = gradient.transpose(1, 2, 0, 3).reshape(rows, width)
-
-    pack = LANES // rank
-    low_rows = low.reshape(pack, rows // pack, rank).transpose(1, 0, 2).reshape(rows // pack, LANES)
-    low_rows = jnp.pad(low_rows, ((0, own - rows // pack), (0, 0)))
-    sum_first = jnp.concatenate(
-        [
-            sum_first.reshape(half, own, block),
-            jnp.broadcast_to(low_rows[None], (half, own, LANES)),
-        ],
-        axis=2,
-    )
-    sum_first = exchange(sum_first)
-    sum_second = exchange(after(sum_second.reshape(half, own, block), sum_first))
-    low = sum_first[:, : rows // pack, block:].reshape(half, rows // pack, pack, rank)
-    low = low.transpose(0, 2, 1, 3).reshape(half * rows, rank)
-    down_grad = jnp.stack([sum_first[:, :, :block], sum_second], axis=0)
-    down_grad = down_grad.transpose(2, 0, 1, 3).reshape(held, rank, width)
-
-    pair = jnp.arange(held, dtype=jnp.int32) + here % half * held
-    pair = jnp.concatenate([pair + my_half * half * held, pair + (1 - my_half) * half * held])
-    spread = jnp.where(
-        half_ids[:, None] == jnp.repeat(pair, rank)[None, :],
-        jnp.tile(low, (1, 2 * held)),
-        jnp.zeros((), BF16),
-    )
-    up_part = (ADAPTER_SCALE * dot(spread, half_cot, ((0,), (0,)))).reshape(2, own, out_width)
-    up_grad = (up_part[0] + swapped(up_part[1])).astype(BF16)
-    return gradient, down_grad, up_grad.reshape(held, rank, out_width)
-
-
-def shape(*dims, kind=BF16):
-    return jax.ShapeDtypeStruct(dims, kind)
-
-
-def with_kernels(x, cot, ids, frozen, down, up):
-    n = lax.axis_size("adapt")
-    half = n // 2
-    rows, width = x.shape
-    out_width = cot.shape[1]
-    held, rank, _ = down.shape
-    own = held * rank
-    piece = own // 2
-    block = width // n
-    pair = 2 * block
-    half_rows = half * rows
-    halves = [list(range(half)), list(range(half, n))]
-    here = lax.axis_index("adapt")
-    group = lax.axis_index("groups")
-    my_half = here // half
-    core = here % 2
-
-    def exchange(parts):
-        return lax.all_to_all(
-            parts, "adapt", split_axis=0, concat_axis=0, tiled=True, axis_index_groups=halves
-        )
-
-    def swapped(part):
-        return lax.ppermute(part, "adapt", [(i, (i + half) % n) for i in range(n)])
-
-    def flipped(part, bit):
-        return lax.ppermute(part, "adapt", [(i, i ^ bit) for i in range(n)])
-
-    def other_group(part):
-        return lax.ppermute(part, "groups", [(0, 1), (1, 0)])
-
-    smem = pl.BlockSpec(memory_space=pltpu.SMEM)
-    vmem = pl.BlockSpec(memory_space=pltpu.VMEM)
-    params = pltpu.CompilerParams(vmem_limit_bytes=VMEM_BYTES)
-
-    def cost(flops, moved):
-        return pl.CostEstimate(flops=flops, bytes_accessed=moved, transcendentals=0)
-
-    frozen_piece = lax.dynamic_slice_in_dim(frozen, group * (block // 2), block // 2, axis=0)
-    down_piece = lax.dynamic_slice_in_dim(down.reshape(own, width), group * piece, piece, axis=0)
-    cot_at = pair
-    up_at = cot_at + 2 * out_width
-    id_at = up_at + 2 * out_width
-    wide = id_at + LANES
-    up_near = up.reshape(own, out_width)
-    up_far = swapped(up_near)
-    frozen_near = swapped(after(frozen_piece, up_far))
-
-    def pack_small(down_ref, cot_ref, near_ref, far_ref, id_ref, out_ref):
-        for j in range(half):
-            c = j % 2
-            for q in range(2):
-                out_ref[j, :, q * block : (q + 1) * block] = down_ref[
-                    :, (q * half + j) * block : (q * half + j + 1) * block
-                ]
-                out_ref[j, :, cot_at + q * out_width : cot_at + (q + 1) * out_width] = cot_ref[
-                    (2 * c + q) * piece : (2 * c + q + 1) * piece, :
-                ]
-            for q, up_ref in enumerate((near_ref, far_ref)):
-                out_ref[j, :, up_at + q * out_width : up_at + (q + 1) * out_width] = up_ref[
-                    c * piece : (c + 1) * piece, :
-                ]
-            out_ref[j, :, id_at:] = id_ref[...]
-
-    id_line = jnp.broadcast_to(ids.astype(BF16)[None, :], (piece, LANES))
-    small = pl.pallas_call(
-        pack_small,
-        out_shape=shape(half, piece, wide),
-        compiler_params=params,
-        cost_estimate=cost(0, 4 * half * piece * wide),
-    )(down_piece, cot, up_near, up_far, id_line)
-    small = exchange(small)
-
-    def pack_rows(x_ref, out_ref):
-        for j in range(half):
-            for q in range(2):
-                out_ref[j, :, q * block : (q + 1) * block] = x_ref[
-                    :, (q * half + j) * block : (q * half + j + 1) * block
-                ]
-
-    x_parts = pl.pallas_call(
-        pack_rows,
-        out_shape=shape(half, rows, pair),
-        compiler_params=params,
-        cost_estimate=cost(0, 4 * rows * width),
-    )(x)
-
-    x_parts, small, frozen_near = lax.optimization_barrier((x_parts, small, frozen_near))
-    down_near = small[:, :, :pair].reshape(half * piece, pair)
-    shared = small[:, :, pair:id_at].reshape(half * piece, 4 * out_width)
-    shared_twin = flipped(shared, 1)
-    x_block = exchange(after(x_parts, shared_twin)).reshape(half_rows, pair)
-    down_far = swapped(down_near)
-    near_cross = other_group(down_near)
-    frozen_cross = other_group(frozen_near)
-    half_ids = small[:, 0, id_at:].reshape(half_rows).astype(F32)
-    id_rows = jnp.broadcast_to(half_ids[:, None], (half_rows, LANES))
-    id_lines = jnp.broadcast_to(half_ids[None, :], (8, half_rows))
-    first_piece = jnp.where(group == 0, frozen_near, frozen_cross)
-    last_piece = jnp.where(group == 0, frozen_cross, frozen_near)
-    frozen_far = jnp.concatenate([first_piece, last_piece], axis=0)
-    frozen_low = jnp.where(my_half == 0, frozen, frozen_far)
-    frozen_high = jnp.where(my_half == 0, frozen_far, frozen)
-
-    part = half * piece
-    columns = 4 * part
-
-    def column_ids(at, where, axis, dims):
-        column = lax.broadcasted_iota(jnp.int32, dims, axis) + at
-        crossed, rest = column // (2 * part), column % (2 * part)
-        far, rest = rest // part, rest % part
-        owner, within = rest // piece, rest % piece
-        side = jnp.where(far == 0, where[0], 1 - where[0])
-        which = jnp.where(crossed == 0, where[1], 1 - where[1])
-        return ((side * half + owner) * held + (which * piece + within) // rank).astype(F32)
-
-    where = jnp.stack([my_half, group, core])
-
-    def grads_body(
-        where_ref,
-        mine_ref,
-        twin_ref,
-        id_ref,
-        line_ref,
-        by_row_ref,
-        by_column_ref,
-        cot_ref,
-        up_scratch,
-    ):
-        c = where_ref[2]
-        for owner in range(half):
-            at = owner * piece
-            for q in range(2):
-                for ref, side in ((mine_ref, c), (twin_ref, 1 - c)):
-                    target = pl.multiple_of(owner * rows + (2 * side + q) * piece, piece)
-                    cot_ref[pl.ds(target, piece), :] = ref[
-                        at : at + piece, q * out_width : (q + 1) * out_width
-                    ]
-            for far in range(2):
-                lo, hi = (2 + far) * out_width, (3 + far) * out_width
-                for ref, side in ((mine_ref, c), (twin_ref, 1 - c)):
-                    crossed = jnp.where(side == where_ref[1], 0, 1)
-                    target = (crossed * 2 + far) * part + at
-                    up_scratch[pl.ds(pl.multiple_of(target, piece), piece), :] = ref[
-                        at : at + piece, lo:hi
-                    ]
-        step = 2 * part
-        for at in range(0, columns, step):
-            product = dot(cot_ref[...], up_scratch[at : at + step, :], ((1,), (1,)))
-            match = id_ref[:, :1] == column_ids(at, where_ref, 1, (1, step))
-            by_row_ref[:, at : at + step] = jnp.where(match, product, 0.0).astype(BF16)
-            product = dot(up_scratch[at : at + step, :], cot_ref[...], ((1,), (1,)))
-            match = column_ids(at, where_ref, 0, (step, 1)) == line_ref[:1, :]
-            by_column_ref[at : at + step, :] = jnp.where(match, product, 0.0).astype(BF16)
-
-    by_row, by_column, half_cot = pl.pallas_call(
-        grads_body,
-        out_shape=(
-            shape(half_rows, columns),
-            shape(columns, half_rows),
-            shape(half_rows, out_width),
-        ),
-        in_specs=[smem] + [vmem] * 4,
-        out_specs=(vmem, vmem, vmem),
-        scratch_shapes=[pltpu.VMEM((columns, out_width), BF16)],
-        compiler_params=params,
-        cost_estimate=cost(4 * half_rows * columns * out_width, 8 * half_rows * columns),
-    )(where, shared, shared_twin, id_rows, id_lines)
-
-    far_cross = other_group(after(down_far, half_cot, frozen_low, frozen_high))
-    maps = (down_near, down_far, near_cross, far_cross)
-
     lines = 2 * rows
 
     def rows_body(cot_ref, grads_ref, low_w, high_w, m0, m1, m2, m3, out_ref):
@@ -634,7 +402,7 @@
     )(x)
 
     small, frozen_near, x_parts = lax.optimization_barrier((small, frozen_near, x_parts))
-    down_near = down_near if False else small[:, :, :pair].reshape(half * piece, pair)
+    down_near = small[:, :, :pair].reshape(half * piece, pair)
 
     shared = small[:, :, pair:id_at].reshape(half * piece, 4 * out_width)
     half_ids = small[:, 0, id_at:].reshape(half_rows).astype(F32)
@@ -655,7 +423,7 @@
     frozen_low = jnp.where(my_half == 0, frozen, frozen_far)
     frozen_high = jnp.where(my_half == 0, frozen_far, frozen)
 
-    x_first = exchange(after(x_parts[0], small, shared_twin)).reshape(half_rows, block)
+    x_first = exchange(after(x_parts[0], small)).reshape(half_rows, block)
 
     x_second = exchange(after(x_parts[1], x_first)).reshape(half_rows, block)
 
@@ -674,7 +442,7 @@
     )(where, shared, shared_twin, id_rows, id_lines)
 
 
-    far_cross = other_group(after(down_far, half_cot, frozen_low, frozen_high))
+    far_cross = other_group(after(down_far, half_cot, frozen_low, frozen_high, x_first))
 
     maps = (down_near, down_far, near_cross, far_cross)
     result = pl.pallas_call(
@@ -689,7 +457,7 @@
         + [pl.BlockSpec((part, pair), lambda i: (0, 0))] * 4,
         out_specs=pl.BlockSpec((lines // rows, rows, pair), lambda i: (i, 0, 0)),
         compiler_params=params,
-        cost_estimate=cost(50000000000, 0),
+        cost_estimate=cost(16000000000, 0),
     )(half_cot, by_row, frozen_low, frozen_high, *maps)
 
 
@@ -723,10 +491,11 @@
     kept_second = down_part(0, after(x_second, low), F32)
 
     low_sum = low
-    for bit in (2, 1, 4):
+    for bit in (2, 1):
         low_sum = low_sum + flipped(low_sum, bit)
 
     joined = lax.optimization_barrier((arrived_first, arrived_second, kept_first, kept_second, low_sum))
+    low_sum = joined[4]
     sums = pl.pallas_call(
         add_body,
         out_shape=shape(half, own, pair),
@@ -747,16 +516,22 @@
     low_all = after(low_sum, sums, gradient)
     low_all = low_all.astype(BF16).reshape(half_rows // lines, lines // packed, packed, rank)
     low_all = low_all.transpose(0, 2, 1, 3).reshape(half_rows, rank)
-    near = jnp.arange(held, dtype=jnp.int32) + here % half * held
-    both = jnp.concatenate([near + my_half * half * held, near + (1 - my_half) * half * held])
+    plane = half // 2
+    planes = n // plane
+    level = jnp.bitwise_xor(here // plane, jnp.arange(planes, dtype=jnp.int32))
+    adapters = ((level * plane + here % plane) * held)[:, None] + jnp.arange(held, dtype=jnp.int32)
     spread = jnp.where(
-        half_ids[:, None] == jnp.repeat(both, rank)[None, :].astype(F32),
-        jnp.tile(low_all, (1, 2 * held)),
+        half_ids[:, None] == jnp.repeat(adapters.reshape(-1), rank)[None, :].astype(F32),
+        jnp.tile(low_all, (1, planes * held)),
         jnp.zeros((), BF16),
     )
-    up_part = (ADAPTER_SCALE * dot(spread, half_cot, ((0,), (0,)))).reshape(2, own, out_width)
-
-    up_grad = (up_part[0] + swapped(up_part[1])).astype(BF16)
+    up_part = (ADAPTER_SCALE * dot(spread, half_cot, ((0,), (0,)))).reshape(planes, own, out_width)
+    up_sent = up_part.astype(BF16)
+
+    up_grad = up_part[0]
+    for level in range(1, planes):
+        up_grad = up_grad + flipped(up_sent[level], level * plane).astype(F32)
+    up_grad = up_grad.astype(BF16)
 
     down_grad = pl.pallas_call(
         unpack_down,

time: 228 us -> 221 us (0.969)
  waiting for transfers between devices: 112 us -> 100 us
  starting transfers between devices: 43.7 us -> 46.3 us
    ppermute x6 -> x5, waiting for transfers between devices: 59.2 us -> 40.3 us  [swapped(): return lax.ppermute(part, 'adapt', [(i, (i + half) % n) for i in range(n)])]
    ppermute x3, waiting for transfers between devices: 13.4 us -> 20.9 us  [other_group(): return lax.ppermute(part, 'groups', [(0, 1), (1, 0)])]
    ppermute x4 -> x6, waiting for transfers between devices: 29.2 us -> 24.2 us  [flipped(): return lax.ppermute(part, 'adapt', [(i, i ^ bit) for i in range(n)])]
    all_to_all x5, waiting for transfers between devices: 9.92 us -> 14.5 us  [exchange(): lax.all_to_all(parts, 'adapt', split_axis=0, concat_axis=0, tiled=True, a...]
    ppermute x4 -> x6, starting transfers between devices: 1.76 us -> 6.21 us  [flipped(): return lax.ppermute(part, 'adapt', [(i, i ^ bit) for i in range(n)])]
    all_to_all x5, starting transfers between devices: 29.3 us -> 26.3 us  [exchange(): lax.all_to_all(parts, 'adapt', split_axis=0, concat_axis=0, tiled=True, a...]
    unnamed x48 -> x36, local copies, waits for them, and re-layouts: 12.7 us -> 11.3 us
    ppermute x6 -> x5, starting transfers between devices: 10 us -> 9.33 us  [swapped(): return lax.ppermute(part, 'adapt', [(i, (i + half) % n) for i in range(n)])]
  transfers between devices with their start and end apart: 18 -> 19, of which waited for: 12 -> 11; matrix products, arithmetic and copies ran while one was open for 5% -> 6% of each run, Pallas kernels for 19% -> 20%
where the time goes in v4:
time: 221 us; the launch traced here: 218 us
  waiting for transfers between devices  100 us (45%)
  starting transfers between devices  46.3 us (21%)
  Pallas kernels  46.1 us (21%)
  local copies, waits for them, and re-layouts  17.8 us (8%)
  other arithmetic  5.05 us (2%)
    ppermute x5, waiting for transfers between devices, swapped(): return lax.ppermute(part, 'adapt', [(i, (i + half) % n) for i in range(n)])  40.3 us
    all_to_all x5, starting transfers between devices, exchange(): lax.all_to_all(parts, 'adapt', split_axis=0, concat_axis=0, tiled=True, a...  26.3 us
    ppermute x6, waiting for transfers between devices, flipped(): return lax.ppermute(part, 'adapt', [(i, i ^ bit) for i in range(n)])  24.2 us
    ppermute x3, waiting for transfers between devices, other_group(): return lax.ppermute(part, 'groups', [(0, 1), (1, 0)])  20.9 us
    all_to_all x5, waiting for transfers between devices, exchange(): lax.all_to_all(parts, 'adapt', split_axis=0, concat_axis=0, tiled=True, a...  14.5 us
    unnamed x36, local copies, waits for them, and re-layouts  11.3 us
    pallas_call x1, Pallas kernels, with_kernels(): pl.pallas_call(low_body, grid=(half_rows // lines,), out_shape=shape(half...  11.2 us
    pallas_call x4, Pallas kernels, down_part(): pl.pallas_call(body, grid=(2,), out_shape=shape(2 * part, block, kind=kin...  9.55 us
  transfers between devices with their start and end apart: 19, of which 11 were waited for; matrix products, arithmetic and copies ran while one was open for 6% of the time, Pallas kernels for 20%

profile of v4, /device:TPU:8, one launch (start us, length us, event | category | flops | bytes accessed | tf_op | source)
XLA Modules:
  0.0 217.9 jit_solution(15325009799256149023)
XLA Ops:
  0.7 2.7 %collective-permute-start = (bf16[64,512]{1,0:T(8,128)(2,1)}, bf16[64,512]{1,0:T(8,128)(2,1)S(1)}, u32[]{:S(2)}, u32[]{:S(2)}) collective-permute-start(bf16[64,512]{1,0:T(8,128)(2,1)} %bitcast.23), channel_id=1, source_target_pairs={{0,8},{1,9},{2,10},{3,11},{4,12},{5,13},{6,14},{7,15},{8,0},{9,1},... | collective-permute-start | bytes 196616 | tf_op jit(solution)/shard_map/ppermute | solution.py:202
  3.4 2.9 %collective-permute-done.far_ref = bf16[64,512]{1,0:T(8,128)(2,1)S(1)} collective-permute-done((bf16[64,512]{1,0:T(8,128)(2,1)}, bf16[64,512]{1,0:T(8,128)(2,1)S(1)}, u32[]{:S(2)}, u32[]{:S(2)}) %collective-permute-start) | collective-permute-done | bytes 65568 | tf_op jit(solution)/shard_map/ppermute | solution.py:202
  7.7 4.9 %all-to-all-start = ((bf16[8,32,3712]{2,1,0:T(8,128)(2,1)}), bf16[8,32,3712]{2,1,0:T(8,128)(2,1)S(1)}, u32[]{:S(2)}, u32[]{:S(2)}) async-start(bf16[8,32,3712]{2,1,0:T(8,128)(2,1)} %shard_map.85), calls=%async_computation | async-start | bytes 3801088 | tf_op jit(solution)/shard_map/all_to_all | solution.py:197
  13.6 2.7 %collective-permute-start.1 = (bf16[384,512]{1,0:T(8,128)(2,1)S(1)}, bf16[384,512]{1,0:T(8,128)(2,1)}, u32[]{:S(2)}, u32[]{:S(2)}) collective-permute-start(bf16[384,512]{1,0:T(8,128)(2,1)S(1)} %constant_dynamic-slice_fusion), channel_id=1, source_target_pairs={{0,8},{1,9},{2,10},{3,11},{4,12},{5,13},{6,14},{7,15},{8,0},{9,1},... | collective-permute-start | bytes 1179656 | tf_op jit(solution)/shard_map/ppermute | solution.py:202
  16.3 2.1 shard_map.86
  20.7 24.6 %collective-permute-done.1 = bf16[384,512]{1,0:T(8,128)(2,1)} collective-permute-done((bf16[384,512]{1,0:T(8,128)(2,1)S(1)}, bf16[384,512]{1,0:T(8,128)(2,1)}, u32[]{:S(2)}, u32[]{:S(2)}) %collective-permute-start.1) | collective-permute-done | bytes 393248 | tf_op jit(solution)/shard_map/ppermute | solution.py:202
  46.6 4.2 %all-to-all-start.1 = ((bf16[8,128,768]{2,1,0:T(8,128)(2,1)}), bf16[8,128,768]{2,1,0:T(8,128)(2,1)S(1)}, u32[]{:S(2)}, u32[]{:S(2)}) async-start(bf16[8,128,768]{2,1,0:T(8,128)(2,1)} %copy-done.7), calls=%async_computation.1 | async-start | bytes 3145728 | tf_op jit(solution)/shard_map/all_to_all | solution.py:197
  50.8 2.3 %slice.25 = bf16[8,32,2048]{2,1,0:T(8,128)(2,1)} slice(bf16[8,32,3712]{2,1,0:T(8,128)(2,1)} %copy-done.16), slice={[0:8], [0:32], [1536:3584]} | slice | bytes 2097152 | tf_op jit(solution)/shard_map/slice | solution.py:407
  54.8 2.1 slice.27
  58.7 6.9 %collective-permute-done.3 = bf16[384,512]{1,0:T(8,128)(2,1)} collective-permute-done((bf16[384,512]{1,0:T(8,128)(2,1)}, bf16[384,512]{1,0:T(8,128)(2,1)}, u32[]{:S(2)}, u32[]{:S(2)}) %collective-permute-start.3) | collective-permute-done | bytes 393248 | tf_op jit(solution)/shard_map/ppermute | solution.py:208
  65.5 1.9 broadcast_select_fusion.3
  67.4 11.1 %all-to-all-done.1 = bf16[8,128,768]{2,1,0:T(8,128)(2,1)S(1)} async-done(((bf16[8,128,768]{2,1,0:T(8,128)(2,1)}), bf16[8,128,768]{2,1,0:T(8,128)(2,1)S(1)}, u32[]{:S(2)}, u32[]{:S(2)}) %all-to-all-start.1) | async-done | bytes 1572896 | tf_op jit(solution)/shard_map/all_to_all | solution.py:197
  78.5 6.6 %all-to-all-start.3 = ((bf16[8,128,768]{2,1,0:T(8,128)(2,1)}), bf16[8,128,768]{2,1,0:T(8,128)(2,1)}, u32[]{:S(2)}, u32[]{:S(2)}) async-start(bf16[8,128,768]{2,1,0:T(8,128)(2,1)} %copy-done.5), calls=%async_computation.3 | async-start | bytes 3145728 | tf_op jit(solution)/shard_map/all_to_all | solution.py:197
  86.9 6.0 %shard_map.87 = (bf16[1024,1024]{1,0:T(8,128)(2,1)S(1)}, bf16[1024,1024]{1,0:T(8,128)(2,1)}, bf16[1024,512]{1,0:T(8,128)(2,1)S(1)}) custom-call(s32[3]{0:T(128)S(1)} %pad_add_fusion.where_ref, bf16[256,2048]{1,0:T(8,128)(2,1)} %bitcast.5.mine_ref, bf16[256,2048]{1,0:T(8,128)(2,1)} %collective-permute-done.2.twin_ref, ...), custom_call_target="tpu_custom_call" | custom-call | flops 2147483648 | bytes 8388608 | tf_op jit(solution)/shard_map/pallas_call | solution.py:430
  94.3 2.5 %collective-permute-start.6 = (bf16[256,1536]{1,0:T(8,128)(2,1)}, bf16[256,1536]{1,0:T(8,128)(2,1)S(1)}, u32[]{:S(2)}, u32[]{:S(2)}) collective-permute-start(bf16[256,1536]{1,0:T(8,128)(2,1)} %collective-permute-done.4.m1), channel_id=1, source_target_pairs={{0,16},{16,0},{1,17},{17,1},{2,18},{18,2},{3,19},{19,3},{4,20},{20... | collective-permute-start | bytes 2359304 | tf_op jit(solution)/shard_map/ppermute | solution.py:208
  98.3 2.4 %shard_map.90 = bf16[512,768]{1,0:T(8,128)(2,1)} custom-call(bf16[1024,1024]{1,0:T(8,128)(2,1)S(1)} %copy-done.1, bf16[1024,1024]{1,0:T(8,128)(2,1)S(1)} %copy-done.1, bf16[1024,768]{1,0:T(8,128)(2,1)S(1)} %bitcast.20), custom_call_target="tpu_custom_call" | custom-call | flops 805306368 | bytes 1572864 | tf_op jit(solution)/shard_map/pallas_call | solution.py:291
  100.7 14.1 %collective-permute-done.6.m3 = bf16[256,1536]{1,0:T(8,128)(2,1)S(1)} collective-permute-done((bf16[256,1536]{1,0:T(8,128)(2,1)}, bf16[256,1536]{1,0:T(8,128)(2,1)S(1)}, u32[]{:S(2)}, u32[]{:S(2)}) %collective-permute-start.6) | collective-permute-done | bytes 786464 | tf_op jit(solution)/shard_map/ppermute | solution.py:208
  114.8 8.3 %shard_map.88 = bf16[8,128,1536]{2,1,0:T(8,128)(2,1)} custom-call(bf16[1024,512]{1,0:T(8,128)(2,1)S(1)} %get-tuple-element.32.cot_ref, bf16[1024,1024]{1,0:T(8,128)(2,1)} %copy-done.15, bf16[768,512]{1,0:T(8,128)(2,1)S(1)} %get-tuple-element.54.low_w, bf16[768,512]{1,0:T(8,128)(2,1)S(1)} %get-tuple-element.53.high_w, bf16[256,1536]{1,0:T(8,128)(2,1)} %bitcast.7.m0, ...), custom_call_target="tpu_custom_call" | custom-call | flops 16000000000 | tf_op jit(solution)/shard_map/pallas_call | solution.py:448
  124.0 4.7 %all-to-all-start.2 = ((bf16[8,128,1536]{2,1,0:T(8,128)(2,1)}), bf16[8,128,1536]{2,1,0:T(8,128)(2,1)}, u32[]{:S(2)}, u32[]{:S(2)}) async-start(bf16[8,128,1536]{2,1,0:T(8,128)(2,1)} %shard_map.88), calls=%async_computation.2 | async-start | bytes 6291456 | tf_op jit(solution)/shard_map/all_to_all | solution.py:197
  128.6 6.4 %collective-permute-done.7.first_ref = bf16[512,768]{1,0:T(8,128)(2,1)} collective-permute-done((bf16[512,768]{1,0:T(8,128)(2,1)}, bf16[512,768]{1,0:T(8,128)(2,1)}, u32[]{:S(2)}, u32[]{:S(2)}) %collective-permute-start.7) | collective-permute-done | bytes 786464 | tf_op jit(solution)/shard_map/ppermute | solution.py:202
  136.7 2.8 %shard_map.91 = bf16[512,768]{1,0:T(8,128)(2,1)S(1)} custom-call(bf16[1024,1024]{1,0:T(8,128)(2,1)S(1)} %copy-done.2, bf16[1024,1024]{1,0:T(8,128)(2,1)S(1)} %copy-done.2, bf16[1024,768]{1,0:T(8,128)(2,1)} %bitcast.9.x_ref.second_ref), custom_call_target="tpu_custom_call" | custom-call | flops 805306368 | bytes 1572864 | tf_op jit(solution)/shard_map/pallas_call | solution.py:291
  139.4 3.5 %collective-permute-start.8 = (bf16[512,768]{1,0:T(8,128)(2,1)S(1)}, bf16[512,768]{1,0:T(8,128)(2,1)S(1)}, u32[]{:S(2)}, u32[]{:S(2)}) collective-permute-start(bf16[512,768]{1,0:T(8,128)(2,1)S(1)} %shard_map.91), channel_id=1, source_target_pairs={{0,8},{1,9},{2,10},{3,11},{4,12},{5,13},{6,14},{7,15},{8,0},{9,1},... | collective-permute-start | bytes 2359304 | tf_op jit(solution)/shard_map/ppermute | solution.py:202
  143.0 11.2 %shard_map.92 = f32[256,128]{1,0:T(8,128)S(1)} custom-call(s32[3]{0:T(128)S(1)} %pad_add_fusion.where_ref, bf16[1024,768]{1,0:T(8,128)(2,1)S(1)} %bitcast.21, bf16[1024,768]{1,0:T(8,128)(2,1)} %bitcast.9.x_ref.second_ref, f32[1024,128]{1,0:T(8,128)S(1)} %copy-done.9, bf16[256,1536]{1,0:T(8,128)(2,1)} %bitcast.7.m0, ...), custom_call_target="tpu_custom_call" | custom-call | flops 3221225472 | bytes 3145728 | tf_op jit(solution)/shard_map/pallas_call | solution.py:474
  155.7 12.1 %collective-permute-done.9 = f32[256,128]{1,0:T(8,128)S(1)} collective-permute-done((f32[256,128]{1,0:T(8,128)S(1)}, f32[256,128]{1,0:T(8,128)S(1)}, u32[]{:S(2)}, u32[]{:S(2)}) %collective-permute-start.9) | collective-permute-done | bytes 131104 | tf_op jit(solution)/shard_map/ppermute | solution.py:205
  168.0 2.7 %shard_map.94.kept_second_ref = f32[512,768]{1,0:T(8,128)S(1)} custom-call(bf16[1024,1024]{1,0:T(8,128)(2,1)S(1)} %copy-done.3, bf16[1024,1024]{1,0:T(8,128)(2,1)S(1)} %copy-done.3, bf16[1024,768]{1,0:T(8,128)(2,1)} %bitcast.9.x_ref.second_ref), custom_call_target="tpu_custom_call" | custom-call | flops 805306368 | bytes 1572864 | tf_op jit(solution)/shard_map/pallas_call | solution.py:291
  173.6 6.4 %collective-permute-done.8.second_ref = bf16[512,768]{1,0:T(8,128)(2,1)S(1)} collective-permute-done((bf16[512,768]{1,0:T(8,128)(2,1)S(1)}, bf16[512,768]{1,0:T(8,128)(2,1)S(1)}, u32[]{:S(2)}, u32[]{:S(2)}) %collective-permute-start.8) | collective-permute-done | bytes 786464 | tf_op jit(solution)/shard_map/ppermute | solution.py:202
  180.0 2.0 shard_map.95
  183.1 3.4 %all-to-all-done.2.in_ref = bf16[8,128,1536]{2,1,0:T(8,128)(2,1)} async-done(((bf16[8,128,1536]{2,1,0:T(8,128)(2,1)}), bf16[8,128,1536]{2,1,0:T(8,128)(2,1)}, u32[]{:S(2)}, u32[]{:S(2)}) %all-to-all-start.2) | async-done | bytes 3145760 | tf_op jit(solution)/shard_map/all_to_all | solution.py:197
  186.6 6.0 %all-to-all-start.4 = ((bf16[8,64,1536]{2,1,0:T(8,128)(2,1)}), bf16[8,64,1536]{2,1,0:T(8,128)(2,1)S(1)}, u32[]{:S(2)}, u32[]{:S(2)}) async-start(bf16[8,64,1536]{2,1,0:T(8,128)(2,1)} %copy-done.6), calls=%async_computation.4 | async-start | bytes 3145728 | tf_op jit(solution)/shard_map/all_to_all | solution.py:197
  192.9 3.8 %shard_map.89 = bf16[128,12288]{1,0:T(8,128)(2,1)} custom-call(bf16[8,128,1536]{2,1,0:T(8,128)(2,1)} %all-to-all-done.2.in_ref), custom_call_target="tpu_custom_call" | custom-call | bytes 6291456 | tf_op jit(solution)/shard_map/pallas_call | solution.py:508
  200.2 3.2 %collective-permute-start.12 = (bf16[64,512]{1,0:T(8,128)(2,1)S(1)}, bf16[64,512]{1,0:T(8,128)(2,1)S(1)}, u32[]{:S(2)}, u32[]{:S(2)}) collective-permute-start(bf16[64,512]{1,0:T(8,128)(2,1)S(1)} %get-tuple-element.59), channel_id=1, source_target_pairs={{0,8},{1,9},{2,10},{3,11},{4,12},{5,13},{6,14},{7,15},{8,0},{9,1},... | collective-permute-start | bytes 196616 | tf_op jit(solution)/shard_map/ppermute | solution.py:205
  203.4 11.0 %collective-permute-done.11 = bf16[64,512]{1,0:T(8,128)(2,1)S(1)} collective-permute-done((bf16[64,512]{1,0:T(8,128)(2,1)S(1)}, bf16[64,512]{1,0:T(8,128)(2,1)S(1)}, u32[]{:S(2)}, u32[]{:S(2)}) %collective-permute-start.11) | collective-permute-done | bytes 65568 | tf_op jit(solution)/shard_map/ppermute | solution.py:205
  (81 shorter events, 29.7 us)
Async XLA Ops:
  0.6 2.7 %copy-start = (bf16[2,32,12288]{2,1,0:T(8,128)(2,1)S(1)}, bf16[2,32,12288]{2,1,0:T(8,128)(2,1)}, u32[]{:S(2)}) copy-start(bf16[2,32,12288]{2,1,0:T(8,128)(2,1)} %param.10) | copy-start | bytes 4718596
  0.6 5.6 %copy-start.11 = (bf16[2,32,512]{2,1,0:T(8,128)(2,1)S(1)}, bf16[2,32,512]{2,1,0:T(8,128)(2,1)}, u32[]{:S(2)}) copy-start(bf16[2,32,512]{2,1,0:T(8,128)(2,1)} %param.11) | copy-start | bytes 196612
  0.7 2.7 %copy-start.17 = (s32[128]{0:T(128)S(1)}, s32[128]{0:T(128)}, u32[]{:S(2)}) copy-start(s32[128]{0:T(128)} %param.8) | copy-start | bytes 1540
  0.7 5.6 %copy-start.10 = (bf16[128,512]{1,0:T(8,128)(2,1)S(1)}, bf16[128,512]{1,0:T(8,128)(2,1)}, u32[]{:S(2)}) copy-start(bf16[128,512]{1,0:T(8,128)(2,1)} %cot_ref.1) | copy-start | bytes 393220
  0.7 5.6 %collective-permute-start = (bf16[64,512]{1,0:T(8,128)(2,1)}, bf16[64,512]{1,0:T(8,128)(2,1)S(1)}, u32[]{:S(2)}, u32[]{:S(2)}) collective-permute-start(bf16[64,512]{1,0:T(8,128)(2,1)} %bitcast.23), channel_id=1, source_target_pairs={{0,8},{1,9},{2,10},{3,11},{4,12},{5,13},{6,14},{7,15},{8,0},{9,1},... | collective-permute-start | bytes 196616 | tf_op jit(solution)/shard_map/ppermute | solution.py:202
  7.7 37.6 %all-to-all-start = ((bf16[8,32,3712]{2,1,0:T(8,128)(2,1)}), bf16[8,32,3712]{2,1,0:T(8,128)(2,1)S(1)}, u32[]{:S(2)}, u32[]{:S(2)}) async-start(bf16[8,32,3712]{2,1,0:T(8,128)(2,1)} %shard_map.85), calls=%async_computation | async-start | bytes 3801088 | tf_op jit(solution)/shard_map/all_to_all | solution.py:197
  13.6 31.7 %collective-permute-start.1 = (bf16[384,512]{1,0:T(8,128)(2,1)S(1)}, bf16[384,512]{1,0:T(8,128)(2,1)}, u32[]{:S(2)}, u32[]{:S(2)}) collective-permute-start(bf16[384,512]{1,0:T(8,128)(2,1)S(1)} %constant_dynamic-slice_fusion), channel_id=1, source_target_pairs={{0,8},{1,9},{2,10},{3,11},{4,12},{5,13},{6,14},{7,15},{8,0},{9,1},... | collective-permute-start | bytes 1179656 | tf_op jit(solution)/shard_map/ppermute | solution.py:202
  45.3 1.3 copy-start.16
  46.6 32.0 %all-to-all-start.1 = ((bf16[8,128,768]{2,1,0:T(8,128)(2,1)}), bf16[8,128,768]{2,1,0:T(8,128)(2,1)S(1)}, u32[]{:S(2)}, u32[]{:S(2)}) async-start(bf16[8,128,768]{2,1,0:T(8,128)(2,1)} %copy-done.7), calls=%async_computation.1 | async-start | bytes 3145728 | tf_op jit(solution)/shard_map/all_to_all | solution.py:197
  53.1 33.6 %collective-permute-start.2 = (bf16[256,2048]{1,0:T(8,128)(2,1)}, bf16[256,2048]{1,0:T(8,128)(2,1)}, u32[]{:S(2)}, u32[]{:S(2)}) collective-permute-start(bf16[256,2048]{1,0:T(8,128)(2,1)} %bitcast.5.mine_ref), channel_id=1, source_target_pairs={{0,1},{1,0},{2,3},{3,2},{4,5},{5,4},{6,7},{7,6},{8,9},{9,8},{10,11... | collective-permute-start | bytes 3145736 | tf_op jit(solution)/shard_map/ppermute | solution.py:205
  53.3 12.3 %collective-permute-start.3 = (bf16[384,512]{1,0:T(8,128)(2,1)}, bf16[384,512]{1,0:T(8,128)(2,1)}, u32[]{:S(2)}, u32[]{:S(2)}) collective-permute-start(bf16[384,512]{1,0:T(8,128)(2,1)} %collective-permute-done.1), channel_id=1, source_target_pairs={{0,16},{16,0},{1,17},{17,1},{2,18},{18,2},{3,19},{19,3},{4,20},{20... | collective-permute-start | bytes 1179656 | tf_op jit(solution)/shard_map/ppermute | solution.py:208
  56.9 37.3 %collective-permute-start.4 = (bf16[256,1536]{1,0:T(8,128)(2,1)}, bf16[256,1536]{1,0:T(8,128)(2,1)}, u32[]{:S(2)}, u32[]{:S(2)}) collective-permute-start(bf16[256,1536]{1,0:T(8,128)(2,1)} %bitcast.7.m0), channel_id=1, source_target_pairs={{0,8},{1,9},{2,10},{3,11},{4,12},{5,13},{6,14},{7,15},{8,0},{9,1},... | collective-permute-start | bytes 2359304 | tf_op jit(solution)/shard_map/ppermute | solution.py:202
  58.1 42.6 %collective-permute-start.5 = (bf16[256,1536]{1,0:T(8,128)(2,1)}, bf16[256,1536]{1,0:T(8,128)(2,1)}, u32[]{:S(2)}, u32[]{:S(2)}) collective-permute-start(bf16[256,1536]{1,0:T(8,128)(2,1)} %bitcast.7.m0), channel_id=1, source_target_pairs={{0,16},{16,0},{1,17},{17,1},{2,18},{18,2},{3,19},{19,3},{4,20},{20... | collective-permute-start | bytes 2359304 | tf_op jit(solution)/shard_map/ppermute | solution.py:208
  78.5 45.4 %all-to-all-start.3 = ((bf16[8,128,768]{2,1,0:T(8,128)(2,1)}), bf16[8,128,768]{2,1,0:T(8,128)(2,1)}, u32[]{:S(2)}, u32[]{:S(2)}) async-start(bf16[8,128,768]{2,1,0:T(8,128)(2,1)} %copy-done.5), calls=%async_computation.3 | async-start | bytes 3145728 | tf_op jit(solution)/shard_map/all_to_all | solution.py:197
  86.9 6.1 %copy-start.8 = (f32[1024,128]{1,0:T(8,128)}, f32[1024,128]{1,0:T(8,128)S(1)}, u32[]{:S(2)}) copy-start(f32[1024,128]{1,0:T(8,128)S(1)} %broadcast_in_dim.12.id_ref) | copy-start | bytes 1572868
  92.9 1.3 copy-start.15
  94.3 20.5 %copy-start.14 = (bf16[1024,512]{1,0:T(8,128)(2,1)}, bf16[1024,512]{1,0:T(8,128)(2,1)S(1)}, u32[]{:S(2)}) copy-start(bf16[1024,512]{1,0:T(8,128)(2,1)S(1)} %get-tuple-element.32.cot_ref) | copy-start | bytes 3145732
  94.3 20.5 %collective-permute-start.6 = (bf16[256,1536]{1,0:T(8,128)(2,1)}, bf16[256,1536]{1,0:T(8,128)(2,1)S(1)}, u32[]{:S(2)}, u32[]{:S(2)}) collective-permute-start(bf16[256,1536]{1,0:T(8,128)(2,1)} %collective-permute-done.4.m1), channel_id=1, source_target_pairs={{0,16},{16,0},{1,17},{17,1},{2,18},{18,2},{3,19},{19,3},{4,20},{20... | collective-permute-start | bytes 2359304 | tf_op jit(solution)/shard_map/ppermute | solution.py:208
  96.7 1.6 copy-start.1
  100.7 34.4 %collective-permute-start.7 = (bf16[512,768]{1,0:T(8,128)(2,1)}, bf16[512,768]{1,0:T(8,128)(2,1)}, u32[]{:S(2)}, u32[]{:S(2)}) collective-permute-start(bf16[512,768]{1,0:T(8,128)(2,1)} %shard_map.90), channel_id=1, source_target_pairs={{0,8},{1,9},{2,10},{3,11},{4,12},{5,13},{6,14},{7,15},{8,0},{9,1},... | collective-permute-start | bytes 2359304 | tf_op jit(solution)/shard_map/ppermute | solution.py:202
  124.0 62.6 %all-to-all-start.2 = ((bf16[8,128,1536]{2,1,0:T(8,128)(2,1)}), bf16[8,128,1536]{2,1,0:T(8,128)(2,1)}, u32[]{:S(2)}, u32[]{:S(2)}) async-start(bf16[8,128,1536]{2,1,0:T(8,128)(2,1)} %shard_map.88), calls=%async_computation.2 | async-start | bytes 6291456 | tf_op jit(solution)/shard_map/all_to_all | solution.py:197
  135.1 1.6 copy-start.2
  136.7 6.3 %copy-start.9 = (f32[1024,128]{1,0:T(8,128)S(1)}, f32[1024,128]{1,0:T(8,128)}, u32[]{:S(2)}) copy-start(f32[1024,128]{1,0:T(8,128)} %copy-done.8) | copy-start | bytes 1572868
  136.7 6.3 %copy-start.13 = (bf16[256,1536]{1,0:T(8,128)(2,1)S(1)}, bf16[256,1536]{1,0:T(8,128)(2,1)}, u32[]{:S(2)}) copy-start(bf16[256,1536]{1,0:T(8,128)(2,1)} %copy-done.12) | copy-start | bytes 2359300
  139.4 40.5 %collective-permute-start.8 = (bf16[512,768]{1,0:T(8,128)(2,1)S(1)}, bf16[512,768]{1,0:T(8,128)(2,1)S(1)}, u32[]{:S(2)}, u32[]{:S(2)}) collective-permute-start(bf16[512,768]{1,0:T(8,128)(2,1)S(1)} %shard_map.91), channel_id=1, source_target_pairs={{0,8},{1,9},{2,10},{3,11},{4,12},{5,13},{6,14},{7,15},{8,0},{9,1},... | collective-permute-start | bytes 2359304 | tf_op jit(solution)/shard_map/ppermute | solution.py:202
  142.9 25.0 %copy-start.3 = (bf16[1024,1024]{1,0:T(8,128)(2,1)S(1)}, bf16[1024,1024]{1,0:T(8,128)(2,1)}, u32[]{:S(2)}) copy-start(bf16[1024,1024]{1,0:T(8,128)(2,1)} %get-tuple-element.38.first_ref.second_ref) | copy-start | bytes 6291460
  154.2 13.7 %collective-permute-start.9 = (f32[256,128]{1,0:T(8,128)S(1)}, f32[256,128]{1,0:T(8,128)S(1)}, u32[]{:S(2)}, u32[]{:S(2)}) collective-permute-start(f32[256,128]{1,0:T(8,128)S(1)} %shard_map.92), channel_id=1, source_target_pairs={{0,2},{1,3},{2,0},{3,1},{4,6},{5,7},{6,4},{7,5},{8,10},{9,11},{10,... | collective-permute-start | bytes 393224 | tf_op jit(solution)/shard_map/ppermute | solution.py:205
  167.9 5.7 %collective-permute-start.10 = (f32[256,128]{1,0:T(8,128)S(1)}, f32[256,128]{1,0:T(8,128)S(1)}, u32[]{:S(2)}, u32[]{:S(2)}) collective-permute-start(f32[256,128]{1,0:T(8,128)S(1)} %add.58), channel_id=1, source_target_pairs={{0,1},{1,0},{2,3},{3,2},{4,5},{5,4},{6,7},{7,6},{8,9},{9,8},{10,11... | collective-permute-start | bytes 393224 | tf_op jit(solution)/shard_map/ppermute | solution.py:205
  186.6 29.6 %all-to-all-start.4 = ((bf16[8,64,1536]{2,1,0:T(8,128)(2,1)}), bf16[8,64,1536]{2,1,0:T(8,128)(2,1)S(1)}, u32[]{:S(2)}, u32[]{:S(2)}) async-start(bf16[8,64,1536]{2,1,0:T(8,128)(2,1)} %copy-done.6), calls=%async_computation.4 | async-start | bytes 3145728 | tf_op jit(solution)/shard_map/all_to_all | solution.py:197
  198.9 15.4 %collective-permute-start.11 = (bf16[64,512]{1,0:T(8,128)(2,1)S(1)}, bf16[64,512]{1,0:T(8,128)(2,1)S(1)}, u32[]{:S(2)}, u32[]{:S(2)}) collective-permute-start(bf16[64,512]{1,0:T(8,128)(2,1)S(1)} %get-tuple-element.57), channel_id=1, source_target_pairs={{0,4},{1,5},{2,6},{3,7},{4,0},{5,1},{6,2},{7,3},{8,12},{9,13},{10,... | collective-permute-start | bytes 196616 | tf_op jit(solution)/shard_map/ppermute | solution.py:205
  199.1 15.2 %collective-permute-start.13 = (bf16[64,512]{1,0:T(8,128)(2,1)S(1)}, bf16[64,512]{1,0:T(8,128)(2,1)S(1)}, u32[]{:S(2)}, u32[]{:S(2)}) collective-permute-start(bf16[64,512]{1,0:T(8,128)(2,1)S(1)} %get-tuple-element.58), channel_id=1, source_target_pairs={{0,12},{1,13},{2,14},{3,15},{4,8},{5,9},{6,10},{7,11},{8,4},{9,5},... | collective-permute-start | bytes 196616 | tf_op jit(solution)/shard_map/ppermute | solution.py:205
  200.2 15.2 %collective-permute-start.12 = (bf16[64,512]{1,0:T(8,128)(2,1)S(1)}, bf16[64,512]{1,0:T(8,128)(2,1)S(1)}, u32[]{:S(2)}, u32[]{:S(2)}) collective-permute-start(bf16[64,512]{1,0:T(8,128)(2,1)S(1)} %get-tuple-element.59), channel_id=1, source_target_pairs={{0,8},{1,9},{2,10},{3,11},{4,12},{5,13},{6,14},{7,15},{8,0},{9,1},... | collective-permute-start | bytes 196616 | tf_op jit(solution)/shard_map/ppermute | solution.py:205
  (5 other events, 5.5 us)

commit v5 on v4

--- a/solution.py
+++ b/solution.py
@@ -9,7 +9,7 @@
 F32 = jnp.float32
 BF16 = jnp.bfloat16
 LANES = 128
-VMEM_BYTES = 48 * 1024 * 1024
+VMEM_BYTES = 28 * 1024 * 1024
 
 
 def dot(a, b, dims):

time: 221 us -> 217 us (0.982)
  Pallas kernels: 46.1 us -> 41.1 us
    all_to_all x5, waiting for transfers between devices: 14.5 us -> 11.2 us  [exchange(): lax.all_to_all(parts, 'adapt', split_axis=0, concat_axis=0, tiled=True, a...]
    ppermute x6, waiting for transfers between devices: 24.2 us -> 27.1 us  [flipped(): return lax.ppermute(part, 'adapt', [(i, i ^ bit) for i in range(n)])]
  transfers between devices with their start and end apart: 19 -> 19, of which waited for: 11 -> 12; matrix products, arithmetic and copies ran while one was open for 6% -> 6% of each run, Pallas kernels for 20% -> 18%
where the time goes in v5:
time: 217 us; the launch traced here: 214 us
  waiting for transfers between devices  99.5 us (46%)
  starting transfers between devices  48.5 us (22%)
  Pallas kernels  41.1 us (19%)
  local copies, waits for them, and re-layouts  17.3 us (8%)
  other arithmetic  5.03 us (2%)
    ppermute x5, waiting for transfers between devices, swapped(): return lax.ppermute(part, 'adapt', [(i, (i + half) % n) for i in range(n)])  40.1 us
    ppermute x6, waiting for transfers between devices, flipped(): return lax.ppermute(part, 'adapt', [(i, i ^ bit) for i in range(n)])  27.1 us
    all_to_all x5, starting transfers between devices, exchange(): lax.all_to_all(parts, 'adapt', split_axis=0, concat_axis=0, tiled=True, a...  27 us
    ppermute x3, waiting for transfers between devices, other_group(): return lax.ppermute(part, 'groups', [(0, 1), (1, 0)])  21 us
    all_to_all x5, waiting for transfers between devices, exchange(): lax.all_to_all(parts, 'adapt', split_axis=0, concat_axis=0, tiled=True, a...  11.2 us
    pallas_call x1, Pallas kernels, with_kernels(): pl.pallas_call(low_body, grid=(half_rows // lines,), out_shape=shape(half...  11.2 us
    ppermute x5, starting transfers between devices, swapped(): return lax.ppermute(part, 'adapt', [(i, (i + half) % n) for i in range(n)])  10.9 us
    unnamed x36, local copies, waits for them, and re-layouts  10.8 us
  transfers between devices with their start and end apart: 19, of which 12 were waited for; matrix products, arithmetic and copies ran while one was open for 6% of the time, Pallas kernels for 18%

profile of v5, /device:TPU:8, one launch (start us, length us, event | category | flops | bytes accessed | tf_op | source)
XLA Modules:
  0.0 214.0 jit_solution(14961380437557282862)
XLA Ops:
  0.7 2.7 %collective-permute-start = (bf16[64,512]{1,0:T(8,128)(2,1)}, bf16[64,512]{1,0:T(8,128)(2,1)S(1)}, u32[]{:S(2)}, u32[]{:S(2)}) collective-permute-start(bf16[64,512]{1,0:T(8,128)(2,1)} %bitcast.23), channel_id=1, source_target_pairs={{0,8},{1,9},{2,10},{3,11},{4,12},{5,13},{6,14},{7,15},{8,0},{9,1},... | collective-permute-start | bytes 196616 | tf_op jit(solution)/shard_map/ppermute | solution.py:202
  3.4 2.9 %collective-permute-done.far_ref = bf16[64,512]{1,0:T(8,128)(2,1)S(1)} collective-permute-done((bf16[64,512]{1,0:T(8,128)(2,1)}, bf16[64,512]{1,0:T(8,128)(2,1)S(1)}, u32[]{:S(2)}, u32[]{:S(2)}) %collective-permute-start) | collective-permute-done | bytes 65568 | tf_op jit(solution)/shard_map/ppermute | solution.py:202
  7.7 4.9 %all-to-all-start = ((bf16[8,32,3712]{2,1,0:T(8,128)(2,1)}), bf16[8,32,3712]{2,1,0:T(8,128)(2,1)S(1)}, u32[]{:S(2)}, u32[]{:S(2)}) async-start(bf16[8,32,3712]{2,1,0:T(8,128)(2,1)} %shard_map.85), calls=%async_computation | async-start | bytes 3801088 | tf_op jit(solution)/shard_map/all_to_all | solution.py:197
  13.6 2.7 %collective-permute-start.1 = (bf16[384,512]{1,0:T(8,128)(2,1)S(1)}, bf16[384,512]{1,0:T(8,128)(2,1)}, u32[]{:S(2)}, u32[]{:S(2)}) collective-permute-start(bf16[384,512]{1,0:T(8,128)(2,1)S(1)} %constant_dynamic-slice_fusion), channel_id=1, source_target_pairs={{0,8},{1,9},{2,10},{3,11},{4,12},{5,13},{6,14},{7,15},{8,0},{9,1},... | collective-permute-start | bytes 1179656 | tf_op jit(solution)/shard_map/ppermute | solution.py:202
  16.3 1.9 copy-done.4
  20.7 24.6 %collective-permute-done.1 = bf16[384,512]{1,0:T(8,128)(2,1)} collective-permute-done((bf16[384,512]{1,0:T(8,128)(2,1)S(1)}, bf16[384,512]{1,0:T(8,128)(2,1)}, u32[]{:S(2)}, u32[]{:S(2)}) %collective-permute-start.1) | collective-permute-done | bytes 393248 | tf_op jit(solution)/shard_map/ppermute | solution.py:202
  46.6 4.2 %all-to-all-start.1 = ((bf16[8,128,768]{2,1,0:T(8,128)(2,1)}), bf16[8,128,768]{2,1,0:T(8,128)(2,1)S(1)}, u32[]{:S(2)}, u32[]{:S(2)}) async-start(bf16[8,128,768]{2,1,0:T(8,128)(2,1)} %copy-done.8), calls=%async_computation.1 | async-start | bytes 3145728 | tf_op jit(solution)/shard_map/all_to_all | solution.py:197
  50.8 2.3 %slice.25 = bf16[8,32,2048]{2,1,0:T(8,128)(2,1)} slice(bf16[8,32,3712]{2,1,0:T(8,128)(2,1)} %copy-done.16), slice={[0:8], [0:32], [1536:3584]} | slice | bytes 2097152 | tf_op jit(solution)/shard_map/slice | solution.py:407
  54.8 2.2 %slice.27 = bf16[8,32,1536]{2,1,0:T(8,128)(2,1)} slice(bf16[8,32,3712]{2,1,0:T(8,128)(2,1)} %copy-done.16), slice={[0:8], [0:32], [0:1536]} | slice | bytes 1572864 | tf_op jit(solution)/shard_map/slice | solution.py:405
  58.7 6.8 %collective-permute-done.3 = bf16[384,512]{1,0:T(8,128)(2,1)} collective-permute-done((bf16[384,512]{1,0:T(8,128)(2,1)}, bf16[384,512]{1,0:T(8,128)(2,1)}, u32[]{:S(2)}, u32[]{:S(2)}) %collective-permute-start.3) | collective-permute-done | bytes 393248 | tf_op jit(solution)/shard_map/ppermute | solution.py:208
  65.5 1.9 broadcast_select_fusion.3
  67.4 11.1 %all-to-all-done.1 = bf16[8,128,768]{2,1,0:T(8,128)(2,1)S(1)} async-done(((bf16[8,128,768]{2,1,0:T(8,128)(2,1)}), bf16[8,128,768]{2,1,0:T(8,128)(2,1)S(1)}, u32[]{:S(2)}, u32[]{:S(2)}) %all-to-all-start.1) | async-done | bytes 1572896 | tf_op jit(solution)/shard_map/all_to_all | solution.py:197
  78.5 6.6 %all-to-all-start.3 = ((bf16[8,128,768]{2,1,0:T(8,128)(2,1)}), bf16[8,128,768]{2,1,0:T(8,128)(2,1)}, u32[]{:S(2)}, u32[]{:S(2)}) async-start(bf16[8,128,768]{2,1,0:T(8,128)(2,1)} %copy-done.6), calls=%async_computation.3 | async-start | bytes 3145728 | tf_op jit(solution)/shard_map/all_to_all | solution.py:197
  86.9 4.7 %shard_map.87 = (bf16[1024,1024]{1,0:T(8,128)(2,1)S(1)}, bf16[1024,1024]{1,0:T(8,128)(2,1)S(1)}, bf16[1024,512]{1,0:T(8,128)(2,1)S(1)}) custom-call(s32[3]{0:T(128)S(1)} %pad_add_fusion.where_ref, bf16[256,2048]{1,0:T(8,128)(2,1)} %bitcast.5.mine_ref, bf16[256,2048]{1,0:T(8,128)(2,1)} %collective-permute-done.2.twin_ref, ...), custom_call_target="tpu_custom_call" | custom-call | flops 2147483648 | bytes 8388608 | tf_op jit(solution)/shard_map/pallas_call | solution.py:430
  91.7 2.4 %collective-permute-start.6 = (bf16[256,1536]{1,0:T(8,128)(2,1)}, bf16[256,1536]{1,0:T(8,128)(2,1)S(1)}, u32[]{:S(2)}, u32[]{:S(2)}) collective-permute-start(bf16[256,1536]{1,0:T(8,128)(2,1)} %collective-permute-done.4.m1), channel_id=1, source_target_pairs={{0,16},{16,0},{1,17},{17,1},{2,18},{18,2},{3,19},{19,3},{4,20},{20... | collective-permute-start | bytes 2359304 | tf_op jit(solution)/shard_map/ppermute | solution.py:208
  94.1 2.3 %shard_map.90 = bf16[512,768]{1,0:T(8,128)(2,1)} custom-call(bf16[1024,1024]{1,0:T(8,128)(2,1)S(1)} %get-tuple-element.38.first_ref.second_ref, bf16[1024,1024]{1,0:T(8,128)(2,1)S(1)} %get-tuple-element.38.first_ref.second_ref, bf16[1024,768]{1,0:T(8,128)(2,1)S(1)} %bitcast.20), custom_call_target="tpu_custom_call" | custom-call | flops 805306368 | bytes 1572864 | tf_op jit(solution)/shard_map/pallas_call | solution.py:291
  98.0 14.2 %collective-permute-done.6.m3 = bf16[256,1536]{1,0:T(8,128)(2,1)S(1)} collective-permute-done((bf16[256,1536]{1,0:T(8,128)(2,1)}, bf16[256,1536]{1,0:T(8,128)(2,1)S(1)}, u32[]{:S(2)}, u32[]{:S(2)}) %collective-permute-start.6) | collective-permute-done | bytes 786464 | tf_op jit(solution)/shard_map/ppermute | solution.py:208
  112.2 7.2 %shard_map.88 = bf16[8,128,1536]{2,1,0:T(8,128)(2,1)S(1)} custom-call(bf16[1024,512]{1,0:T(8,128)(2,1)S(1)} %get-tuple-element.32.cot_ref, bf16[1024,1024]{1,0:T(8,128)(2,1)S(1)} %get-tuple-element.33.grads_ref, bf16[768,512]{1,0:T(8,128)(2,1)S(1)} %get-tuple-element.54.low_w, bf16[768,512]{1,0:T(8,128)(2,1)S(1)} %get-tuple-element.53.high_w, ...), custom_call_target="tpu_custom_call" | custom-call | flops 16000000000 | tf_op jit(solution)/shard_map/pallas_call | solution.py:448
  121.9 5.3 %all-to-all-start.2 = ((bf16[8,128,1536]{2,1,0:T(8,128)(2,1)}), bf16[8,128,1536]{2,1,0:T(8,128)(2,1)}, u32[]{:S(2)}, u32[]{:S(2)}) async-start(bf16[8,128,1536]{2,1,0:T(8,128)(2,1)} %copy-done.5), calls=%async_computation.2 | async-start | bytes 6291456 | tf_op jit(solution)/shard_map/all_to_all | solution.py:197
  127.3 3.9 %collective-permute-done.7.first_ref = bf16[512,768]{1,0:T(8,128)(2,1)} collective-permute-done((bf16[512,768]{1,0:T(8,128)(2,1)}, bf16[512,768]{1,0:T(8,128)(2,1)}, u32[]{:S(2)}, u32[]{:S(2)}) %collective-permute-start.7) | collective-permute-done | bytes 786464 | tf_op jit(solution)/shard_map/ppermute | solution.py:202
  132.7 2.7 %shard_map.91 = bf16[512,768]{1,0:T(8,128)(2,1)S(1)} custom-call(bf16[1024,1024]{1,0:T(8,128)(2,1)S(1)} %copy-done.2, bf16[1024,1024]{1,0:T(8,128)(2,1)S(1)} %copy-done.2, bf16[1024,768]{1,0:T(8,128)(2,1)} %bitcast.9.x_ref.second_ref), custom_call_target="tpu_custom_call" | custom-call | flops 805306368 | bytes 1572864 | tf_op jit(solution)/shard_map/pallas_call | solution.py:291
  135.5 3.5 %collective-permute-start.8 = (bf16[512,768]{1,0:T(8,128)(2,1)S(1)}, bf16[512,768]{1,0:T(8,128)(2,1)S(1)}, u32[]{:S(2)}, u32[]{:S(2)}) collective-permute-start(bf16[512,768]{1,0:T(8,128)(2,1)S(1)} %shard_map.91), channel_id=1, source_target_pairs={{0,8},{1,9},{2,10},{3,11},{4,12},{5,13},{6,14},{7,15},{8,0},{9,1},... | collective-permute-start | bytes 2359304 | tf_op jit(solution)/shard_map/ppermute | solution.py:202
  139.0 11.2 %shard_map.92 = f32[256,128]{1,0:T(8,128)S(1)} custom-call(s32[3]{0:T(128)S(1)} %pad_add_fusion.where_ref, bf16[1024,768]{1,0:T(8,128)(2,1)S(1)} %bitcast.21, bf16[1024,768]{1,0:T(8,128)(2,1)} %bitcast.9.x_ref.second_ref, f32[1024,128]{1,0:T(8,128)S(1)} %copy-done.10, bf16[256,1536]{1,0:T(8,128)(2,1)} %bitcast.7.m0, ...), custom_call_target="tpu_custom_call" | custom-call | flops 3221225472 | bytes 3145728 | tf_op jit(solution)/shard_map/pallas_call | solution.py:474
  151.7 14.7 %collective-permute-done.9 = f32[256,128]{1,0:T(8,128)S(1)} collective-permute-done((f32[256,128]{1,0:T(8,128)S(1)}, f32[256,128]{1,0:T(8,128)S(1)}, u32[]{:S(2)}, u32[]{:S(2)}) %collective-permute-start.9) | collective-permute-done | bytes 131104 | tf_op jit(solution)/shard_map/ppermute | solution.py:205
  166.6 2.7 %shard_map.94.kept_second_ref = f32[512,768]{1,0:T(8,128)S(1)} custom-call(bf16[1024,1024]{1,0:T(8,128)(2,1)S(1)} %copy-done.3, bf16[1024,1024]{1,0:T(8,128)(2,1)S(1)} %copy-done.3, bf16[1024,768]{1,0:T(8,128)(2,1)} %bitcast.9.x_ref.second_ref), custom_call_target="tpu_custom_call" | custom-call | flops 805306368 | bytes 1572864 | tf_op jit(solution)/shard_map/pallas_call | solution.py:291
  171.0 8.7 %collective-permute-done.8.second_ref = bf16[512,768]{1,0:T(8,128)(2,1)S(1)} collective-permute-done((bf16[512,768]{1,0:T(8,128)(2,1)S(1)}, bf16[512,768]{1,0:T(8,128)(2,1)S(1)}, u32[]{:S(2)}, u32[]{:S(2)}) %collective-permute-start.8) | collective-permute-done | bytes 786464 | tf_op jit(solution)/shard_map/ppermute | solution.py:202
  182.3 6.0 %all-to-all-start.4 = ((bf16[8,64,1536]{2,1,0:T(8,128)(2,1)}), bf16[8,64,1536]{2,1,0:T(8,128)(2,1)S(1)}, u32[]{:S(2)}, u32[]{:S(2)}) async-start(bf16[8,64,1536]{2,1,0:T(8,128)(2,1)} %copy-done.7), calls=%async_computation.4 | async-start | bytes 3145728 | tf_op jit(solution)/shard_map/all_to_all | solution.py:197
  188.6 3.8 %shard_map.89 = bf16[128,12288]{1,0:T(8,128)(2,1)} custom-call(bf16[8,128,1536]{2,1,0:T(8,128)(2,1)} %all-to-all-done.2.in_ref), custom_call_target="tpu_custom_call" | custom-call | bytes 6291456 | tf_op jit(solution)/shard_map/pallas_call | solution.py:508
  192.9 1.7 fusion.8
  196.2 2.9 %collective-permute-start.12 = (bf16[64,512]{1,0:T(8,128)(2,1)S(1)}, bf16[64,512]{1,0:T(8,128)(2,1)S(1)}, u32[]{:S(2)}, u32[]{:S(2)}) collective-permute-start(bf16[64,512]{1,0:T(8,128)(2,1)S(1)} %get-tuple-element.59), channel_id=1, source_target_pairs={{0,8},{1,9},{2,10},{3,11},{4,12},{5,13},{6,14},{7,15},{8,0},{9,1},... | collective-permute-start | bytes 196616 | tf_op jit(solution)/shard_map/ppermute | solution.py:205
  199.1 11.0 %collective-permute-done.11 = bf16[64,512]{1,0:T(8,128)(2,1)S(1)} collective-permute-done((bf16[64,512]{1,0:T(8,128)(2,1)S(1)}, bf16[64,512]{1,0:T(8,128)(2,1)S(1)}, u32[]{:S(2)}, u32[]{:S(2)}) %collective-permute-start.11) | collective-permute-done | bytes 65568 | tf_op jit(solution)/shard_map/ppermute | solution.py:205
  212.2 1.8 shard_map.96
  (81 shorter events, 27.6 us)
Async XLA Ops:
  0.6 2.7 %copy-start = (bf16[2,32,12288]{2,1,0:T(8,128)(2,1)S(1)}, bf16[2,32,12288]{2,1,0:T(8,128)(2,1)}, u32[]{:S(2)}) copy-start(bf16[2,32,12288]{2,1,0:T(8,128)(2,1)} %param.10) | copy-start | bytes 4718596
  0.6 5.6 %copy-start.12 = (bf16[2,32,512]{2,1,0:T(8,128)(2,1)S(1)}, bf16[2,32,512]{2,1,0:T(8,128)(2,1)}, u32[]{:S(2)}) copy-start(bf16[2,32,512]{2,1,0:T(8,128)(2,1)} %param.11) | copy-start | bytes 196612
  0.7 2.7 %copy-start.17 = (s32[128]{0:T(128)S(1)}, s32[128]{0:T(128)}, u32[]{:S(2)}) copy-start(s32[128]{0:T(128)} %param.8) | copy-start | bytes 1540
  0.7 5.6 %copy-start.11 = (bf16[128,512]{1,0:T(8,128)(2,1)S(1)}, bf16[128,512]{1,0:T(8,128)(2,1)}, u32[]{:S(2)}) copy-start(bf16[128,512]{1,0:T(8,128)(2,1)} %cot_ref.1) | copy-start | bytes 393220
  0.7 5.6 %collective-permute-start = (bf16[64,512]{1,0:T(8,128)(2,1)}, bf16[64,512]{1,0:T(8,128)(2,1)S(1)}, u32[]{:S(2)}, u32[]{:S(2)}) collective-permute-start(bf16[64,512]{1,0:T(8,128)(2,1)} %bitcast.23), channel_id=1, source_target_pairs={{0,8},{1,9},{2,10},{3,11},{4,12},{5,13},{6,14},{7,15},{8,0},{9,1},... | collective-permute-start | bytes 196616 | tf_op jit(solution)/shard_map/ppermute | solution.py:202
  7.7 37.6 %all-to-all-start = ((bf16[8,32,3712]{2,1,0:T(8,128)(2,1)}), bf16[8,32,3712]{2,1,0:T(8,128)(2,1)S(1)}, u32[]{:S(2)}, u32[]{:S(2)}) async-start(bf16[8,32,3712]{2,1,0:T(8,128)(2,1)} %shard_map.85), calls=%async_computation | async-start | bytes 3801088 | tf_op jit(solution)/shard_map/all_to_all | solution.py:197
  13.6 31.7 %collective-permute-start.1 = (bf16[384,512]{1,0:T(8,128)(2,1)S(1)}, bf16[384,512]{1,0:T(8,128)(2,1)}, u32[]{:S(2)}, u32[]{:S(2)}) collective-permute-start(bf16[384,512]{1,0:T(8,128)(2,1)S(1)} %constant_dynamic-slice_fusion), channel_id=1, source_target_pairs={{0,8},{1,9},{2,10},{3,11},{4,12},{5,13},{6,14},{7,15},{8,0},{9,1},... | collective-permute-start | bytes 1179656 | tf_op jit(solution)/shard_map/ppermute | solution.py:202
  16.3 1.9 copy-start.4
  46.6 32.0 %all-to-all-start.1 = ((bf16[8,128,768]{2,1,0:T(8,128)(2,1)}), bf16[8,128,768]{2,1,0:T(8,128)(2,1)S(1)}, u32[]{:S(2)}, u32[]{:S(2)}) async-start(bf16[8,128,768]{2,1,0:T(8,128)(2,1)} %copy-done.8), calls=%async_computation.1 | async-start | bytes 3145728 | tf_op jit(solution)/shard_map/all_to_all | solution.py:197
  53.1 33.6 %collective-permute-start.2 = (bf16[256,2048]{1,0:T(8,128)(2,1)}, bf16[256,2048]{1,0:T(8,128)(2,1)}, u32[]{:S(2)}, u32[]{:S(2)}) collective-permute-start(bf16[256,2048]{1,0:T(8,128)(2,1)} %bitcast.5.mine_ref), channel_id=1, source_target_pairs={{0,1},{1,0},{2,3},{3,2},{4,5},{5,4},{6,7},{7,6},{8,9},{9,8},{10,11... | collective-permute-start | bytes 3145736 | tf_op jit(solution)/shard_map/ppermute | solution.py:205
  53.2 12.3 %collective-permute-start.3 = (bf16[384,512]{1,0:T(8,128)(2,1)}, bf16[384,512]{1,0:T(8,128)(2,1)}, u32[]{:S(2)}, u32[]{:S(2)}) collective-permute-start(bf16[384,512]{1,0:T(8,128)(2,1)} %collective-permute-done.1), channel_id=1, source_target_pairs={{0,16},{16,0},{1,17},{17,1},{2,18},{18,2},{3,19},{19,3},{4,20},{20... | collective-permute-start | bytes 1179656 | tf_op jit(solution)/shard_map/ppermute | solution.py:208
  57.0 34.7 %collective-permute-start.4 = (bf16[256,1536]{1,0:T(8,128)(2,1)}, bf16[256,1536]{1,0:T(8,128)(2,1)}, u32[]{:S(2)}, u32[]{:S(2)}) collective-permute-start(bf16[256,1536]{1,0:T(8,128)(2,1)} %bitcast.7.m0), channel_id=1, source_target_pairs={{0,8},{1,9},{2,10},{3,11},{4,12},{5,13},{6,14},{7,15},{8,0},{9,1},... | collective-permute-start | bytes 2359304 | tf_op jit(solution)/shard_map/ppermute | solution.py:202
  58.1 39.9 %collective-permute-start.5 = (bf16[256,1536]{1,0:T(8,128)(2,1)}, bf16[256,1536]{1,0:T(8,128)(2,1)}, u32[]{:S(2)}, u32[]{:S(2)}) collective-permute-start(bf16[256,1536]{1,0:T(8,128)(2,1)} %bitcast.7.m0), channel_id=1, source_target_pairs={{0,16},{16,0},{1,17},{17,1},{2,18},{18,2},{3,19},{19,3},{4,20},{20... | collective-permute-start | bytes 2359304 | tf_op jit(solution)/shard_map/ppermute | solution.py:208
  78.5 43.4 %all-to-all-start.3 = ((bf16[8,128,768]{2,1,0:T(8,128)(2,1)}), bf16[8,128,768]{2,1,0:T(8,128)(2,1)}, u32[]{:S(2)}, u32[]{:S(2)}) async-start(bf16[8,128,768]{2,1,0:T(8,128)(2,1)} %copy-done.6), calls=%async_computation.3 | async-start | bytes 3145728 | tf_op jit(solution)/shard_map/all_to_all | solution.py:197
  86.9 4.7 %copy-start.9 = (f32[1024,128]{1,0:T(8,128)}, f32[1024,128]{1,0:T(8,128)S(1)}, u32[]{:S(2)}) copy-start(f32[1024,128]{1,0:T(8,128)S(1)} %broadcast_in_dim.12.id_ref) | copy-start | bytes 1572868
  91.6 4.9 %copy-start.1 = (bf16[1024,1024]{1,0:T(8,128)(2,1)}, bf16[1024,1024]{1,0:T(8,128)(2,1)S(1)}, u32[]{:S(2)}) copy-start(bf16[1024,1024]{1,0:T(8,128)(2,1)S(1)} %get-tuple-element.38.first_ref.second_ref) | copy-start | bytes 6291460
  91.6 20.6 %copy-start.15 = (bf16[1024,512]{1,0:T(8,128)(2,1)}, bf16[1024,512]{1,0:T(8,128)(2,1)S(1)}, u32[]{:S(2)}) copy-start(bf16[1024,512]{1,0:T(8,128)(2,1)S(1)} %get-tuple-element.32.cot_ref) | copy-start | bytes 3145732
  91.7 20.5 %collective-permute-start.6 = (bf16[256,1536]{1,0:T(8,128)(2,1)}, bf16[256,1536]{1,0:T(8,128)(2,1)S(1)}, u32[]{:S(2)}, u32[]{:S(2)}) collective-permute-start(bf16[256,1536]{1,0:T(8,128)(2,1)} %collective-permute-done.4.m1), channel_id=1, source_target_pairs={{0,16},{16,0},{1,17},{17,1},{2,18},{18,2},{3,19},{19,3},{4,20},{20... | collective-permute-start | bytes 2359304 | tf_op jit(solution)/shard_map/ppermute | solution.py:208
  96.5 34.7 %collective-permute-start.7 = (bf16[512,768]{1,0:T(8,128)(2,1)}, bf16[512,768]{1,0:T(8,128)(2,1)}, u32[]{:S(2)}, u32[]{:S(2)}) collective-permute-start(bf16[512,768]{1,0:T(8,128)(2,1)} %shard_map.90), channel_id=1, source_target_pairs={{0,8},{1,9},{2,10},{3,11},{4,12},{5,13},{6,14},{7,15},{8,0},{9,1},... | collective-permute-start | bytes 2359304 | tf_op jit(solution)/shard_map/ppermute | solution.py:202
  119.4 1.7 copy-start.5
  121.9 60.4 %all-to-all-start.2 = ((bf16[8,128,1536]{2,1,0:T(8,128)(2,1)}), bf16[8,128,1536]{2,1,0:T(8,128)(2,1)}, u32[]{:S(2)}, u32[]{:S(2)}) async-start(bf16[8,128,1536]{2,1,0:T(8,128)(2,1)} %copy-done.5), calls=%async_computation.2 | async-start | bytes 6291456 | tf_op jit(solution)/shard_map/all_to_all | solution.py:197
  131.1 1.6 copy-start.2
  132.7 6.2 %copy-start.10 = (f32[1024,128]{1,0:T(8,128)S(1)}, f32[1024,128]{1,0:T(8,128)}, u32[]{:S(2)}) copy-start(f32[1024,128]{1,0:T(8,128)} %copy-done.9) | copy-start | bytes 1572868
  132.7 6.2 %copy-start.14 = (bf16[256,1536]{1,0:T(8,128)(2,1)S(1)}, bf16[256,1536]{1,0:T(8,128)(2,1)}, u32[]{:S(2)}) copy-start(bf16[256,1536]{1,0:T(8,128)(2,1)} %copy-done.13) | copy-start | bytes 2359300
  135.5 44.2 %collective-permute-start.8 = (bf16[512,768]{1,0:T(8,128)(2,1)S(1)}, bf16[512,768]{1,0:T(8,128)(2,1)S(1)}, u32[]{:S(2)}, u32[]{:S(2)}) collective-permute-start(bf16[512,768]{1,0:T(8,128)(2,1)S(1)} %shard_map.91), channel_id=1, source_target_pairs={{0,8},{1,9},{2,10},{3,11},{4,12},{5,13},{6,14},{7,15},{8,0},{9,1},... | collective-permute-start | bytes 2359304 | tf_op jit(solution)/shard_map/ppermute | solution.py:202
  139.0 27.6 %copy-start.3 = (bf16[1024,1024]{1,0:T(8,128)(2,1)S(1)}, bf16[1024,1024]{1,0:T(8,128)(2,1)}, u32[]{:S(2)}) copy-start(bf16[1024,1024]{1,0:T(8,128)(2,1)} %copy-done.1) | copy-start | bytes 6291460
  150.2 16.3 %collective-permute-start.9 = (f32[256,128]{1,0:T(8,128)S(1)}, f32[256,128]{1,0:T(8,128)S(1)}, u32[]{:S(2)}, u32[]{:S(2)}) collective-permute-start(f32[256,128]{1,0:T(8,128)S(1)} %shard_map.92), channel_id=1, source_target_pairs={{0,2},{1,3},{2,0},{3,1},{4,6},{5,7},{6,4},{7,5},{8,10},{9,11},{10,... | collective-permute-start | bytes 393224 | tf_op jit(solution)/shard_map/ppermute | solution.py:205
  166.5 4.5 %collective-permute-start.10 = (f32[256,128]{1,0:T(8,128)S(1)}, f32[256,128]{1,0:T(8,128)S(1)}, u32[]{:S(2)}, u32[]{:S(2)}) collective-permute-start(f32[256,128]{1,0:T(8,128)S(1)} %add.58), channel_id=1, source_target_pairs={{0,1},{1,0},{2,3},{3,2},{4,5},{5,4},{6,7},{7,6},{8,9},{9,8},{10,11... | collective-permute-start | bytes 393224 | tf_op jit(solution)/shard_map/ppermute | solution.py:205
  182.3 29.9 %all-to-all-start.4 = ((bf16[8,64,1536]{2,1,0:T(8,128)(2,1)}), bf16[8,64,1536]{2,1,0:T(8,128)(2,1)S(1)}, u32[]{:S(2)}, u32[]{:S(2)}) async-start(bf16[8,64,1536]{2,1,0:T(8,128)(2,1)} %copy-done.7), calls=%async_computation.4 | async-start | bytes 3145728 | tf_op jit(solution)/shard_map/all_to_all | solution.py:197
  194.7 15.5 %collective-permute-start.11 = (bf16[64,512]{1,0:T(8,128)(2,1)S(1)}, bf16[64,512]{1,0:T(8,128)(2,1)S(1)}, u32[]{:S(2)}, u32[]{:S(2)}) collective-permute-start(bf16[64,512]{1,0:T(8,128)(2,1)S(1)} %get-tuple-element.57), channel_id=1, source_target_pairs={{0,4},{1,5},{2,6},{3,7},{4,0},{5,1},{6,2},{7,3},{8,12},{9,13},{10,... | collective-permute-start | bytes 196616 | tf_op jit(solution)/shard_map/ppermute | solution.py:205
  194.9 15.3 %collective-permute-start.13 = (bf16[64,512]{1,0:T(8,128)(2,1)S(1)}, bf16[64,512]{1,0:T(8,128)(2,1)S(1)}, u32[]{:S(2)}, u32[]{:S(2)}) collective-permute-start(bf16[64,512]{1,0:T(8,128)(2,1)S(1)} %get-tuple-element.58), channel_id=1, source_target_pairs={{0,12},{1,13},{2,14},{3,15},{4,8},{5,9},{6,10},{7,11},{8,4},{9,5},... | collective-permute-start | bytes 196616 | tf_op jit(solution)/shard_map/ppermute | solution.py:205
  196.2 15.3 %collective-permute-start.12 = (bf16[64,512]{1,0:T(8,128)(2,1)S(1)}, bf16[64,512]{1,0:T(8,128)(2,1)S(1)}, u32[]{:S(2)}, u32[]{:S(2)}) collective-permute-start(bf16[64,512]{1,0:T(8,128)(2,1)S(1)} %get-tuple-element.59), channel_id=1, source_target_pairs={{0,8},{1,9},{2,10},{3,11},{4,12},{5,13},{6,14},{7,15},{8,0},{9,1},... | collective-permute-start | bytes 196616 | tf_op jit(solution)/shard_map/ppermute | solution.py:205
  (5 other events, 5.6 us)
